TPU v7x, 32 devices: a whole 2x2x4 slice. The times are simulated.
32 devices in a mesh: dp: 8 (over z, y), seq: 4 (over x, core).
Axes of the slice: x: 2, y: 2, z: 4, core: 2. Of those that a mesh axis runs over, the one named last changes fastest.
Arguments:
- signal: bfloat16 [8, 2048, 1536], P('dp', 'seq'), may hold values from -6 to 6
- norm_gain: bfloat16 [1536], replicated, may hold values from 0.5 to 1.5
- norm_bias: bfloat16 [1536], replicated, may hold values from -3 to 3
- expand_weight: bfloat16 [1536, 3072], P('dp'), may hold values from -0.15625 to 0.15625
- expand_bias: bfloat16 [3072], replicated, may hold values from -3 to 3
- depth_kernel: bfloat16 [31, 1536], replicated, may hold values from -1 to 1
- batch_scale: bfloat16 [1536], replicated, may hold values from 0.5 to 2
- batch_shift: bfloat16 [1536], replicated, may hold values from -3 to 3
- project_weight: bfloat16 [1536, 1536], P('dp'), may hold values from -0.15625 to 0.15625
- project_bias: bfloat16 [1536], replicated, may hold values from -3 to 3
Outputs:
- result: bfloat16 [8, 2048, 1536], P('dp', 'seq')
All inputs are finite; a program needn't handle non-finite values.
Results may differ from a plain program's by a relative error of at most 0.0047.
Values may be sent and summed in bfloat16 or wider, within the bound.
No kernel may reach another device: no remote copies, remote signals or barrier semaphores. Data moves between devices by JAX's collectives and lax.ppermute only.
A program may use at most 64 MiB of HBM per device.

v0:
```python
import jax
import jax.numpy as jnp
from jax import lax
from jax.sharding import PartitionSpec as P


def extended(block, sides, width):
    for axis, dim in sides:
        count = lax.axis_size(axis)
        forward = [(i, i + 1) for i in range(count - 1)]
        backward = [(target, source) for source, target in forward]
        low = lax.ppermute(
            lax.slice_in_dim(block, block.shape[dim] - width, None, axis=dim), axis, forward
        )
        high = lax.ppermute(lax.slice_in_dim(block, 0, width, axis=dim), axis, backward)
        block = jnp.concatenate([low, block, high], axis=dim)
    return block


def fold_rows(left_side, blocks):
    return jnp.dot(left_side, blocks, preferred_element_type=jnp.float32)


def local(
    signal,
    norm_gain,
    norm_bias,
    expand_weight,
    expand_bias,
    depth_kernel,
    batch_scale,
    batch_shift,
    project_weight,
    project_bias,
):
    length = signal.shape[1]
    width = signal.shape[2]
    values = signal[0].astype(jnp.float32)
    average = jnp.mean(values, axis=-1, keepdims=True)
    centred = values - average
    spread = jnp.mean(centred * centred, axis=-1, keepdims=True)
    normed = (
        centred * lax.rsqrt(spread + 1e-05) * norm_gain.astype(jnp.float32)
        + norm_bias.astype(jnp.float32)
    ).astype(jnp.bfloat16)
    hidden = fold_rows(normed, lax.all_gather(expand_weight, "dp", axis=0, tiled=True))
    hidden = hidden + expand_bias.astype(jnp.float32)
    gated = (hidden[:, :width] * jax.nn.sigmoid(hidden[:, width:])).astype(jnp.bfloat16)
    halo_width = (depth_kernel.shape[0] - 1) // 2
    padded = extended(gated[None], (("seq", 1),), halo_width)[0].astype(jnp.float32)
    kernel = depth_kernel.astype(jnp.float32)
    depth = jnp.zeros((length, width), jnp.float32)
    for tap in range(depth_kernel.shape[0]):
        depth = depth + kernel[tap][None, :] * padded[tap : tap + length]
    scaled = depth * batch_scale.astype(jnp.float32) + batch_shift.astype(jnp.float32)
    activated = (scaled * jax.nn.sigmoid(scaled)).astype(jnp.bfloat16)
    mixed = fold_rows(activated, lax.all_gather(project_weight, "dp", axis=0, tiled=True))
    outcome = values + mixed + project_bias.astype(jnp.float32)
    return outcome.astype(jnp.bfloat16)[None]


def solution(mesh):
    in_specs = (
        P("dp", "seq", None),
        P(),
        P(),
        P("dp", None),
        P(),
        P(),
        P(),
        P(),
        P("dp", None),
        P(),
    )
    out_specs = P("dp", "seq", None)
    return jax.shard_map(local, mesh=mesh, in_specs=in_specs, out_specs=out_specs, check_vma=False)
```

profile of v0, /device:TPU:0, one launch (start us, length us, event | category | flops | bytes accessed | tf_op | source)
XLA Modules:
  0.0 292.6 jit_solution(512188425817700206)
XLA Ops:
  6.5 0.0 copy-start
  6.5 0.0 all-gather.3.cloned.1.call-start
  6.5 0.7 all-gather.3.cloned.1.call-update
  7.3 0.0 all-gather.5.cloned.1.call-start
  7.3 0.7 all-gather.5.cloned.1.call-update
  8.0 0.9 convert_element_type.45
  8.9 0.7 convert_element_type.49
  9.6 0.7 convert_element_type.46
  10.3 0.7 convert_element_type.47
  11.0 0.3 slice_reduce_fusion.30
  11.3 0.0 copy-done
  11.3 0.3 convert_reduce_fusion
  11.6 0.5 fusion.5
  12.2 138.2 %all-gather.3.cloned.1.call-done = bf16[1536,3072]{1,0:T(8,128)(2,1)} async-done(((bf16[192,3072]{1,0:T(8,128)(2,1)}), bf16[1536,3072]{1,0:T(8,128)(2,1)}) %all-gather.3.cloned.1.call-update) | async-done | bytes 9437200 | tf_op jit(solution)/shard_map/all_gather | solution.py:46
  150.3 7.7 %convolution_add_fusion = f32[512,3072]{1,0:T(8,128)S(1)} fusion(bf16[1536,3072]{1,0:T(8,128)(2,1)} %all-gather.3.cloned.1.call-done, f32[3072]{0:T(1024)S(1)} %convert_element_type.49, bf16[1,512,1536]{2,1,0:T(8,128)(2,1)S(1)} %copy-done, f32[1536]{0:T(1024)S(1)} %convert_element_type.47, f32[1536]{0:T(1024)S(1)} %convert_element_type.46, ...), kind=kOutput, calls=%fused_computation | convolution fusion | flops 4838129664 | bytes 17330176 | tf_op jit(solution)/shard_map/dot_general | solution.py:21
  158.0 0.0 copy-start.1
  158.1 0.0 copy-start.2
  158.1 0.0 copy-start.3
  158.1 0.8 fusion.84
  159.0 1.3 collective-permute-start
  160.3 1.3 collective-permute-start.1
  161.6 0.2 slice_reduce_fusion.29
  161.8 0.0 copy-done.1
  161.8 0.0 copy-done.2
  161.8 0.0 copy-done.3
  161.9 0.0 collective-permute-done
  161.9 3.2 %collective-permute-done.1 = bf16[1,15,1536]{2,1,0:T(8,128)(2,1)S(1)} collective-permute-done((bf16[1,15,1536]{2,1,0:T(8,128)(2,1)S(1)}, bf16[1,15,1536]{2,1,0:T(8,128)(2,1)S(1)}, u32[]{:S(2)}, u32[]{:S(2)}) %collective-permute-start.1) | collective-permute-done | bytes 46112 | tf_op jit(solution)/shard_map/ppermute | solution.py:15
  165.1 2.2 maximum_convert_fusion
  167.3 63.4 %all-gather.5.cloned.1.call-done = bf16[1536,1536]{1,0:T(8,128)(2,1)} async-done(((bf16[192,1536]{1,0:T(8,128)(2,1)}), bf16[1536,1536]{1,0:T(8,128)(2,1)}) %all-gather.5.cloned.1.call-update) | async-done | bytes 4718608 | tf_op jit(solution)/shard_map/all_gather | solution.py:57
  230.6 55.1 %fusion.78 = bf16[1,512,1536]{2,1,0:T(8,128)(2,1)} fusion(bf16[1536,1536]{1,0:T(8,128)(2,1)} %all-gather.5.cloned.1.call-done, bf16[1,512,1536]{2,1,0:T(8,128)(2,1)S(1)} %copy-done, f32[1536]{0:T(1024)S(1)} %convert_element_type.55, f32[1,542,1536]{2,1,0:T(8,128)} %maximum_convert_fusion, f32[1536]{0:T(1024)S(1)} %convert_element_type.53, ...), kind=kOutput, calls=%fused_computation.114 | convolution fusion | flops 2472542208 | bytes 105590784 | tf_op jit(solution)/shard_map/dot_general | solution.py:21
  (6 shorter events, 0.0 us)
Async XLA Ops:
  6.5 4.8 %copy-start = (bf16[1,512,1536]{2,1,0:T(8,128)(2,1)S(1)}, bf16[1,512,1536]{2,1,0:T(8,128)(2,1)}, u32[]{:S(2)}) copy-start(bf16[1,512,1536]{2,1,0:T(8,128)(2,1)} %param.10) | copy-start | bytes 4718596
  6.5 143.8 %all-gather.3.cloned.1.call-start = ((), (), s32[]{:S(2)}) async-start(), calls=%async_computation | async-start | bytes 10616832 | tf_op jit(solution)/shard_map/all_gather | solution.py:46
  7.3 223.4 %all-gather.5.cloned.1.call-start = ((), (), s32[]{:S(2)}) async-start(), calls=%async_computation.1 | async-start | bytes 5308416 | tf_op jit(solution)/shard_map/all_gather | solution.py:57
  158.0 3.8 %copy-start.1 = (bf16[1536]{0:T(1024)(128)(2,1)S(1)}, bf16[1536]{0:T(1024)(128)(2,1)}, u32[]{:S(2)}) copy-start(bf16[1536]{0:T(1024)(128)(2,1)} %param.16) | copy-start | bytes 9220
  158.1 3.8 %copy-start.2 = (bf16[1536]{0:T(1024)(128)(2,1)S(1)}, bf16[1536]{0:T(1024)(128)(2,1)}, u32[]{:S(2)}) copy-start(bf16[1536]{0:T(1024)(128)(2,1)} %param.17) | copy-start | bytes 9220
  158.1 3.8 %copy-start.3 = (bf16[1536]{0:T(1024)(128)(2,1)S(1)}, bf16[1536]{0:T(1024)(128)(2,1)}, u32[]{:S(2)}) copy-start(bf16[1536]{0:T(1024)(128)(2,1)} %param.19) | copy-start | bytes 9220
  159.0 2.9 collective-permute-start
  160.3 4.8 %collective-permute-start.1 = (bf16[1,15,1536]{2,1,0:T(8,128)(2,1)S(1)}, bf16[1,15,1536]{2,1,0:T(8,128)(2,1)S(1)}, u32[]{:S(2)}, u32[]{:S(2)}) collective-permute-start(bf16[1,15,1536]{2,1,0:T(8,128)(2,1)S(1)} %get-tuple-element.37), channel_id=1, source_target_pairs={{1,0},{2,1},{3,2},{5,4},{6,5},{7,6},{9,8},{10,9},{11,10},{13,12},{... | collective-permute-start | bytes 138248 | tf_op jit(solution)/shard_map/ppermute | solution.py:15
Sparse Core Ops, SparseCore 0:
  9.5 140.7 all-gather.2
  152.5 78.0 all-gather.4
where the time goes:
time: 293 us
  waiting for transfers between devices  206 us (70%)
  matrix products  62.8 us (21%)
  between operations  13.6 us (5%)
  other arithmetic  6.85 us (2%)
    all_gather x1, waiting for transfers between devices, local(): lax.all_gather(expand_weight, 'dp', axis=0, tiled=True)  138 us
    all_gather x1, waiting for transfers between devices, local(): lax.all_gather(project_weight, 'dp', axis=0, tiled=True)  63.4 us
    dot_general x2, matrix products, fold_rows(): return jnp.dot(left_side, blocks, preferred_element_type=jnp.float32)  62.8 us
  transfers between devices with their start and end apart: 4, of which 3 were waited for; matrix products, arithmetic and copies ran while one was open for 5% of the time, Pallas kernels for 0%

commit v1 on v0

--- a/solution.py
+++ b/solution.py
@@ -1,7 +1,275 @@
+import functools
+
 import jax
 import jax.numpy as jnp
 from jax import lax
+from jax.experimental import pallas as pl
+from jax.experimental.pallas import tpu as pltpu
 from jax.sharding import PartitionSpec as P
+
+LANES = 128
+VMEM_LIMIT = 48 * 1024 * 1024
+ANY = pl.BlockSpec(memory_space=pl.ANY)
+VMEM = pl.BlockSpec(memory_space=pltpu.VMEM)
+
+
+def params(**kw):
+    return pltpu.CompilerParams(vmem_limit_bytes=VMEM_LIMIT, **kw)
+
+
+def sigmoid(x):
+    return 0.5 + 0.5 * jnp.tanh(0.5 * x)
+
+
+GAIN, NBIAS, VBIAS, GBIAS, BSCALE, BSHIFT, PBIAS, TAPS = 0, 1, 2, 3, 4, 5, 6, 8
+
+
+def norm_body(signal, packed, out):
+    values = signal[...].astype(jnp.float32)
+    average = jnp.mean(values, axis=-1, keepdims=True)
+    centred = values - average
+    spread = jnp.mean(centred * centred, axis=-1, keepdims=True)
+    out[...] = (
+        centred * lax.rsqrt(spread + 1e-05) * packed[GAIN : GAIN + 1, :]
+        + packed[NBIAS : NBIAS + 1, :]
+    ).astype(jnp.bfloat16)
+
+
+def norm(signal, packed):
+    frames, width = signal.shape
+    tile = 128
+    return pl.pallas_call(
+        norm_body,
+        grid=(frames // tile,),
+        in_specs=[
+            pl.BlockSpec((tile, width), lambda i: (i, 0)),
+            pl.BlockSpec((8, width), lambda i: (0, 0)),
+        ],
+        out_specs=pl.BlockSpec((tile, width), lambda i: (i, 0)),
+        out_shape=jax.ShapeDtypeStruct((frames, width), jnp.bfloat16),
+        compiler_params=params(),
+        cost_estimate=pl.CostEstimate(
+            flops=10 * frames * width, bytes_accessed=4 * frames * width, transcendentals=frames
+        ),
+        name="layer_norm",
+    )(signal, packed)
+
+
+def conv_body(offset, share, taps, packed, first, second, third, fourth, *refs):
+    normed, outs = refs[:4], refs[4:8]
+    weight, frames_in, gated, sems = refs[8:]
+    seq, dp = lax.axis_index("seq"), lax.axis_index("dp")
+    rows = first.shape[0] // 2
+    channels = outs[0].shape[1]
+    length = normed[0].shape[0]
+    total = 4 * length
+    half = (taps - 1) // 2
+
+    copies = []
+    for which, pair in enumerate((first, second, third, fourth)):
+        for k in range(2):
+            owner = dp ^ ((which % 2) * 4 + k * 2) ^ (which // 2)
+            copies.append(
+                pltpu.make_async_copy(
+                    pair.at[pl.ds(k * rows, rows)],
+                    weight.at[pl.ds(pl.multiple_of(owner * rows, 16), rows)],
+                    sems.at[len(copies)],
+                )
+            )
+    blocks = []
+    for k in range(4):
+        start = pl.multiple_of((seq ^ k) * length, length)
+        blocks.append(
+            pltpu.make_async_copy(
+                normed[k], frames_in.at[pl.ds(start, length)], sems.at[len(copies) + k]
+            )
+        )
+    for copy in copies + blocks:
+        copy.start()
+
+    base = seq * share + offset
+    lanes = [pl.ds(pl.multiple_of(base + LANES * b, LANES), LANES) for b in range(channels // LANES)]
+    value_bias = jnp.concatenate([packed[VBIAS : VBIAS + 1, at] for at in lanes], axis=1)
+    gate_bias = jnp.concatenate([packed[GBIAS : GBIAS + 1, at] for at in lanes], axis=1)
+    edge = jnp.zeros((16, LANES), jnp.float32)
+    for b in range(len(lanes)):
+        gated[b, 0:16, :] = edge
+        gated[b, 16 + total : 32 + total, :] = edge
+    for copy in copies:
+        copy.wait()
+
+    tile = 256
+    for k in range(4):
+        blocks[k].wait()
+
+        def expand(i, _, k=k):
+            start = pl.multiple_of((seq ^ k) * length + i * tile, tile)
+            hidden = jnp.dot(
+                frames_in[pl.ds(start, tile), :], weight[...], preferred_element_type=jnp.float32
+            )
+            result = (hidden[:, :channels] + value_bias) * sigmoid(hidden[:, channels:] + gate_bias)
+            for b in range(len(lanes)):
+                gated[b, pl.ds(16 + start, tile), :] = result[:, b * LANES : (b + 1) * LANES]
+            return 0
+
+        lax.fori_loop(0, length // tile, expand, 0)
+
+    step = 64
+    for b, at in enumerate(lanes):
+        kernel = [packed[TAPS + t : TAPS + t + 1, at] for t in range(taps)]
+        scale, shift = packed[BSCALE : BSCALE + 1, at], packed[BSHIFT : BSHIFT + 1, at]
+        for k in range(4):
+
+            def depthwise(i, _, k=k, b=b, kernel=kernel, scale=scale, shift=shift):
+                start = pl.multiple_of((seq ^ k) * length + i * step, step)
+                depth = jnp.zeros((step, LANES), jnp.float32)
+                for t in range(taps):
+                    depth = depth + kernel[t] * gated[b, pl.ds(start + (16 - half + t), step), :]
+                scaled = depth * scale + shift
+                outs[k][pl.ds(pl.multiple_of(i * step, step), step), b * LANES : (b + 1) * LANES] = (
+                    scaled * sigmoid(scaled)
+                ).astype(jnp.bfloat16)
+                return 0
+
+            lax.fori_loop(0, length // step, depthwise, 0)
+
+
+def conv(offset, channels, share, taps, packed, pairs, normed):
+    length, width = normed[0].shape
+    flops = 2 * 4 * length * width * 2 * channels
+    return pl.pallas_call(
+        functools.partial(conv_body, offset, share, taps),
+        in_specs=[VMEM] + [ANY] * 8,
+        out_specs=[VMEM] * 4,
+        out_shape=[jax.ShapeDtypeStruct((length, channels), jnp.bfloat16)] * 4,
+        scratch_shapes=[
+            pltpu.VMEM((width, 2 * channels), jnp.bfloat16),
+            pltpu.VMEM((4 * length, width), jnp.bfloat16),
+            pltpu.VMEM((channels // LANES, 4 * length + 32, LANES), jnp.float32),
+            pltpu.SemaphoreType.DMA((12,)),
+        ],
+        compiler_params=params(),
+        cost_estimate=pl.CostEstimate(
+            flops=4 * flops, bytes_accessed=8 * length * width, transcendentals=0
+        ),
+        name="expand_and_depthwise",
+    )(packed, *pairs, *normed)
+
+
+def project_body(chunks, share, signal, packed, *refs):
+    count = 4 * len(chunks)
+    acts, pairs, out = refs[:count], refs[count : count + 8], refs[count + 8]
+    weight, left, sems = refs[count + 9 :]
+    seq, dp = lax.axis_index("seq"), lax.axis_index("dp")
+    rows = pairs[0].shape[0] // 2
+    cols = pairs[0].shape[1]
+    copies = []
+
+    def add(source, target):
+        copies.append(pltpu.make_async_copy(source, target, sems.at[len(copies)]))
+
+    for side in range(2):
+        at = pl.ds(pl.multiple_of(((seq & 1) ^ side) * cols, LANES), cols)
+        for which in range(4):
+            for k in range(2):
+                owner = dp ^ ((which % 2) * 4 + k * 2) ^ (which // 2)
+                add(
+                    pairs[4 * side + which].at[pl.ds(k * rows, rows)],
+                    weight.at[pl.ds(pl.multiple_of(owner * rows, 16), rows), at],
+                )
+    for j, (offset, channels) in enumerate(chunks):
+        for k in range(4):
+            at = pl.ds(pl.multiple_of((seq ^ k) * share + offset, LANES), channels)
+            add(acts[4 * j + k], left.at[:, at])
+    for copy in copies:
+        copy.start()
+    for copy in copies:
+        copy.wait()
+    tile = 128
+
+    def one(i, _):
+        at = pl.ds(pl.multiple_of(i * tile, tile), tile)
+        mixed = jnp.dot(left[at, :], weight[...], preferred_element_type=jnp.float32)
+        out[at, :] = (
+            signal[at, :].astype(jnp.float32) + mixed + packed[PBIAS : PBIAS + 1, :]
+        ).astype(jnp.bfloat16)
+        return 0
+
+    lax.fori_loop(0, out.shape[0] // tile, one, 0)
+
+
+def project(chunks, share, signal, packed, acts, pairs):
+    length, width = signal.shape
+    return pl.pallas_call(
+        functools.partial(project_body, chunks, share),
+        in_specs=[VMEM, VMEM] + [ANY] * (len(acts) + len(pairs)),
+        out_specs=VMEM,
+        out_shape=jax.ShapeDtypeStruct((length, width), jnp.bfloat16),
+        scratch_shapes=[
+            pltpu.VMEM((width, width), jnp.bfloat16),
+            pltpu.VMEM((length, width), jnp.bfloat16),
+            pltpu.SemaphoreType.DMA((len(acts) + 16,)),
+        ],
+        compiler_params=params(),
+        cost_estimate=pl.CostEstimate(
+            flops=2 * length * width * width, bytes_accessed=2 * width * width, transcendentals=0
+        ),
+        name="project_and_residual",
+    )(signal, packed, *acts, *pairs)
+
+
+def across(array, axis, bits):
+    count = lax.axis_size(axis)
+    return lax.ppermute(array, axis, [(i, i ^ bits) for i in range(count)])
+
+
+def spread(own):
+    near = across(own, "dp", 2)
+    far = across(own, "dp", 4)
+    diagonal = across(own, "dp", 6)
+    first = jnp.concatenate([own, near], axis=0)
+    second = jnp.concatenate([far, diagonal], axis=0)
+    return [first, second, across(first, "dp", 1), across(second, "dp", 1)]
+
+
+def on_the_plane(
+    signal, norm_gain, norm_bias, expand_weight, expand_bias, depth_kernel,
+    batch_scale, batch_shift, project_weight, project_bias,
+):
+    width = signal.shape[2]
+    taps = depth_kernel.shape[0]
+    seq = lax.axis_index("seq")
+    share = width // 4
+    chunks = ((0, 256), (256, 128))
+    pad = jnp.zeros((1, width), jnp.bfloat16)
+    packed = jnp.concatenate(
+        [
+            norm_gain[None], norm_bias[None], expand_bias.reshape(2, width), batch_scale[None],
+            batch_shift[None], project_bias[None], pad, depth_kernel, pad,
+        ],
+        axis=0,
+    ).astype(jnp.float32)
+
+    weights = []
+    for offset, channels in chunks:
+        value = lax.dynamic_slice_in_dim(expand_weight, seq * share + offset, channels, 1)
+        gate = lax.dynamic_slice_in_dim(expand_weight, width + seq * share + offset, channels, 1)
+        weights.append(spread(jnp.concatenate([value, gate], axis=1)))
+
+    normed = norm(signal[0], packed)
+    beside = across(normed, "seq", 1)
+    facing = across(normed, "seq", 2)
+    normed = [normed, beside, facing, across(facing, "seq", 1)]
+
+    half = width // 2
+    mine = spread(lax.dynamic_slice_in_dim(project_weight, (seq & 1) * half, half, 1))
+    pairs = mine + [across(pair, "seq", 1) for pair in mine]
+
+    acts = []
+    for (offset, channels), pieces in zip(chunks, weights):
+        parts = conv(offset, channels, share, taps, packed, pieces, normed)
+        acts += [parts[0]] + [across(parts[k], "seq", k) for k in range(1, 4)]
+    return project(chunks, share, signal[0], packed, acts, pairs)[None]
 
 
 def extended(block, sides, width):
@@ -21,17 +289,9 @@
     return jnp.dot(left_side, blocks, preferred_element_type=jnp.float32)
 
 
-def local(
-    signal,
-    norm_gain,
-    norm_bias,
-    expand_weight,
-    expand_bias,
-    depth_kernel,
-    batch_scale,
-    batch_shift,
-    project_weight,
-    project_bias,
+def gathered(
+    signal, norm_gain, norm_bias, expand_weight, expand_bias, depth_kernel,
+    batch_scale, batch_shift, project_weight, project_bias,
 ):
     length = signal.shape[1]
     width = signal.shape[2]
@@ -60,6 +320,7 @@
 
 
 def solution(mesh):
+    local = on_the_plane if (mesh.shape["dp"], mesh.shape["seq"]) == (8, 4) else gathered
     in_specs = (
         P("dp", "seq", None),
         P(),

time: 293 us -> 196 us (0.67)
  waiting for transfers between devices: 206 us -> 112 us
  matrix products: 62.8 us -> 0 us
  starting transfers between devices: 2.67 us -> 43.2 us
  Pallas kernels: 0 us -> 30.6 us
  between operations: 13.6 us -> 0.18 us
  local copies, waits for them, and re-layouts: 0.54 us -> 8.53 us
  other arithmetic: 6.85 us -> 0.13 us
    all_gather x2 -> x0, waiting for transfers between devices: 202 us -> none  [the longest x1 138 us: local(): lax.all_gather(expand_weight, 'dp', axis=0, tiled=True)]
    ppermute x2 -> x28, waiting for transfers between devices: 3.22 us -> 112 us  [across(): return lax.ppermute(array, axis, [(i, i ^ bits) for i in range(count)])]
    dot_general x2 -> x0, matrix products: 62.8 us -> none  [fold_rows(): return jnp.dot(left_side, blocks, preferred_element_type=jnp.float32)]
    ppermute x2 -> x28, starting transfers between devices: 2.63 us -> 43.2 us  [across(): return lax.ppermute(array, axis, [(i, i ^ bits) for i in range(count)])]
    pallas_call x0 -> x4, Pallas kernels: none -> 30.6 us  [the longest x2 22 us: conv(): pl.pallas_call(functools.partial(conv_body, offset, share, taps), in_spec...]
    convert_element_type x8 -> x1, other arithmetic: 5.16 us -> 0.02 us  [on_the_plane(): packed = jnp.concatenate([norm_gain[None], norm_bias[None], expand_bias.r...]
    broadcast_in_dim x0 -> x6, local copies, waits for them, and re-layouts: none -> 3.53 us  [the longest x1 0.75 us: on_the_plane(): norm_gain[None]]
  transfers between devices with their start and end apart: 4 -> 28, of which waited for: 3 -> 12; matrix products, arithmetic and copies ran while one was open for 5% -> 1% of each run, Pallas kernels for 0% -> 11%
where the time goes in v1:
time: 196 us; the launch traced here: 195 us
  waiting for transfers between devices  112 us (57%)
  starting transfers between devices  43.2 us (22%)
  Pallas kernels  30.6 us (16%)
  local copies, waits for them, and re-layouts  8.53 us (4%)
    ppermute x28, waiting for transfers between devices, across(): return lax.ppermute(array, axis, [(i, i ^ bits) for i in range(count)])  112 us
    ppermute x28, starting transfers between devices, across(): return lax.ppermute(array, axis, [(i, i ^ bits) for i in range(count)])  43.2 us
    pallas_call x2, Pallas kernels, conv(): pl.pallas_call(functools.partial(conv_body, offset, share, taps), in_spec...  22 us
    pallas_call x1, Pallas kernels, project(): pl.pallas_call(functools.partial(project_body, chunks, share), in_specs=[...  7.32 us
  transfers between devices with their start and end apart: 28, of which 12 were waited for; matrix products, arithmetic and copies ran while one was open for 1% of the time, Pallas kernels for 11%

profile of v1, /device:TPU:0, one launch (start us, length us, event | category | flops | bytes accessed | tf_op | source)
XLA Modules:
  0.0 195.1 jit_solution(15955868582524288263)
XLA Ops:
  0.0 0.8 broadcast_in_dim.21
  0.8 0.7 broadcast_in_dim.22
  1.4 0.7 reshape.3
  2.2 0.7 broadcast_in_dim.23
  2.8 0.7 broadcast_in_dim.24
  3.5 0.7 broadcast_in_dim.25
  4.2 1.0 concatenate.27
  5.3 0.0 copy-start.1
  5.3 1.4 copy-done.1
  6.7 1.3 layer_norm.1.refs_0_
  8.0 3.0 %collective-permute-start.6 = (bf16[512,1536]{1,0:T(8,128)(2,1)S(1)}, bf16[512,1536]{1,0:T(8,128)(2,1)}, u32[]{:S(2)}, u32[]{:S(2)}) collective-permute-start(bf16[512,1536]{1,0:T(8,128)(2,1)S(1)} %layer_norm.1.refs_0_), channel_id=1, source_target_pairs={{0,2},{1,3},{2,0},{3,1},{4,6},{5,7},{6,4},{7,5},{8,10},{9,11},{10,... | collective-permute-start | bytes 4718600 | tf_op jit(solution)/shard_map/ppermute | solution.py:223
  11.0 0.0 collective-permute-start.5
  11.0 34.5 %collective-permute-done.6.refs_2_ = bf16[512,1536]{1,0:T(8,128)(2,1)} collective-permute-done((bf16[512,1536]{1,0:T(8,128)(2,1)S(1)}, bf16[512,1536]{1,0:T(8,128)(2,1)}, u32[]{:S(2)}, u32[]{:S(2)}) %collective-permute-start.6) | collective-permute-done | bytes 1572896 | tf_op jit(solution)/shard_map/ppermute | solution.py:223
  45.5 0.0 collective-permute-start.7
  45.5 1.0 constant_dynamic-slice_fusion.4
  46.5 1.9 collective-permute-start
  48.4 2.6 %collective-permute-start.1 = (bf16[192,512]{1,0:T(8,128)(2,1)S(1)}, bf16[192,512]{1,0:T(8,128)(2,1)S(1)}, u32[]{:S(2)}, u32[]{:S(2)}) collective-permute-start(bf16[192,512]{1,0:T(8,128)(2,1)S(1)} %pad_maximum_fusion.2), channel_id=1, source_target_pairs={{0,16},{4,20},{8,24},{12,28},{16,0},{20,4},{24,8},{28,12},{1,17},{... | collective-permute-start | bytes 589832 | tf_op jit(solution)/shard_map/ppermute | solution.py:223
  51.0 0.8 constant_dynamic-slice_fusion.2
  51.8 0.4 collective-permute-start.12
  52.3 12.5 %collective-permute-done.12 = bf16[192,256]{1,0:T(8,128)(2,1)S(1)} collective-permute-done((bf16[192,256]{1,0:T(8,128)(2,1)S(1)}, bf16[192,256]{1,0:T(8,128)(2,1)S(1)}, u32[]{:S(2)}, u32[]{:S(2)}) %collective-permute-start.12) | collective-permute-done | bytes 98336 | tf_op jit(solution)/shard_map/ppermute | solution.py:223
  64.8 0.0 collective-permute-start.11
  64.8 4.6 %collective-permute-done.11 = bf16[192,256]{1,0:T(8,128)(2,1)S(1)} collective-permute-done((bf16[192,256]{1,0:T(8,128)(2,1)S(1)}, bf16[192,256]{1,0:T(8,128)(2,1)S(1)}, u32[]{:S(2)}, u32[]{:S(2)}) %collective-permute-start.11) | collective-permute-done | bytes 98336 | tf_op jit(solution)/shard_map/ppermute | solution.py:223
  69.4 2.5 %collective-permute-start.2 = (bf16[192,512]{1,0:T(8,128)(2,1)S(1)}, bf16[192,512]{1,0:T(8,128)(2,1)S(1)}, u32[]{:S(2)}, u32[]{:S(2)}) collective-permute-start(bf16[192,512]{1,0:T(8,128)(2,1)S(1)} %pad_maximum_fusion.2), channel_id=1, source_target_pairs={{0,24},{4,28},{8,16},{12,20},{16,8},{20,12},{24,0},{28,4},{1,25},{... | collective-permute-start | bytes 589832 | tf_op jit(solution)/shard_map/ppermute | solution.py:223
  71.9 0.0 collective-permute-done
  71.9 0.1 collective-permute-start.20
  72.0 0.0 collective-permute-done.1
  72.0 1.4 collective-permute-start.21
  73.5 5.6 %collective-permute-done.2 = bf16[192,512]{1,0:T(8,128)(2,1)S(1)} collective-permute-done((bf16[192,512]{1,0:T(8,128)(2,1)S(1)}, bf16[192,512]{1,0:T(8,128)(2,1)S(1)}, u32[]{:S(2)}, u32[]{:S(2)}) %collective-permute-start.2) | collective-permute-done | bytes 196640 | tf_op jit(solution)/shard_map/ppermute | solution.py:223
  79.1 2.5 %collective-permute-start.13 = (bf16[192,256]{1,0:T(8,128)(2,1)S(1)}, bf16[192,256]{1,0:T(8,128)(2,1)S(1)}, u32[]{:S(2)}, u32[]{:S(2)}) collective-permute-start(bf16[192,256]{1,0:T(8,128)(2,1)S(1)} %pad_maximum_fusion.4), channel_id=1, source_target_pairs={{0,24},{4,28},{8,16},{12,20},{16,8},{20,12},{24,0},{28,4},{1,25},{... | collective-permute-start | bytes 294920 | tf_op jit(solution)/shard_map/ppermute | solution.py:223
  81.6 9.5 %collective-permute-done.13 = bf16[192,256]{1,0:T(8,128)(2,1)S(1)} collective-permute-done((bf16[192,256]{1,0:T(8,128)(2,1)S(1)}, bf16[192,256]{1,0:T(8,128)(2,1)S(1)}, u32[]{:S(2)}, u32[]{:S(2)}) %collective-permute-start.13) | collective-permute-done | bytes 98336 | tf_op jit(solution)/shard_map/ppermute | solution.py:223
  91.1 17.3 %collective-permute-start.19 = (bf16[192,768]{1,0:T(8,128)(2,1)S(1)}, bf16[192,768]{1,0:T(8,128)(2,1)S(1)}, u32[]{:S(2)}, u32[]{:S(2)}) collective-permute-start(bf16[192,768]{1,0:T(8,128)(2,1)S(1)} %constant_dynamic-slice_fusion), channel_id=1, source_target_pairs={{0,8},{4,12},{8,0},{12,4},{16,24},{20,28},{24,16},{28,20},{1,9},{5... | collective-permute-start | bytes 884744 | tf_op jit(solution)/shard_map/ppermute | solution.py:223
  108.5 0.0 collective-permute-done.20
  108.5 1.5 collective-permute-start.3
  110.0 0.0 collective-permute-done.21
  110.0 0.5 collective-permute-start.4
  110.6 3.1 %collective-permute-done.19 = bf16[192,768]{1,0:T(8,128)(2,1)S(1)} collective-permute-done((bf16[192,768]{1,0:T(8,128)(2,1)S(1)}, bf16[192,768]{1,0:T(8,128)(2,1)S(1)}, u32[]{:S(2)}, u32[]{:S(2)}) %collective-permute-start.19) | collective-permute-done | bytes 294944 | tf_op jit(solution)/shard_map/ppermute | solution.py:223
  113.7 1.5 collective-permute-start.14
  115.3 5.2 %collective-permute-done.3.third = bf16[384,512]{1,0:T(8,128)(2,1)S(1)} collective-permute-done((bf16[384,512]{1,0:T(8,128)(2,1)S(1)}, bf16[384,512]{1,0:T(8,128)(2,1)S(1)}, u32[]{:S(2)}, u32[]{:S(2)}) %collective-permute-start.3) | collective-permute-done | bytes 393248 | tf_op jit(solution)/shard_map/ppermute | solution.py:223
  120.5 1.5 collective-permute-start.15
  122.1 6.9 %collective-permute-done.4.fourth = bf16[384,512]{1,0:T(8,128)(2,1)S(1)} collective-permute-done((bf16[384,512]{1,0:T(8,128)(2,1)S(1)}, bf16[384,512]{1,0:T(8,128)(2,1)S(1)}, u32[]{:S(2)}, u32[]{:S(2)}) %collective-permute-start.4) | collective-permute-done | bytes 393248 | tf_op jit(solution)/shard_map/ppermute | solution.py:223
  129.0 1.5 collective-permute-start.22
  130.5 0.0 collective-permute-done.5.refs_1_
  130.5 0.0 collective-permute-start.24
  130.5 0.0 collective-permute-done.7.refs_3_
  130.5 0.6 collective-permute-start.23
  131.1 13.8 %expand_and_depthwise.2 = (bf16[512,256]{1,0:T(8,128)(2,1)S(1)}, bf16[512,256]{1,0:T(8,128)(2,1)S(1)}, bf16[512,256]{1,0:T(8,128)(2,1)S(1)}, bf16[512,256]{1,0:T(8,128)(2,1)S(1)}) custom-call(f32[40,1536]{1,0:T(8,128)S(1)} %convert_element_type.3.packed, bf16[384,512]{1,0:T(8,128)(2,1)S(1)} %pad_maximum_fusion.1.first, ...), custom_call_target="tpu_custom_call" | custom-call | flops 12884901888 | bytes 6291456 | tf_op jit(solution)/shard_map/expand_and_depthwise/pallas_call | solution.py:140
  144.9 0.0 collective-permute-done.14.third
  144.9 0.2 collective-permute-start.25
  145.1 4.9 %collective-permute-done.22.refs_10_ = bf16[384,768]{1,0:T(8,128)(2,1)S(1)} collective-permute-done((bf16[384,768]{1,0:T(8,128)(2,1)S(1)}, bf16[384,768]{1,0:T(8,128)(2,1)S(1)}, u32[]{:S(2)}, u32[]{:S(2)}) %collective-permute-start.22) | collective-permute-done | bytes 589856 | tf_op jit(solution)/shard_map/ppermute | solution.py:223
  150.0 9.4 %collective-permute-done.23.refs_11_ = bf16[384,768]{1,0:T(8,128)(2,1)S(1)} collective-permute-done((bf16[384,768]{1,0:T(8,128)(2,1)S(1)}, bf16[384,768]{1,0:T(8,128)(2,1)S(1)}, u32[]{:S(2)}, u32[]{:S(2)}) %collective-permute-start.23) | collective-permute-done | bytes 589856 | tf_op jit(solution)/shard_map/ppermute | solution.py:223
  159.4 0.0 collective-permute-start.27
  159.4 0.0 collective-permute-done.15.fourth
  159.4 0.5 collective-permute-start.8
  159.9 8.2 %expand_and_depthwise.3 = (bf16[512,128]{1,0:T(8,128)(2,1)S(1)}, bf16[512,128]{1,0:T(8,128)(2,1)S(1)}, bf16[512,128]{1,0:T(8,128)(2,1)S(1)}, bf16[512,128]{1,0:T(8,128)(2,1)S(1)}) custom-call(f32[40,1536]{1,0:T(8,128)S(1)} %convert_element_type.3.packed, bf16[384,256]{1,0:T(8,128)(2,1)S(1)} %pad_maximum_fusion.3.first, ...), custom_call_target="tpu_custom_call" | custom-call | flops 6442450944 | bytes 6291456 | tf_op jit(solution)/shard_map/expand_and_depthwise/pallas_call | solution.py:140
  168.2 0.0 collective-permute-done.24.refs_12_
  168.2 0.1 collective-permute-start.16
  168.3 0.0 collective-permute-done.25.refs_13_
  168.3 1.5 collective-permute-start.9
  169.8 0.3 collective-permute-start.10
  170.1 1.5 collective-permute-start.17
  171.6 0.2 collective-permute-start.18
  171.8 14.0 %collective-permute-done.17.refs_6_ = bf16[512,128]{1,0:T(8,128)(2,1)S(1)} collective-permute-done((bf16[512,128]{1,0:T(8,128)(2,1)S(1)}, bf16[512,128]{1,0:T(8,128)(2,1)S(1)}, u32[]{:S(2)}, u32[]{:S(2)}) %collective-permute-start.17) | collective-permute-done | bytes 131104 | tf_op jit(solution)/shard_map/ppermute | solution.py:223
  185.9 1.9 collective-permute-done.18.refs_7_
  187.8 7.3 %project_and_residual.1 = bf16[512,1536]{1,0:T(8,128)(2,1)} custom-call(bf16[512,1536]{1,0:T(8,128)(2,1)} %bitcast.2, f32[40,1536]{1,0:T(8,128)S(1)} %convert_element_type.3.packed, bf16[512,256]{1,0:T(8,128)(2,1)S(1)} %get-tuple-element.13.refs_0_, bf16[512,256]{1,0:T(8,128)(2,1)S(1)} %collective-permute-done.8.refs_1_, ...), custom_call_target="tpu_custom_call" | custom-call | flops 2415919104 | bytes 4718592 | tf_op jit(solution)/shard_map/project_and_residual/pallas_call | solution.py:203
  (25 shorter events, 0.3 us)
Async XLA Ops:
  0.0 52.2 %copy-start = (bf16[192,1536]{1,0:T(8,128)(2,1)S(1)}, bf16[192,1536]{1,0:T(8,128)(2,1)}, u32[]{:S(2)}) copy-start(bf16[192,1536]{1,0:T(8,128)(2,1)} %param.18) | copy-start | bytes 1769476
  5.3 1.4 copy-start.1
  8.0 37.5 %collective-permute-start.6 = (bf16[512,1536]{1,0:T(8,128)(2,1)S(1)}, bf16[512,1536]{1,0:T(8,128)(2,1)}, u32[]{:S(2)}, u32[]{:S(2)}) collective-permute-start(bf16[512,1536]{1,0:T(8,128)(2,1)S(1)} %layer_norm.1.refs_0_), channel_id=1, source_target_pairs={{0,2},{1,3},{2,0},{3,1},{4,6},{5,7},{6,4},{7,5},{8,10},{9,11},{10,... | collective-permute-start | bytes 4718600 | tf_op jit(solution)/shard_map/ppermute | solution.py:223
  11.0 119.5 %collective-permute-start.5 = (bf16[512,1536]{1,0:T(8,128)(2,1)S(1)}, bf16[512,1536]{1,0:T(8,128)(2,1)}, u32[]{:S(2)}, u32[]{:S(2)}) collective-permute-start(bf16[512,1536]{1,0:T(8,128)(2,1)S(1)} %layer_norm.1.refs_0_), channel_id=1, source_target_pairs={{0,1},{1,0},{2,3},{3,2},{4,5},{5,4},{6,7},{7,6},{8,9},{9,8},{10,11... | collective-permute-start | bytes 4718600 | tf_op jit(solution)/shard_map/ppermute | solution.py:223
  45.5 85.0 %collective-permute-start.7 = (bf16[512,1536]{1,0:T(8,128)(2,1)}, bf16[512,1536]{1,0:T(8,128)(2,1)}, u32[]{:S(2)}, u32[]{:S(2)}) collective-permute-start(bf16[512,1536]{1,0:T(8,128)(2,1)} %collective-permute-done.6.refs_2_), channel_id=1, source_target_pairs={{0,1},{1,0},{2,3},{3,2},{4,5},{5,4},{6,7},{7,6},{8,9},{9,8},{10,11... | collective-permute-start | bytes 4718600 | tf_op jit(solution)/shard_map/ppermute | solution.py:223
  46.5 25.4 %collective-permute-start = (bf16[192,512]{1,0:T(8,128)(2,1)S(1)}, bf16[192,512]{1,0:T(8,128)(2,1)S(1)}, u32[]{:S(2)}, u32[]{:S(2)}) collective-permute-start(bf16[192,512]{1,0:T(8,128)(2,1)S(1)} %pad_maximum_fusion.2), channel_id=1, source_target_pairs={{0,8},{4,12},{8,0},{12,4},{16,24},{20,28},{24,16},{28,20},{1,9},{5... | collective-permute-start | bytes 589832 | tf_op jit(solution)/shard_map/ppermute | solution.py:223
  48.4 23.6 %collective-permute-start.1 = (bf16[192,512]{1,0:T(8,128)(2,1)S(1)}, bf16[192,512]{1,0:T(8,128)(2,1)S(1)}, u32[]{:S(2)}, u32[]{:S(2)}) collective-permute-start(bf16[192,512]{1,0:T(8,128)(2,1)S(1)} %pad_maximum_fusion.2), channel_id=1, source_target_pairs={{0,16},{4,20},{8,24},{12,28},{16,0},{20,4},{24,8},{28,12},{1,17},{... | collective-permute-start | bytes 589832 | tf_op jit(solution)/shard_map/ppermute | solution.py:223
  51.8 13.0 %collective-permute-start.12 = (bf16[192,256]{1,0:T(8,128)(2,1)S(1)}, bf16[192,256]{1,0:T(8,128)(2,1)S(1)}, u32[]{:S(2)}, u32[]{:S(2)}) collective-permute-start(bf16[192,256]{1,0:T(8,128)(2,1)S(1)} %pad_maximum_fusion.4), channel_id=1, source_target_pairs={{0,16},{4,20},{8,24},{12,28},{16,0},{20,4},{24,8},{28,12},{1,17},{... | collective-permute-start | bytes 294920 | tf_op jit(solution)/shard_map/ppermute | solution.py:223
  64.8 4.6 %collective-permute-start.11 = (bf16[192,256]{1,0:T(8,128)(2,1)S(1)}, bf16[192,256]{1,0:T(8,128)(2,1)S(1)}, u32[]{:S(2)}, u32[]{:S(2)}) collective-permute-start(bf16[192,256]{1,0:T(8,128)(2,1)S(1)} %pad_maximum_fusion.4), channel_id=1, source_target_pairs={{0,8},{4,12},{8,0},{12,4},{16,24},{20,28},{24,16},{28,20},{1,9},{5... | collective-permute-start | bytes 294920 | tf_op jit(solution)/shard_map/ppermute | solution.py:223
  69.4 9.7 %collective-permute-start.2 = (bf16[192,512]{1,0:T(8,128)(2,1)S(1)}, bf16[192,512]{1,0:T(8,128)(2,1)S(1)}, u32[]{:S(2)}, u32[]{:S(2)}) collective-permute-start(bf16[192,512]{1,0:T(8,128)(2,1)S(1)} %pad_maximum_fusion.2), channel_id=1, source_target_pairs={{0,24},{4,28},{8,16},{12,20},{16,8},{20,12},{24,0},{28,4},{1,25},{... | collective-permute-start | bytes 589832 | tf_op jit(solution)/shard_map/ppermute | solution.py:223
  71.9 36.6 %collective-permute-start.20 = (bf16[192,768]{1,0:T(8,128)(2,1)S(1)}, bf16[192,768]{1,0:T(8,128)(2,1)S(1)}, u32[]{:S(2)}, u32[]{:S(2)}) collective-permute-start(bf16[192,768]{1,0:T(8,128)(2,1)S(1)} %constant_dynamic-slice_fusion), channel_id=1, source_target_pairs={{0,16},{4,20},{8,24},{12,28},{16,0},{20,4},{24,8},{28,12},{1,17},{... | collective-permute-start | bytes 884744 | tf_op jit(solution)/shard_map/ppermute | solution.py:223
  72.0 38.0 %collective-permute-start.21 = (bf16[192,768]{1,0:T(8,128)(2,1)S(1)}, bf16[192,768]{1,0:T(8,128)(2,1)S(1)}, u32[]{:S(2)}, u32[]{:S(2)}) collective-permute-start(bf16[192,768]{1,0:T(8,128)(2,1)S(1)} %constant_dynamic-slice_fusion), channel_id=1, source_target_pairs={{0,24},{4,28},{8,16},{12,20},{16,8},{20,12},{24,0},{28,4},{1,25},{... | collective-permute-start | bytes 884744 | tf_op jit(solution)/shard_map/ppermute | solution.py:223
  79.1 12.0 %collective-permute-start.13 = (bf16[192,256]{1,0:T(8,128)(2,1)S(1)}, bf16[192,256]{1,0:T(8,128)(2,1)S(1)}, u32[]{:S(2)}, u32[]{:S(2)}) collective-permute-start(bf16[192,256]{1,0:T(8,128)(2,1)S(1)} %pad_maximum_fusion.4), channel_id=1, source_target_pairs={{0,24},{4,28},{8,16},{12,20},{16,8},{20,12},{24,0},{28,4},{1,25},{... | collective-permute-start | bytes 294920 | tf_op jit(solution)/shard_map/ppermute | solution.py:223
  91.1 22.6 %collective-permute-start.19 = (bf16[192,768]{1,0:T(8,128)(2,1)S(1)}, bf16[192,768]{1,0:T(8,128)(2,1)S(1)}, u32[]{:S(2)}, u32[]{:S(2)}) collective-permute-start(bf16[192,768]{1,0:T(8,128)(2,1)S(1)} %constant_dynamic-slice_fusion), channel_id=1, source_target_pairs={{0,8},{4,12},{8,0},{12,4},{16,24},{20,28},{24,16},{28,20},{1,9},{5... | collective-permute-start | bytes 884744 | tf_op jit(solution)/shard_map/ppermute | solution.py:223
  108.5 12.1 %collective-permute-start.3 = (bf16[384,512]{1,0:T(8,128)(2,1)S(1)}, bf16[384,512]{1,0:T(8,128)(2,1)S(1)}, u32[]{:S(2)}, u32[]{:S(2)}) collective-permute-start(bf16[384,512]{1,0:T(8,128)(2,1)S(1)} %pad_maximum_fusion.1.first), channel_id=1, source_target_pairs={{0,4},{4,0},{8,12},{12,8},{16,20},{20,16},{24,28},{28,24},{1,5},{5... | collective-permute-start | bytes 1179656 | tf_op jit(solution)/shard_map/ppermute | solution.py:223
  110.0 19.0 %collective-permute-start.4 = (bf16[384,512]{1,0:T(8,128)(2,1)S(1)}, bf16[384,512]{1,0:T(8,128)(2,1)S(1)}, u32[]{:S(2)}, u32[]{:S(2)}) collective-permute-start(bf16[384,512]{1,0:T(8,128)(2,1)S(1)} %constant_dynamic-update-slice_fusion.second), channel_id=1, source_target_pairs={{0,4},{4,0},{8,12},{12,8},{16,20},{20,16},{24,28},{28,24},{1,5},{5... | collective-permute-start | bytes 1179656 | tf_op jit(solution)/shard_map/ppermute | solution.py:223
  113.7 31.1 %collective-permute-start.14 = (bf16[384,256]{1,0:T(8,128)(2,1)S(1)}, bf16[384,256]{1,0:T(8,128)(2,1)S(1)}, u32[]{:S(2)}, u32[]{:S(2)}) collective-permute-start(bf16[384,256]{1,0:T(8,128)(2,1)S(1)} %pad_maximum_fusion.3.first), channel_id=1, source_target_pairs={{0,4},{4,0},{8,12},{12,8},{16,20},{20,16},{24,28},{28,24},{1,5},{5... | collective-permute-start | bytes 589832 | tf_op jit(solution)/shard_map/ppermute | solution.py:223
  120.5 38.9 %collective-permute-start.15 = (bf16[384,256]{1,0:T(8,128)(2,1)S(1)}, bf16[384,256]{1,0:T(8,128)(2,1)S(1)}, u32[]{:S(2)}, u32[]{:S(2)}) collective-permute-start(bf16[384,256]{1,0:T(8,128)(2,1)S(1)} %constant_dynamic-update-slice_fusion.2.second), channel_id=1, source_target_pairs={{0,4},{4,0},{8,12},{12,8},{16,20},{20,16},{24,28},{28,24},{1,5},{5... | collective-permute-start | bytes 589832 | tf_op jit(solution)/shard_map/ppermute | solution.py:223
  129.0 21.1 %collective-permute-start.22 = (bf16[384,768]{1,0:T(8,128)(2,1)S(1)}, bf16[384,768]{1,0:T(8,128)(2,1)S(1)}, u32[]{:S(2)}, u32[]{:S(2)}) collective-permute-start(bf16[384,768]{1,0:T(8,128)(2,1)S(1)} %pad_maximum_fusion.refs_8_), channel_id=1, source_target_pairs={{0,4},{4,0},{8,12},{12,8},{16,20},{20,16},{24,28},{28,24},{1,5},{5... | collective-permute-start | bytes 1769480 | tf_op jit(solution)/shard_map/ppermute | solution.py:223
  130.5 37.7 %collective-permute-start.24 = (bf16[384,768]{1,0:T(8,128)(2,1)S(1)}, bf16[384,768]{1,0:T(8,128)(2,1)S(1)}, u32[]{:S(2)}, u32[]{:S(2)}) collective-permute-start(bf16[384,768]{1,0:T(8,128)(2,1)S(1)} %pad_maximum_fusion.refs_8_), channel_id=1, source_target_pairs={{0,1},{1,0},{2,3},{3,2},{4,5},{5,4},{6,7},{7,6},{8,9},{9,8},{10,11... | collective-permute-start | bytes 1769480 | tf_op jit(solution)/shard_map/ppermute | solution.py:223
  130.5 28.9 %collective-permute-start.23 = (bf16[384,768]{1,0:T(8,128)(2,1)S(1)}, bf16[384,768]{1,0:T(8,128)(2,1)S(1)}, u32[]{:S(2)}, u32[]{:S(2)}) collective-permute-start(bf16[384,768]{1,0:T(8,128)(2,1)S(1)} %constant_dynamic-update-slice_fusion.4.refs_9_), channel_id=1, source_target_pairs={{0,4},{4,0},{8,12},{12,8},{16,20},{20,16},{24,28},{28,24},{1,5},{5... | collective-permute-start | bytes 1769480 | tf_op jit(solution)/shard_map/ppermute | solution.py:223
  144.9 23.4 %collective-permute-start.25 = (bf16[384,768]{1,0:T(8,128)(2,1)S(1)}, bf16[384,768]{1,0:T(8,128)(2,1)S(1)}, u32[]{:S(2)}, u32[]{:S(2)}) collective-permute-start(bf16[384,768]{1,0:T(8,128)(2,1)S(1)} %constant_dynamic-update-slice_fusion.4.refs_9_), channel_id=1, source_target_pairs={{0,1},{1,0},{2,3},{3,2},{4,5},{5,4},{6,7},{7,6},{8,9},{9,8},{10,11... | collective-permute-start | bytes 1769480 | tf_op jit(solution)/shard_map/ppermute | solution.py:223
  150.0 19.8 %collective-permute-start.26 = (bf16[384,768]{1,0:T(8,128)(2,1)S(1)}, bf16[384,768]{1,0:T(8,128)(2,1)S(1)}, u32[]{:S(2)}, u32[]{:S(2)}) collective-permute-start(bf16[384,768]{1,0:T(8,128)(2,1)S(1)} %collective-permute-done.22.refs_10_), channel_id=1, source_target_pairs={{0,1},{1,0},{2,3},{3,2},{4,5},{5,4},{6,7},{7,6},{8,9},{9,8},{10,11... | collective-permute-start | bytes 1769480 | tf_op jit(solution)/shard_map/ppermute | solution.py:223
  159.4 10.7 %collective-permute-start.27 = (bf16[384,768]{1,0:T(8,128)(2,1)S(1)}, bf16[384,768]{1,0:T(8,128)(2,1)S(1)}, u32[]{:S(2)}, u32[]{:S(2)}) collective-permute-start(bf16[384,768]{1,0:T(8,128)(2,1)S(1)} %collective-permute-done.23.refs_11_), channel_id=1, source_target_pairs={{0,1},{1,0},{2,3},{3,2},{4,5},{5,4},{6,7},{7,6},{8,9},{9,8},{10,11... | collective-permute-start | bytes 1769480 | tf_op jit(solution)/shard_map/ppermute | solution.py:223
  159.4 28.3 %collective-permute-start.8 = (bf16[512,256]{1,0:T(8,128)(2,1)S(1)}, bf16[512,256]{1,0:T(8,128)(2,1)S(1)}, u32[]{:S(2)}, u32[]{:S(2)}) collective-permute-start(bf16[512,256]{1,0:T(8,128)(2,1)S(1)} %get-tuple-element.14), channel_id=1, source_target_pairs={{0,1},{1,0},{2,3},{3,2},{4,5},{5,4},{6,7},{7,6},{8,9},{9,8},{10,11... | collective-permute-start | bytes 786440 | tf_op jit(solution)/shard_map/ppermute | solution.py:223
  168.2 3.4 %collective-permute-start.16 = (bf16[512,128]{1,0:T(8,128)(2,1)S(1)}, bf16[512,128]{1,0:T(8,128)(2,1)S(1)}, u32[]{:S(2)}, u32[]{:S(2)}) collective-permute-start(bf16[512,128]{1,0:T(8,128)(2,1)S(1)} %get-tuple-element.18), channel_id=1, source_target_pairs={{0,1},{1,0},{2,3},{3,2},{4,5},{5,4},{6,7},{7,6},{8,9},{9,8},{10,11... | collective-permute-start | bytes 393224 | tf_op jit(solution)/shard_map/ppermute | solution.py:223
  168.3 19.5 %collective-permute-start.9 = (bf16[512,256]{1,0:T(8,128)(2,1)S(1)}, bf16[512,256]{1,0:T(8,128)(2,1)S(1)}, u32[]{:S(2)}, u32[]{:S(2)}) collective-permute-start(bf16[512,256]{1,0:T(8,128)(2,1)S(1)} %get-tuple-element.15), channel_id=1, source_target_pairs={{0,2},{1,3},{2,0},{3,1},{4,6},{5,7},{6,4},{7,5},{8,10},{9,11},{10,... | collective-permute-start | bytes 786440 | tf_op jit(solution)/shard_map/ppermute | solution.py:223
  169.8 17.9 %collective-permute-start.10 = (bf16[512,256]{1,0:T(8,128)(2,1)S(1)}, bf16[512,256]{1,0:T(8,128)(2,1)S(1)}, u32[]{:S(2)}, u32[]{:S(2)}) collective-permute-start(bf16[512,256]{1,0:T(8,128)(2,1)S(1)} %get-tuple-element.16), channel_id=1, source_target_pairs={{0,3},{1,2},{2,1},{3,0},{4,7},{5,6},{6,5},{7,4},{8,11},{9,10},{10,... | collective-permute-start | bytes 786440 | tf_op jit(solution)/shard_map/ppermute | solution.py:223
  170.1 17.6 %copy-start.2 = (bf16[384,768]{1,0:T(8,128)(2,1)}, bf16[384,768]{1,0:T(8,128)(2,1)S(1)}, u32[]{:S(2)}) copy-start(bf16[384,768]{1,0:T(8,128)(2,1)S(1)} %collective-permute-done.27.refs_15_) | copy-start | bytes 1769476
  170.1 15.7 %collective-permute-start.17 = (bf16[512,128]{1,0:T(8,128)(2,1)S(1)}, bf16[512,128]{1,0:T(8,128)(2,1)S(1)}, u32[]{:S(2)}, u32[]{:S(2)}) collective-permute-start(bf16[512,128]{1,0:T(8,128)(2,1)S(1)} %get-tuple-element.19), channel_id=1, source_target_pairs={{0,2},{1,3},{2,0},{3,1},{4,6},{5,7},{6,4},{7,5},{8,10},{9,11},{10,... | collective-permute-start | bytes 393224 | tf_op jit(solution)/shard_map/ppermute | solution.py:223
  171.6 16.1 %collective-permute-start.18 = (bf16[512,128]{1,0:T(8,128)(2,1)S(1)}, bf16[512,128]{1,0:T(8,128)(2,1)S(1)}, u32[]{:S(2)}, u32[]{:S(2)}) collective-permute-start(bf16[512,128]{1,0:T(8,128)(2,1)S(1)} %get-tuple-element.20), channel_id=1, source_target_pairs={{0,3},{1,2},{2,1},{3,0},{4,7},{5,6},{6,5},{7,4},{8,11},{9,10},{10,... | collective-permute-start | bytes 393224 | tf_op jit(solution)/shard_map/ppermute | solution.py:223

commit v2 on v0

--- a/solution.py
+++ b/solution.py
@@ -1,7 +1,369 @@
+import functools
+
 import jax
 import jax.numpy as jnp
 from jax import lax
+from jax.experimental import pallas as pl
+from jax.experimental.pallas import tpu as pltpu
 from jax.sharding import PartitionSpec as P
+
+LANES = 128
+LARGE = 60 * 1024 * 1024
+CONV = 24 * 1024 * 1024
+ANY = pl.BlockSpec(memory_space=pl.ANY)
+VMEM = pl.BlockSpec(memory_space=pltpu.VMEM)
+
+
+def params(limit=32 * 1024 * 1024):
+    return pltpu.CompilerParams(vmem_limit_bytes=limit)
+
+
+def sigmoid(x):
+    return 0.5 + 0.5 * jnp.tanh(0.5 * x)
+
+
+GAIN, NBIAS, VBIAS, GBIAS, BSCALE, BSHIFT, PBIAS = range(7)
+EDGE = 16
+PIECES = (208, 416)
+FREE = pl.CostEstimate(flops=0, bytes_accessed=0, transcendentals=0)
+
+
+def cut_body(cuts, signal, expand, project, first, second, *refs):
+    pieces, sems = refs[:-1], refs[-1]
+    seq = lax.axis_index("seq")
+    share = first.shape[1] // 2
+    half = second.shape[1]
+    width = expand.shape[1] // 2
+    copies = []
+
+    def add(source, target):
+        copies.append(pltpu.make_async_copy(source, target, sems.at[len(copies)]))
+
+    for side in range(2):
+        at = pl.ds(pl.multiple_of(side * width + seq * share, LANES), share)
+        add(expand.at[:, at], first.at[:, side * share : (side + 1) * share])
+    add(project.at[:, pl.ds(pl.multiple_of((seq & 1) * half, LANES), half)], second)
+    for (start, stop), piece in zip(cuts, pieces):
+        add(signal.at[start:stop], piece)
+    for copy in copies:
+        copy.start()
+    for copy in copies:
+        copy.wait()
+
+
+def cut(cuts, signal, expand, project, parts):
+    rows, width = project.shape
+    share = width // parts
+    shapes = [(rows, 2 * share), (rows, width // 2)] + [(b - a, width) for a, b in cuts]
+    return pl.pallas_call(
+        functools.partial(cut_body, cuts),
+        in_specs=[ANY] * 3,
+        out_specs=[VMEM] * len(shapes),
+        out_shape=[jax.ShapeDtypeStruct(shape, expand.dtype) for shape in shapes],
+        scratch_shapes=[pltpu.SemaphoreType.DMA((len(cuts) + 3,))],
+        compiler_params=params(LARGE),
+        cost_estimate=FREE,
+        name="cut",
+    )(signal, expand, project)
+
+
+def norm_body(packed, *refs):
+    pieces, out = refs[:-1], refs[-1]
+    base = 0
+    for piece in pieces:
+        tile = next(t for t in (128, 104, 96, 16) if piece.shape[0] % t == 0)
+
+        def one(i, _, piece=piece, base=base, tile=tile):
+            at = pl.multiple_of(i * tile, tile)
+            values = piece[pl.ds(at, tile), :].astype(jnp.float32)
+            average = jnp.mean(values, axis=-1, keepdims=True)
+            centred = values - average
+            spread = jnp.mean(centred * centred, axis=-1, keepdims=True)
+            out[pl.ds(base + at, tile), :] = (
+                centred * lax.rsqrt(spread + 1e-05) * packed[GAIN : GAIN + 1, :]
+                + packed[NBIAS : NBIAS + 1, :]
+            ).astype(jnp.bfloat16)
+            return 0
+
+        lax.fori_loop(0, piece.shape[0] // tile, one, 0)
+        base += piece.shape[0]
+
+
+def norm(packed, *pieces):
+    width = packed.shape[1]
+    return pl.pallas_call(
+        norm_body,
+        in_specs=[VMEM] * (1 + len(pieces)),
+        out_specs=VMEM,
+        out_shape=jax.ShapeDtypeStruct((sum(p.shape[0] for p in pieces), width), jnp.bfloat16),
+        compiler_params=params(),
+        cost_estimate=FREE,
+        name="layer_norm",
+    )(packed, *pieces)
+
+
+def gather_body(places, *refs):
+    pieces, out, sems = refs[: len(places)], refs[-2], refs[-1]
+    dp = lax.axis_index("dp")
+    rows = pieces[0].shape[0]
+    copies = []
+    for piece, (bits, first) in zip(pieces, places):
+        at = pl.multiple_of((dp ^ bits) * rows + first, 16)
+        copies.append(
+            pltpu.make_async_copy(piece, out.at[pl.ds(at, piece.shape[0])], sems.at[len(copies)])
+        )
+    for copy in copies:
+        copy.start()
+    for copy in copies:
+        copy.wait()
+
+
+def gather(places, pieces):
+    rows = sum(piece.shape[0] for piece in pieces)
+    return pl.pallas_call(
+        functools.partial(gather_body, places),
+        in_specs=[ANY] * len(pieces),
+        out_specs=VMEM,
+        out_shape=jax.ShapeDtypeStruct((rows, pieces[0].shape[1]), pieces[0].dtype),
+        scratch_shapes=[pltpu.SemaphoreType.DMA((len(pieces),))],
+        compiler_params=params(),
+        cost_estimate=FREE,
+        name="gather_shards",
+    )(*pieces)
+
+
+def conv_body(across_x, across_core, packed, kernel, weight, block, sibling, outer, out, frames, gated, taps):
+    seq = lax.axis_index("seq")
+    chip, odd = (seq >> 1) ^ across_x, (seq & 1) ^ across_core
+    length, channels = out.shape
+    count = kernel.shape[0]
+    half = (count - 1) // 2
+    lanes = [
+        pl.ds(pl.multiple_of(seq * channels + LANES * b, LANES), LANES)
+        for b in range(channels // LANES)
+    ]
+    for b, at in enumerate(lanes):
+        taps[b, 0:count, :] = kernel[:, at].astype(jnp.float32)
+    frames[EDGE : EDGE + length, :] = block[...]
+    for edges, first in ((sibling, odd), (outer, 1 - odd)):
+        source = pl.ds(pl.multiple_of(first * (edges.shape[0] - EDGE), EDGE), EDGE)
+        frames[pl.ds(pl.multiple_of((1 - first) * (EDGE + length), EDGE), EDGE), :] = edges[source, :]
+    starts = jnp.logical_and(chip == 0, odd == 0)
+    ends = jnp.logical_and(chip == 1, odd == 1)
+
+    def expand(b):
+        columns = jnp.concatenate(
+            [
+                weight[:, b * LANES : (b + 1) * LANES],
+                weight[:, channels + b * LANES : channels + (b + 1) * LANES],
+            ],
+            axis=1,
+        )
+        hidden = jnp.dot(frames[...], columns, preferred_element_type=jnp.float32)
+        value = hidden[:, :LANES] + packed[VBIAS : VBIAS + 1, lanes[b]]
+        gate = hidden[:, LANES:] + packed[GBIAS : GBIAS + 1, lanes[b]]
+        result = value * sigmoid(gate)
+        gated[b, 0:EDGE, :] = jnp.where(starts, 0.0, result[0:EDGE, :])
+        gated[b, EDGE : EDGE + length, :] = result[EDGE : EDGE + length, :]
+        gated[b, EDGE + length :, :] = jnp.where(ends, 0.0, result[EDGE + length :, :])
+
+    step = 64
+
+    def depthwise(b):
+        at = lanes[b]
+        scale, shift = packed[BSCALE : BSCALE + 1, at], packed[BSHIFT : BSHIFT + 1, at]
+        for start in range(0, length, step):
+            depth = jnp.zeros((step, LANES), jnp.float32)
+            for t in range(count):
+                first = start + EDGE - half + t
+                depth = depth + taps[b, t : t + 1, :] * gated[b, first : first + step, :]
+            scaled = depth * scale + shift
+            out[start : start + step, b * LANES : (b + 1) * LANES] = (
+                scaled * sigmoid(scaled)
+            ).astype(jnp.bfloat16)
+
+    for b in range(len(lanes)):
+        expand(b)
+        if b:
+            depthwise(b - 1)
+    depthwise(len(lanes) - 1)
+
+
+def conv(across_x, across_core, packed, kernel, weight, block, sibling, outer):
+    length, width = block.shape
+    channels = weight.shape[1] // 2
+    extent = length + 2 * EDGE
+    return pl.pallas_call(
+        functools.partial(conv_body, across_x, across_core),
+        in_specs=[VMEM] * 6,
+        out_specs=VMEM,
+        out_shape=jax.ShapeDtypeStruct((length, channels), jnp.bfloat16),
+        scratch_shapes=[
+            pltpu.VMEM((extent, width), jnp.bfloat16),
+            pltpu.VMEM((channels // LANES, extent, LANES), jnp.float32),
+            pltpu.VMEM((channels // LANES, kernel.shape[0] + 1, LANES), jnp.float32),
+        ],
+        compiler_params=params(CONV),
+        cost_estimate=FREE,
+        name="expand_and_depthwise",
+    )(packed, kernel, weight, block, sibling, outer)
+
+
+def project_body(places, packed, signal, whole, *refs):
+    count = 2 * len(places)
+    pieces, acts, out = refs[:count], refs[count : count + 4], refs[count + 4]
+    weight, left, frames, result, sems = refs[count + 5 :]
+    seq, dp = lax.axis_index("seq"), lax.axis_index("dp")
+    share = acts[0].shape[1]
+    rows, cols = whole.shape[0], pieces[0].shape[1]
+    length = out.shape[0]
+    tile = 256
+    copies = []
+
+    def add(source, target):
+        copies.append(pltpu.make_async_copy(source, target, sems.at[len(copies)]))
+        copies[-1].start()
+
+    ats = [pl.ds(pl.multiple_of(((seq & 1) ^ side) * cols, LANES), cols) for side in range(2)]
+    for side in range(2):
+        sources = [(whole.at[:, ats[side]], 0, 0)]
+        sources += [
+            (piece, *place) for piece, place in zip(pieces[side * len(places) :], places)
+        ]
+        for source, bits, first in sources:
+            at = pl.ds(pl.multiple_of((dp ^ bits) * rows + first, 16), source.shape[0])
+            add(source, weight.at[side, at])
+        if side == 0:
+            for k in range(4):
+                at = pl.ds(pl.multiple_of((seq ^ k) * share, LANES), share)
+                add(acts[k], left.at[:, at])
+            add(signal, frames)
+    split = len(places) + 6
+    parts = []
+    for side, ready in enumerate((copies[:split], copies[split:])):
+        for copy in ready:
+            copy.wait()
+        for start in range(0, length, tile):
+            mixed = jnp.dot(
+                left[start : start + tile, :], weight[side], preferred_element_type=jnp.float32
+            )
+            mixed = mixed + packed[PBIAS : PBIAS + 1, ats[side]]
+            mixed = mixed + frames[start : start + tile, ats[side]].astype(jnp.float32)
+            result[side, start : start + tile, :] = mixed.astype(jnp.bfloat16)
+            part = pltpu.make_async_copy(
+                result.at[side, start : start + tile],
+                out.at[start : start + tile, ats[side]],
+                sems.at[len(copies) + len(parts)],
+            )
+            part.start()
+            parts.append(part)
+    for part in parts:
+        part.wait()
+
+
+def project(packed, signal, whole, places, mine, other, acts):
+    length, width = signal.shape
+    return pl.pallas_call(
+        functools.partial(project_body, places),
+        in_specs=[VMEM] + [ANY] * (2 + 2 * len(places) + 4),
+        out_specs=ANY,
+        out_shape=jax.ShapeDtypeStruct((length, width), jnp.bfloat16),
+        scratch_shapes=[
+            pltpu.VMEM((2, width, width // 2), jnp.bfloat16),
+            pltpu.VMEM((length, width), jnp.bfloat16),
+            pltpu.VMEM((length, width), jnp.bfloat16),
+            pltpu.VMEM((2, length, width // 2), jnp.bfloat16),
+            pltpu.SemaphoreType.DMA((2 * len(places) + 7 + 2 * (length // 256),)),
+        ],
+        compiler_params=params(),
+        cost_estimate=FREE,
+        name="project_and_residual",
+    )(packed, signal, whole, *mine, *other, *acts)
+
+
+def across(array, axis, bits):
+    count = lax.axis_size(axis)
+    return lax.ppermute(array, axis, [(i, i ^ bits) for i in range(count)])
+
+
+def after(array, *others):
+    return lax.optimization_barrier((array, *others))[0]
+
+
+def on_the_plane(
+    signal, norm_gain, norm_bias, expand_weight, expand_bias, depth_kernel,
+    batch_scale, batch_shift, project_weight, project_bias,
+):
+    width = signal.shape[2]
+    own = signal[0]
+    length = own.shape[0]
+    marks = [0, PIECES[0], PIECES[1], length]
+    cuts = list(zip(marks[:-1], marks[1:]))
+    e_own, p_own, *pieces = cut(cuts, own, expand_weight, project_weight, 4)
+    fold = p_own.shape[0] // 2
+
+    facing = [across(pieces[0], "seq", 2)]
+    e_far, e_near = across(e_own, "dp", 6), across(e_own, "dp", 2)
+    ey_own, py_own = across(e_own, "dp", 1), across(p_own, "dp", 1)
+    done = (facing[0], e_far, e_near, ey_own, py_own)
+
+    facing.append(across(after(pieces[1], *done), "seq", 2))
+    e_middle = across(after(e_own, *done), "dp", 4)
+    p_near = across(after(p_own, *done), "dp", 2)
+    ey_near, ey_far = across(after(e_near, *done), "dp", 1), across(after(e_far, *done), "dp", 1)
+    packed = (
+        jnp.concatenate(
+            [after(norm_gain, *done), norm_bias, expand_bias, batch_scale, batch_shift, project_bias]
+        )
+        .reshape(7, width)
+        .astype(jnp.float32)
+    )
+    normed = norm(packed, own)
+    edges = jnp.concatenate([normed[:EDGE], normed[-EDGE:]], axis=0)
+    done = (facing[1], e_middle, p_near, ey_near, ey_far)
+
+    facing.append(across(after(pieces[2], *done), "seq", 2))
+    ey_middle = across(after(e_middle, *done), "dp", 1)
+    p_far = [across(after(p_own[:fold], *done), "dp", 6)]
+    edges = across(after(edges, *done), "seq", 3)
+    beside = across(after(normed, *done), "seq", 1)
+    e_shards = [e_own, e_near, e_middle, e_far, ey_own, ey_near, ey_middle, ey_far]
+    done = (facing[2], ey_middle, p_far[0], edges, beside)
+
+    normed_facing = norm(packed, after(facing[0], *done), *facing[1:])
+    diagonal = across(normed_facing, "seq", 1)
+    p_far.append(across(after(p_own[fold:], *done), "dp", 6))
+    py_near = across(after(p_near, *done), "dp", 1)
+    py_far = [across(p_far[0], "dp", 1)]
+    weight = gather([(2 * (k % 4) + k // 4, 0) for k in range(8)], e_shards)
+    run = functools.partial(conv, packed=packed, kernel=depth_kernel, weight=weight)
+    part_facing = run(1, 0, block=normed_facing, sibling=edges, outer=beside)
+    done = (part_facing, diagonal, p_far[1])
+
+    act_facing = across(part_facing, "seq", 2)
+    p_middle = across(after(p_own, *done), "dp", 4)
+    py_far.append(across(after(p_far[1], *done), "dp", 1))
+    part_diagonal = run(1, 1, block=after(diagonal, *done), sibling=normed_facing, outer=normed)
+    done = (part_diagonal, py_near, py_far[0])
+
+    act_diagonal = across(part_diagonal, "seq", 3)
+    swap = lambda array: across(after(array, *done), "seq", 1)
+    p_mine = [p_near, p_far[0], py_own, py_near]
+    p_other = [swap(piece) for piece in p_mine]
+    part_beside = run(0, 1, block=after(beside, *done), sibling=normed, outer=normed_facing)
+    done = (part_beside, p_middle, py_far[1], act_facing)
+
+    act_beside = across(part_beside, "seq", 1)
+    py_middle = across(after(p_middle, *done), "dp", 1)
+    late = [p_far[1], py_far[0], py_far[1], p_middle]
+    p_mine += late
+    p_other += [swap(piece) for piece in late]
+    part_own = run(0, 0, block=after(normed, *done), sibling=beside, outer=diagonal)
+    p_mine.append(py_middle)
+    p_other.append(across(after(py_middle, part_own), "seq", 1))
+    places = [(2, 0), (6, 0), (1, 0), (3, 0), (6, fold), (7, 0), (7, fold), (4, 0), (5, 0)]
+    acts = [part_own, act_beside, act_facing, act_diagonal]
+    return project(packed, own, project_weight, places, p_mine, p_other, acts)[None]
 
 
 def extended(block, sides, width):
@@ -21,17 +383,9 @@
     return jnp.dot(left_side, blocks, preferred_element_type=jnp.float32)
 
 
-def local(
-    signal,
-    norm_gain,
-    norm_bias,
-    expand_weight,
-    expand_bias,
-    depth_kernel,
-    batch_scale,
-    batch_shift,
-    project_weight,
-    project_bias,
+def gathered(
+    signal, norm_gain, norm_bias, expand_weight, expand_bias, depth_kernel,
+    batch_scale, batch_shift, project_weight, project_bias,
 ):
     length = signal.shape[1]
     width = signal.shape[2]
@@ -60,6 +414,7 @@
 
 
 def solution(mesh):
+    local = on_the_plane if (mesh.shape["dp"], mesh.shape["seq"]) == (8, 4) else gathered
     in_specs = (
         P("dp", "seq", None),
         P(),

time: 293 us -> 102 us (0.35)
  waiting for transfers between devices: 206 us -> 41.3 us
  matrix products: 62.8 us -> 0 us
  starting transfers between devices: 2.67 us -> 30.6 us
  Pallas kernels: 0 us -> 27.8 us
  between operations: 13.6 us -> 0.41 us
  other arithmetic: 6.85 us -> 0.01 us
    all_gather x2 -> x0, waiting for transfers between devices: 202 us -> none  [the longest x1 138 us: local(): lax.all_gather(expand_weight, 'dp', axis=0, tiled=True)]
    dot_general x2 -> x0, matrix products: 62.8 us -> none  [fold_rows(): return jnp.dot(left_side, blocks, preferred_element_type=jnp.float32)]
    ppermute x2 -> x34, waiting for transfers between devices: 3.22 us -> 41.3 us  [across(): return lax.ppermute(array, axis, [(i, i ^ bits) for i in range(count)])]
    ppermute x2 -> x34, starting transfers between devices: 2.63 us -> 30.6 us  [across(): return lax.ppermute(array, axis, [(i, i ^ bits) for i in range(count)])]
    pallas_call x0 -> x9, Pallas kernels: none -> 27.8 us  [the longest x4 13.7 us: conv(): pl.pallas_call(functools.partial(conv_body, across_x, across_core), in_sp...]
    convert_element_type x8 -> x0, other arithmetic: 5.16 us -> none  [the longest x1 2.17 us: local(): extended(gated[None], (('seq', 1),), halo_width)[0].astype(jnp.float32)]
  transfers between devices with their start and end apart: 4 -> 34, of which waited for: 3 -> 15; matrix products, arithmetic and copies ran while one was open for 5% -> 1% of each run, Pallas kernels for 0% -> 16%
where the time goes in v2:
time: 102 us
  waiting for transfers between devices  41.3 us (40%)
  starting transfers between devices  30.6 us (30%)
  Pallas kernels  27.8 us (27%)
  local copies, waits for them, and re-layouts  1.89 us (2%)
    ppermute x34, waiting for transfers between devices, across(): return lax.ppermute(array, axis, [(i, i ^ bits) for i in range(count)])  41.3 us
    ppermute x34, starting transfers between devices, across(): return lax.ppermute(array, axis, [(i, i ^ bits) for i in range(count)])  30.6 us
    pallas_call x4, Pallas kernels, conv(): pl.pallas_call(functools.partial(conv_body, across_x, across_core), in_sp...  13.7 us
    pallas_call x1, Pallas kernels, project(): pl.pallas_call(functools.partial(project_body, places), in_specs=[VMEM] +...  6.7 us
    pallas_call x1, Pallas kernels, cut(): pl.pallas_call(functools.partial(cut_body, cuts), in_specs=[ANY] * 3, out...  3.09 us
    pallas_call x2, Pallas kernels, norm(): pl.pallas_call(norm_body, in_specs=[VMEM] * (1 + len(pieces)), out_specs=...  2.76 us
  transfers between devices with their start and end apart: 34, of which 15 were waited for; matrix products, arithmetic and copies ran while one was open for 1% of the time, Pallas kernels for 16%

profile of v2, /device:TPU:0, one launch (start us, length us, event | category | flops | bytes accessed | tf_op | source)
XLA Modules:
  0.0 102.0 jit_solution(3208220999766475307)
XLA Ops:
  0.0 3.1 %cut.1 = (bf16[192,768]{1,0:T(8,128)(2,1)}, bf16[192,768]{1,0:T(8,128)(2,1)}, bf16[208,1536]{1,0:T(8,128)(2,1)}, bf16[208,1536]{1,0:T(8,128)(2,1)}, bf16[96,1536]{1,0:T(8,128)(2,1)}) custom-call(bf16[512,1536]{1,0:T(8,128)(2,1)} %bitcast.2, bf16[192,3072]{1,0:T(8,128)(2,1)} %expand.1, bf16[192,1536]{1,0:T(8,128)(2,1)} %whole.1), custom_call_target="tpu_custom_call" | custom-call | tf_op jit(solution)/shard_map/cut/pallas_call | solution.py:58
  3.1 3.0 %collective-permute-start = (bf16[208,1536]{1,0:T(8,128)(2,1)}, bf16[208,1536]{1,0:T(8,128)(2,1)S(1)}, u32[]{:S(2)}, u32[]{:S(2)}) collective-permute-start(bf16[208,1536]{1,0:T(8,128)(2,1)} %get-tuple-element.38), channel_id=1, source_target_pairs={{0,2},{1,3},{2,0},{3,1},{4,6},{5,7},{6,4},{7,5},{8,10},{9,11},{10,... | collective-permute-start | bytes 1916936 | tf_op jit(solution)/shard_map/ppermute | solution.py:286
  6.1 1.5 %collective-permute-start.4 = (bf16[192,768]{1,0:T(8,128)(2,1)}, bf16[192,768]{1,0:T(8,128)(2,1)S(1)}, u32[]{:S(2)}, u32[]{:S(2)}) collective-permute-start(bf16[192,768]{1,0:T(8,128)(2,1)} %get-tuple-element.58), channel_id=1, source_target_pairs={{0,4},{4,0},{8,12},{12,8},{16,20},{20,16},{24,28},{28,24},{1,5},{5... | collective-permute-start | bytes 884744 | tf_op jit(solution)/shard_map/ppermute | solution.py:286
  7.7 0.5 collective-permute-start.3
  8.2 1.6 %collective-permute-start.2 = (bf16[192,768]{1,0:T(8,128)(2,1)}, bf16[192,768]{1,0:T(8,128)(2,1)}, u32[]{:S(2)}, u32[]{:S(2)}) collective-permute-start(bf16[192,768]{1,0:T(8,128)(2,1)} %get-tuple-element.45.refs_0_), channel_id=1, source_target_pairs={{0,8},{4,12},{8,0},{12,4},{16,24},{20,28},{24,16},{28,20},{1,9},{5... | collective-permute-start | bytes 884744 | tf_op jit(solution)/shard_map/ppermute | solution.py:286
  9.8 2.5 %collective-permute-start.1 = (bf16[192,768]{1,0:T(8,128)(2,1)}, bf16[192,768]{1,0:T(8,128)(2,1)}, u32[]{:S(2)}, u32[]{:S(2)}) collective-permute-start(bf16[192,768]{1,0:T(8,128)(2,1)} %get-tuple-element.45.refs_0_), channel_id=1, source_target_pairs={{0,24},{4,28},{8,16},{12,20},{16,8},{20,12},{24,0},{28,4},{1,25},{... | collective-permute-start | bytes 884744 | tf_op jit(solution)/shard_map/ppermute | solution.py:286
  12.2 4.1 %collective-permute-done.4.refs_2_ = bf16[192,768]{1,0:T(8,128)(2,1)S(1)} collective-permute-done((bf16[192,768]{1,0:T(8,128)(2,1)}, bf16[192,768]{1,0:T(8,128)(2,1)S(1)}, u32[]{:S(2)}, u32[]{:S(2)}) %collective-permute-start.4) | collective-permute-done | bytes 294944 | tf_op jit(solution)/shard_map/ppermute | solution.py:286
  16.3 4.9 %collective-permute-done.3.refs_4_ = bf16[192,768]{1,0:T(8,128)(2,1)S(1)} collective-permute-done((bf16[192,768]{1,0:T(8,128)(2,1)}, bf16[192,768]{1,0:T(8,128)(2,1)S(1)}, u32[]{:S(2)}, u32[]{:S(2)}) %collective-permute-start.3) | collective-permute-done | bytes 294944 | tf_op jit(solution)/shard_map/ppermute | solution.py:286
  21.1 0.7 copy-done.4
  21.9 0.0 collective-permute-done.2.refs_1_
  21.9 3.0 %collective-permute-done.1.refs_3_ = bf16[192,768]{1,0:T(8,128)(2,1)} collective-permute-done((bf16[192,768]{1,0:T(8,128)(2,1)}, bf16[192,768]{1,0:T(8,128)(2,1)}, u32[]{:S(2)}, u32[]{:S(2)}) %collective-permute-start.1) | collective-permute-done | bytes 294944 | tf_op jit(solution)/shard_map/ppermute | solution.py:286
  24.9 0.5 collective-permute-start.6
  25.4 0.6 collective-permute-start.5
  26.0 1.4 %collective-permute-start.7 = (bf16[192,768]{1,0:T(8,128)(2,1)}, bf16[192,768]{1,0:T(8,128)(2,1)}, u32[]{:S(2)}, u32[]{:S(2)}) collective-permute-start(bf16[192,768]{1,0:T(8,128)(2,1)} %get-tuple-element.45.refs_0_), channel_id=1, source_target_pairs={{0,16},{4,20},{8,24},{12,28},{16,0},{20,4},{24,8},{28,12},{1,17},{... | collective-permute-start | bytes 884744 | tf_op jit(solution)/shard_map/ppermute | solution.py:286
  27.4 1.5 %collective-permute-start.8 = (bf16[192,768]{1,0:T(8,128)(2,1)}, bf16[192,768]{1,0:T(8,128)(2,1)}, u32[]{:S(2)}, u32[]{:S(2)}) collective-permute-start(bf16[192,768]{1,0:T(8,128)(2,1)} %collective-permute-done.2.refs_1_), channel_id=1, source_target_pairs={{0,4},{4,0},{8,12},{12,8},{16,20},{20,16},{24,28},{28,24},{1,5},{5... | collective-permute-start | bytes 884744 | tf_op jit(solution)/shard_map/ppermute | solution.py:286
  28.9 0.5 collective-permute-start.9
  29.5 0.2 dynamic-update-slice
  29.6 0.3 dynamic-update-slice.1
  29.9 0.3 dynamic-update-slice.3
  30.2 0.3 dynamic-update-slice.4
  30.5 0.1 reshape.3.packed
  30.6 1.3 %layer_norm.2.outer.sibling.block = bf16[512,1536]{1,0:T(8,128)(2,1)S(1)} custom-call(f32[7,1536]{1,0:T(8,128)S(1)} %reshape.3.packed, bf16[512,1536]{1,0:T(8,128)(2,1)S(1)} %bitcast.3), custom_call_target="tpu_custom_call" | custom-call | tf_op jit(solution)/shard_map/layer_norm/pallas_call | solution.py:94
  31.9 6.0 %collective-permute-done.5.refs_0_ = bf16[192,768]{1,0:T(8,128)(2,1)S(1)} collective-permute-done((bf16[192,768]{1,0:T(8,128)(2,1)}, bf16[192,768]{1,0:T(8,128)(2,1)S(1)}, u32[]{:S(2)}, u32[]{:S(2)}) %collective-permute-start.5) | collective-permute-done | bytes 294944 | tf_op jit(solution)/shard_map/ppermute | solution.py:286
  37.9 1.8 %collective-permute-done.7.refs_2_ = bf16[192,768]{1,0:T(8,128)(2,1)} collective-permute-done((bf16[192,768]{1,0:T(8,128)(2,1)}, bf16[192,768]{1,0:T(8,128)(2,1)}, u32[]{:S(2)}, u32[]{:S(2)}) %collective-permute-start.7) | collective-permute-done | bytes 294944 | tf_op jit(solution)/shard_map/ppermute | solution.py:286
  39.7 0.0 collective-permute-done.8.refs_5_
  39.7 0.8 collective-permute-done.9.refs_7_
  40.4 0.0 collective-permute-done.6.refs_1_
  40.5 2.1 %collective-permute-start.10 = (bf16[96,768]{1,0:T(8,128)(2,1)S(1)}, bf16[96,768]{1,0:T(8,128)(2,1)S(1)}, u32[]{:S(2)}, u32[]{:S(2)}) collective-permute-start(bf16[96,768]{1,0:T(8,128)(2,1)S(1)} %get-tuple-element.48), channel_id=1, source_target_pairs={{0,24},{4,28},{8,16},{12,20},{16,8},{20,12},{24,0},{28,4},{1,25},{... | collective-permute-start | bytes 442376 | tf_op jit(solution)/shard_map/ppermute | solution.py:286
  42.6 1.5 %collective-permute-start.11 = (bf16[96,1536]{1,0:T(8,128)(2,1)S(1)}, bf16[96,1536]{1,0:T(8,128)(2,1)S(1)}, u32[]{:S(2)}, u32[]{:S(2)}) collective-permute-start(bf16[96,1536]{1,0:T(8,128)(2,1)S(1)} %copy-done.13), channel_id=1, source_target_pairs={{0,2},{1,3},{2,0},{3,1},{4,6},{5,7},{6,4},{7,5},{8,10},{9,11},{10,... | collective-permute-start | bytes 884744 | tf_op jit(solution)/shard_map/ppermute | solution.py:286
  44.1 1.5 %collective-permute-start.12 = (bf16[192,768]{1,0:T(8,128)(2,1)}, bf16[192,768]{1,0:T(8,128)(2,1)S(1)}, u32[]{:S(2)}, u32[]{:S(2)}) collective-permute-start(bf16[192,768]{1,0:T(8,128)(2,1)} %collective-permute-done.7.refs_2_), channel_id=1, source_target_pairs={{0,4},{4,0},{8,12},{12,8},{16,20},{20,16},{24,28},{28,24},{1,5},{5... | collective-permute-start | bytes 884744 | tf_op jit(solution)/shard_map/ppermute | solution.py:286
  45.7 0.1 collective-permute-start.13
  45.7 7.4 %collective-permute-done.13.sibling = bf16[32,1536]{1,0:T(8,128)(2,1)S(1)} collective-permute-done((bf16[32,1536]{1,0:T(8,128)(2,1)S(1)}, bf16[32,1536]{1,0:T(8,128)(2,1)S(1)}, u32[]{:S(2)}, u32[]{:S(2)}) %collective-permute-start.13) | collective-permute-done | bytes 98336 | tf_op jit(solution)/shard_map/ppermute | solution.py:286
  53.2 0.0 collective-permute-done.12.refs_6_
  53.2 1.5 %layer_norm.3.block.sibling.outer = bf16[512,1536]{1,0:T(8,128)(2,1)S(1)} custom-call(f32[7,1536]{1,0:T(8,128)S(1)} %reshape.3.packed, bf16[208,1536]{1,0:T(8,128)(2,1)S(1)} %collective-permute-done.refs_0_, bf16[208,1536]{1,0:T(8,128)(2,1)S(1)} %collective-permute-done.6.refs_1_, bf16[96,1536]{1,0:T(8,128)(2,1)S(1)} %collective-permute-done.11.refs_2_), custom_call_target="tpu_custom_call" | custom-call | tf_op jit(solution)/shard_map/layer_norm/pallas_call | solution.py:94
  54.7 0.6 collective-permute-start.18
  55.2 1.8 %collective-permute-start.16 = (bf16[96,768]{1,0:T(8,128)(2,1)S(1)}, bf16[96,768]{1,0:T(8,128)(2,1)S(1)}, u32[]{:S(2)}, u32[]{:S(2)}) collective-permute-start(bf16[96,768]{1,0:T(8,128)(2,1)S(1)} %get-tuple-element.55), channel_id=1, source_target_pairs={{0,24},{4,28},{8,16},{12,20},{16,8},{20,12},{24,0},{28,4},{1,25},{... | collective-permute-start | bytes 442376 | tf_op jit(solution)/shard_map/ppermute | solution.py:286
  57.0 1.5 %gather_shards.1.weight = bf16[1536,768]{1,0:T(8,128)(2,1)S(1)} custom-call(bf16[192,768]{1,0:T(8,128)(2,1)S(1)} %copy-done.3, bf16[192,768]{1,0:T(8,128)(2,1)} %collective-permute-done.2.refs_1_, bf16[192,768]{1,0:T(8,128)(2,1)} %collective-permute-done.7.refs_2_, bf16[192,768]{1,0:T(8,128)(2,1)} %collective-permute-done.1.refs_3_, ...), custom_call_target="tpu_custom_call" | custom-call | tf_op jit(solution)/shard_map/gather_shards/pallas_call | solution.py:123
  58.5 3.3 %expand_and_depthwise.4 = bf16[512,384]{1,0:T(8,128)(2,1)S(1)} custom-call(f32[7,1536]{1,0:T(8,128)S(1)} %reshape.3.packed, bf16[31,1536]{1,0:T(8,128)(2,1)S(1)} %copy-done.2, bf16[1536,768]{1,0:T(8,128)(2,1)S(1)} %gather_shards.1.weight, bf16[512,1536]{1,0:T(8,128)(2,1)S(1)} %layer_norm.3.block.sibling.outer, ...), custom_call_target="tpu_custom_call" | custom-call | tf_op jit(solution)/shard_map/expand_and_depthwise/pallas_call | solution.py:196
  61.9 1.2 %collective-permute-start.21 = (bf16[512,384]{1,0:T(8,128)(2,1)S(1)}, bf16[512,384]{1,0:T(8,128)(2,1)S(1)}, u32[]{:S(2)}, u32[]{:S(2)}) collective-permute-start(bf16[512,384]{1,0:T(8,128)(2,1)S(1)} %expand_and_depthwise.4), channel_id=1, source_target_pairs={{0,2},{1,3},{2,0},{3,1},{4,6},{5,7},{6,4},{7,5},{8,10},{9,11},{10,... | collective-permute-start | bytes 1179656 | tf_op jit(solution)/shard_map/ppermute | solution.py:286
  63.1 1.5 %collective-permute-start.15 = (bf16[192,768]{1,0:T(8,128)(2,1)S(1)}, bf16[192,768]{1,0:T(8,128)(2,1)S(1)}, u32[]{:S(2)}, u32[]{:S(2)}) collective-permute-start(bf16[192,768]{1,0:T(8,128)(2,1)S(1)} %collective-permute-done.5.refs_0_), channel_id=1, source_target_pairs={{0,4},{4,0},{8,12},{12,8},{16,20},{20,16},{24,28},{28,24},{1,5},{5... | collective-permute-start | bytes 884744 | tf_op jit(solution)/shard_map/ppermute | solution.py:286
  64.7 1.0 collective-permute-start.17
  65.6 1.1 %collective-permute-start.19 = (bf16[96,768]{1,0:T(8,128)(2,1)S(1)}, bf16[96,768]{1,0:T(8,128)(2,1)S(1)}, u32[]{:S(2)}, u32[]{:S(2)}) collective-permute-start(bf16[96,768]{1,0:T(8,128)(2,1)S(1)} %collective-permute-done.16.refs_4_), channel_id=1, source_target_pairs={{0,4},{4,0},{8,12},{12,8},{16,20},{20,16},{24,28},{28,24},{1,5},{5... | collective-permute-start | bytes 442376 | tf_op jit(solution)/shard_map/ppermute | solution.py:286
  66.7 3.4 %expand_and_depthwise.5 = bf16[512,384]{1,0:T(8,128)(2,1)S(1)} custom-call(f32[7,1536]{1,0:T(8,128)S(1)} %reshape.3.packed, bf16[31,1536]{1,0:T(8,128)(2,1)S(1)} %copy-done.2, bf16[1536,768]{1,0:T(8,128)(2,1)S(1)} %gather_shards.1.weight, bf16[512,1536]{1,0:T(8,128)(2,1)S(1)} %collective-permute-done.18.block.outer, ...), custom_call_target="tpu_custom_call" | custom-call | tf_op jit(solution)/shard_map/expand_and_depthwise/pallas_call | solution.py:196
  70.2 6.0 %collective-permute-done.17.refs_5_ = bf16[96,768]{1,0:T(8,128)(2,1)S(1)} collective-permute-done((bf16[96,768]{1,0:T(8,128)(2,1)S(1)}, bf16[96,768]{1,0:T(8,128)(2,1)S(1)}, u32[]{:S(2)}, u32[]{:S(2)}) %collective-permute-start.17) | collective-permute-done | bytes 147488 | tf_op jit(solution)/shard_map/ppermute | solution.py:286
  76.2 3.4 %expand_and_depthwise.6 = bf16[512,384]{1,0:T(8,128)(2,1)S(1)} custom-call(f32[7,1536]{1,0:T(8,128)S(1)} %reshape.3.packed, bf16[31,1536]{1,0:T(8,128)(2,1)S(1)} %copy-done.2, bf16[1536,768]{1,0:T(8,128)(2,1)S(1)} %gather_shards.1.weight, bf16[512,1536]{1,0:T(8,128)(2,1)S(1)} %collective-permute-done.14.outer.block.sibling, ...), custom_call_target="tpu_custom_call" | custom-call | tf_op jit(solution)/shard_map/expand_and_depthwise/pallas_call | solution.py:196
  79.7 0.0 copy-start.1
  79.7 0.1 collective-permute-done.20.refs_7_
  79.8 1.5 %collective-permute-start.22 = (bf16[192,768]{1,0:T(8,128)(2,1)S(1)}, bf16[192,768]{1,0:T(8,128)(2,1)S(1)}, u32[]{:S(2)}, u32[]{:S(2)}) collective-permute-start(bf16[192,768]{1,0:T(8,128)(2,1)S(1)} %collective-permute-done.20.refs_7_), channel_id=1, source_target_pairs={{0,4},{4,0},{8,12},{12,8},{16,20},{20,16},{24,28},{28,24},{1,5},{5... | collective-permute-start | bytes 884744 | tf_op jit(solution)/shard_map/ppermute | solution.py:286
  81.3 0.5 collective-permute-start.23
  81.8 0.5 collective-permute-start.32
  82.3 0.3 collective-permute-done.24.refs_10_
  82.7 0.6 collective-permute-start.33
  83.3 5.4 %collective-permute-done.22.refs_8_ = bf16[192,768]{1,0:T(8,128)(2,1)S(1)} collective-permute-done((bf16[192,768]{1,0:T(8,128)(2,1)S(1)}, bf16[192,768]{1,0:T(8,128)(2,1)S(1)}, u32[]{:S(2)}, u32[]{:S(2)}) %collective-permute-start.22) | collective-permute-done | bytes 294944 | tf_op jit(solution)/shard_map/ppermute | solution.py:286
  88.7 3.6 %expand_and_depthwise.7.refs_18_ = bf16[512,384]{1,0:T(8,128)(2,1)S(1)} custom-call(f32[7,1536]{1,0:T(8,128)S(1)} %reshape.3.packed, bf16[31,1536]{1,0:T(8,128)(2,1)S(1)} %copy-done.2, bf16[1536,768]{1,0:T(8,128)(2,1)S(1)} %gather_shards.1.weight, bf16[512,1536]{1,0:T(8,128)(2,1)S(1)} %layer_norm.2.outer.sibling.block, ...), custom_call_target="tpu_custom_call" | custom-call | tf_op jit(solution)/shard_map/expand_and_depthwise/pallas_call | solution.py:196
  92.3 0.6 collective-permute-start.30
  92.8 0.1 collective-permute-start.31
  92.9 0.4 collective-permute-start.27
  93.4 0.1 collective-permute-start.28
  93.5 0.3 collective-permute-done.33.refs_21_
  93.7 0.1 collective-permute-start.29
  93.9 0.8 collective-permute-done.27.refs_13_
  94.7 0.2 collective-permute-done.28.refs_14_
  94.9 0.2 collective-permute-done.29.refs_15_
  95.1 6.7 %project_and_residual.1 = bf16[512,1536]{1,0:T(8,128)(2,1)} custom-call(f32[7,1536]{1,0:T(8,128)S(1)} %reshape.3.packed, bf16[512,1536]{1,0:T(8,128)(2,1)S(1)} %bitcast.4, bf16[192,1536]{1,0:T(8,128)(2,1)S(1)} %copy-done.1, bf16[192,768]{1,0:T(8,128)(2,1)S(1)} %collective-permute-done.5.refs_0_, bf16[96,768]{1,0:T(8,128)(2,1)S(1)} %collective-permute-done.10.refs_1_, ...), custom_call_target="tpu_custom_call" | custom-call | tf_op jit(solution)/shard_map/project_and_residual/pallas_call | solution.py:266
  (52 shorter events, 0.2 us)
Async XLA Ops:
  0.0 29.5 %copy-start.8 = (bf16[1536]{0:T(1024)(128)(2,1)S(1)}, bf16[1536]{0:T(1024)(128)(2,1)}, u32[]{:S(2)}) copy-start(bf16[1536]{0:T(1024)(128)(2,1)} %param.11) | copy-start | bytes 9220
  0.0 29.6 %copy-start.9 = (bf16[1536]{0:T(1024)(128)(2,1)S(1)}, bf16[1536]{0:T(1024)(128)(2,1)}, u32[]{:S(2)}) copy-start(bf16[1536]{0:T(1024)(128)(2,1)} %param.12) | copy-start | bytes 9220
  0.0 29.9 %copy-start.7 = (bf16[3072]{0:T(1024)(128)(2,1)S(1)}, bf16[3072]{0:T(1024)(128)(2,1)}, u32[]{:S(2)}) copy-start(bf16[3072]{0:T(1024)(128)(2,1)} %param.14) | copy-start | bytes 18436
  0.0 29.9 %copy-start.10 = (bf16[1536]{0:T(1024)(128)(2,1)S(1)}, bf16[1536]{0:T(1024)(128)(2,1)}, u32[]{:S(2)}) copy-start(bf16[1536]{0:T(1024)(128)(2,1)} %param.16) | copy-start | bytes 9220
  0.0 30.2 %copy-start.11 = (bf16[1536]{0:T(1024)(128)(2,1)S(1)}, bf16[1536]{0:T(1024)(128)(2,1)}, u32[]{:S(2)}) copy-start(bf16[1536]{0:T(1024)(128)(2,1)} %param.17) | copy-start | bytes 9220
  0.0 30.5 %copy-start.12 = (bf16[1536]{0:T(1024)(128)(2,1)S(1)}, bf16[1536]{0:T(1024)(128)(2,1)}, u32[]{:S(2)}) copy-start(bf16[1536]{0:T(1024)(128)(2,1)} %param.19) | copy-start | bytes 9220
  0.0 30.6 %copy-start = (bf16[1,512,1536]{2,1,0:T(8,128)(2,1)S(1)}, bf16[1,512,1536]{2,1,0:T(8,128)(2,1)}, u32[]{:S(2)}) copy-start(bf16[1,512,1536]{2,1,0:T(8,128)(2,1)} %param.10) | copy-start | bytes 4718596
  3.1 21.7 %collective-permute-start = (bf16[208,1536]{1,0:T(8,128)(2,1)}, bf16[208,1536]{1,0:T(8,128)(2,1)S(1)}, u32[]{:S(2)}, u32[]{:S(2)}) collective-permute-start(bf16[208,1536]{1,0:T(8,128)(2,1)} %get-tuple-element.38), channel_id=1, source_target_pairs={{0,2},{1,3},{2,0},{3,1},{4,6},{5,7},{6,4},{7,5},{8,10},{9,11},{10,... | collective-permute-start | bytes 1916936 | tf_op jit(solution)/shard_map/ppermute | solution.py:286
  6.1 10.1 %collective-permute-start.4 = (bf16[192,768]{1,0:T(8,128)(2,1)}, bf16[192,768]{1,0:T(8,128)(2,1)S(1)}, u32[]{:S(2)}, u32[]{:S(2)}) collective-permute-start(bf16[192,768]{1,0:T(8,128)(2,1)} %get-tuple-element.58), channel_id=1, source_target_pairs={{0,4},{4,0},{8,12},{12,8},{16,20},{20,16},{24,28},{28,24},{1,5},{5... | collective-permute-start | bytes 884744 | tf_op jit(solution)/shard_map/ppermute | solution.py:286
  7.7 13.5 %collective-permute-start.3 = (bf16[192,768]{1,0:T(8,128)(2,1)}, bf16[192,768]{1,0:T(8,128)(2,1)S(1)}, u32[]{:S(2)}, u32[]{:S(2)}) collective-permute-start(bf16[192,768]{1,0:T(8,128)(2,1)} %get-tuple-element.45.refs_0_), channel_id=1, source_target_pairs={{0,4},{4,0},{8,12},{12,8},{16,20},{20,16},{24,28},{28,24},{1,5},{5... | collective-permute-start | bytes 884744 | tf_op jit(solution)/shard_map/ppermute | solution.py:286
  8.2 13.7 %collective-permute-start.2 = (bf16[192,768]{1,0:T(8,128)(2,1)}, bf16[192,768]{1,0:T(8,128)(2,1)}, u32[]{:S(2)}, u32[]{:S(2)}) collective-permute-start(bf16[192,768]{1,0:T(8,128)(2,1)} %get-tuple-element.45.refs_0_), channel_id=1, source_target_pairs={{0,8},{4,12},{8,0},{12,4},{16,24},{20,28},{24,16},{28,20},{1,9},{5... | collective-permute-start | bytes 884744 | tf_op jit(solution)/shard_map/ppermute | solution.py:286
  9.8 15.1 %collective-permute-start.1 = (bf16[192,768]{1,0:T(8,128)(2,1)}, bf16[192,768]{1,0:T(8,128)(2,1)}, u32[]{:S(2)}, u32[]{:S(2)}) collective-permute-start(bf16[192,768]{1,0:T(8,128)(2,1)} %get-tuple-element.45.refs_0_), channel_id=1, source_target_pairs={{0,24},{4,28},{8,16},{12,20},{16,8},{20,12},{24,0},{28,4},{1,25},{... | collective-permute-start | bytes 884744 | tf_op jit(solution)/shard_map/ppermute | solution.py:286
  21.1 0.7 copy-start.4
  24.9 15.6 %collective-permute-start.6 = (bf16[208,1536]{1,0:T(8,128)(2,1)}, bf16[208,1536]{1,0:T(8,128)(2,1)S(1)}, u32[]{:S(2)}, u32[]{:S(2)}) collective-permute-start(bf16[208,1536]{1,0:T(8,128)(2,1)} %get-tuple-element.44), channel_id=1, source_target_pairs={{0,2},{1,3},{2,0},{3,1},{4,6},{5,7},{6,4},{7,5},{8,10},{9,11},{10,... | collective-permute-start | bytes 1916936 | tf_op jit(solution)/shard_map/ppermute | solution.py:286
  25.4 12.5 %collective-permute-start.5 = (bf16[192,768]{1,0:T(8,128)(2,1)}, bf16[192,768]{1,0:T(8,128)(2,1)S(1)}, u32[]{:S(2)}, u32[]{:S(2)}) collective-permute-start(bf16[192,768]{1,0:T(8,128)(2,1)} %get-tuple-element.58), channel_id=1, source_target_pairs={{0,8},{4,12},{8,0},{12,4},{16,24},{20,28},{24,16},{28,20},{1,9},{5... | collective-permute-start | bytes 884744 | tf_op jit(solution)/shard_map/ppermute | solution.py:286
  26.0 13.7 %collective-permute-start.7 = (bf16[192,768]{1,0:T(8,128)(2,1)}, bf16[192,768]{1,0:T(8,128)(2,1)}, u32[]{:S(2)}, u32[]{:S(2)}) collective-permute-start(bf16[192,768]{1,0:T(8,128)(2,1)} %get-tuple-element.45.refs_0_), channel_id=1, source_target_pairs={{0,16},{4,20},{8,24},{12,28},{16,0},{20,4},{24,8},{28,12},{1,17},{... | collective-permute-start | bytes 884744 | tf_op jit(solution)/shard_map/ppermute | solution.py:286
  27.4 12.2 %collective-permute-start.8 = (bf16[192,768]{1,0:T(8,128)(2,1)}, bf16[192,768]{1,0:T(8,128)(2,1)}, u32[]{:S(2)}, u32[]{:S(2)}) collective-permute-start(bf16[192,768]{1,0:T(8,128)(2,1)} %collective-permute-done.2.refs_1_), channel_id=1, source_target_pairs={{0,4},{4,0},{8,12},{12,8},{16,20},{20,16},{24,28},{28,24},{1,5},{5... | collective-permute-start | bytes 884744 | tf_op jit(solution)/shard_map/ppermute | solution.py:286
  28.9 11.5 %collective-permute-start.9 = (bf16[192,768]{1,0:T(8,128)(2,1)}, bf16[192,768]{1,0:T(8,128)(2,1)}, u32[]{:S(2)}, u32[]{:S(2)}) collective-permute-start(bf16[192,768]{1,0:T(8,128)(2,1)} %collective-permute-done.1.refs_3_), channel_id=1, source_target_pairs={{0,4},{4,0},{8,12},{12,8},{16,20},{20,16},{24,28},{28,24},{1,5},{5... | collective-permute-start | bytes 884744 | tf_op jit(solution)/shard_map/ppermute | solution.py:286
  30.6 9.8 %copy-start.6 = (bf16[192,768]{1,0:T(8,128)(2,1)S(1)}, bf16[192,768]{1,0:T(8,128)(2,1)}, u32[]{:S(2)}) copy-start(bf16[192,768]{1,0:T(8,128)(2,1)} %get-tuple-element.58) | copy-start | bytes 884740
  30.6 12.0 %copy-start.13 = (bf16[96,1536]{1,0:T(8,128)(2,1)S(1)}, bf16[96,1536]{1,0:T(8,128)(2,1)}, u32[]{:S(2)}) copy-start(bf16[96,1536]{1,0:T(8,128)(2,1)} %get-tuple-element.50) | copy-start | bytes 884740
  40.4 12.8 %collective-permute-start.14 = (bf16[512,1536]{1,0:T(8,128)(2,1)S(1)}, bf16[512,1536]{1,0:T(8,128)(2,1)S(1)}, u32[]{:S(2)}, u32[]{:S(2)}) collective-permute-start(bf16[512,1536]{1,0:T(8,128)(2,1)S(1)} %layer_norm.2.outer.sibling.block), channel_id=1, source_target_pairs={{0,1},{1,0},{2,3},{3,2},{4,5},{5,4},{6,7},{7,6},{8,9},{9,8},{10,11... | collective-permute-start | bytes 4718600 | tf_op jit(solution)/shard_map/ppermute | solution.py:286
  40.5 12.7 %collective-permute-start.10 = (bf16[96,768]{1,0:T(8,128)(2,1)S(1)}, bf16[96,768]{1,0:T(8,128)(2,1)S(1)}, u32[]{:S(2)}, u32[]{:S(2)}) collective-permute-start(bf16[96,768]{1,0:T(8,128)(2,1)S(1)} %get-tuple-element.48), channel_id=1, source_target_pairs={{0,24},{4,28},{8,16},{12,20},{16,8},{20,12},{24,0},{28,4},{1,25},{... | collective-permute-start | bytes 442376 | tf_op jit(solution)/shard_map/ppermute | solution.py:286
  42.6 10.5 %collective-permute-start.11 = (bf16[96,1536]{1,0:T(8,128)(2,1)S(1)}, bf16[96,1536]{1,0:T(8,128)(2,1)S(1)}, u32[]{:S(2)}, u32[]{:S(2)}) collective-permute-start(bf16[96,1536]{1,0:T(8,128)(2,1)S(1)} %copy-done.13), channel_id=1, source_target_pairs={{0,2},{1,3},{2,0},{3,1},{4,6},{5,7},{6,4},{7,5},{8,10},{9,11},{10,... | collective-permute-start | bytes 884744 | tf_op jit(solution)/shard_map/ppermute | solution.py:286
  44.1 9.1 %collective-permute-start.12 = (bf16[192,768]{1,0:T(8,128)(2,1)}, bf16[192,768]{1,0:T(8,128)(2,1)S(1)}, u32[]{:S(2)}, u32[]{:S(2)}) collective-permute-start(bf16[192,768]{1,0:T(8,128)(2,1)} %collective-permute-done.7.refs_2_), channel_id=1, source_target_pairs={{0,4},{4,0},{8,12},{12,8},{16,20},{20,16},{24,28},{28,24},{1,5},{5... | collective-permute-start | bytes 884744 | tf_op jit(solution)/shard_map/ppermute | solution.py:286
  45.6 11.4 %copy-start.3 = (bf16[192,768]{1,0:T(8,128)(2,1)S(1)}, bf16[192,768]{1,0:T(8,128)(2,1)}, u32[]{:S(2)}) copy-start(bf16[192,768]{1,0:T(8,128)(2,1)} %get-tuple-element.45.refs_0_) | copy-start | bytes 884740
  45.6 11.4 %copy-start.5 = (bf16[192,768]{1,0:T(8,128)(2,1)S(1)}, bf16[192,768]{1,0:T(8,128)(2,1)}, u32[]{:S(2)}) copy-start(bf16[192,768]{1,0:T(8,128)(2,1)} %copy-done.4) | copy-start | bytes 884740
  45.7 7.5 %collective-permute-start.13 = (bf16[32,1536]{1,0:T(8,128)(2,1)S(1)}, bf16[32,1536]{1,0:T(8,128)(2,1)S(1)}, u32[]{:S(2)}, u32[]{:S(2)}) collective-permute-start(bf16[32,1536]{1,0:T(8,128)(2,1)S(1)} %pad_maximum_fusion), channel_id=1, source_target_pairs={{0,3},{1,2},{2,1},{3,0},{4,7},{5,6},{6,5},{7,4},{8,11},{9,10},{10,... | collective-permute-start | bytes 294920 | tf_op jit(solution)/shard_map/ppermute | solution.py:286
  54.7 10.0 %collective-permute-start.18 = (bf16[512,1536]{1,0:T(8,128)(2,1)S(1)}, bf16[512,1536]{1,0:T(8,128)(2,1)S(1)}, u32[]{:S(2)}, u32[]{:S(2)}) collective-permute-start(bf16[512,1536]{1,0:T(8,128)(2,1)S(1)} %layer_norm.3.block.sibling.outer), channel_id=1, source_target_pairs={{0,1},{1,0},{2,3},{3,2},{4,5},{5,4},{6,7},{7,6},{8,9},{9,8},{10,11... | collective-permute-start | bytes 4718600 | tf_op jit(solution)/shard_map/ppermute | solution.py:286
  55.2 3.3 %copy-start.2 = (bf16[31,1536]{1,0:T(8,128)(2,1)S(1)}, bf16[31,1536]{1,0:T(8,128)(2,1)}, u32[]{:S(2)}) copy-start(bf16[31,1536]{1,0:T(8,128)(2,1)} %kernel.7) | copy-start | bytes 285700
  55.2 9.4 %collective-permute-start.16 = (bf16[96,768]{1,0:T(8,128)(2,1)S(1)}, bf16[96,768]{1,0:T(8,128)(2,1)S(1)}, u32[]{:S(2)}, u32[]{:S(2)}) collective-permute-start(bf16[96,768]{1,0:T(8,128)(2,1)S(1)} %get-tuple-element.55), channel_id=1, source_target_pairs={{0,24},{4,28},{8,16},{12,20},{16,8},{20,12},{24,0},{28,4},{1,25},{... | collective-permute-start | bytes 442376 | tf_op jit(solution)/shard_map/ppermute | solution.py:286
  61.9 17.8 %collective-permute-start.21 = (bf16[512,384]{1,0:T(8,128)(2,1)S(1)}, bf16[512,384]{1,0:T(8,128)(2,1)S(1)}, u32[]{:S(2)}, u32[]{:S(2)}) collective-permute-start(bf16[512,384]{1,0:T(8,128)(2,1)S(1)} %expand_and_depthwise.4), channel_id=1, source_target_pairs={{0,2},{1,3},{2,0},{3,1},{4,6},{5,7},{6,4},{7,5},{8,10},{9,11},{10,... | collective-permute-start | bytes 1179656 | tf_op jit(solution)/shard_map/ppermute | solution.py:286
  63.1 13.1 %collective-permute-start.15 = (bf16[192,768]{1,0:T(8,128)(2,1)S(1)}, bf16[192,768]{1,0:T(8,128)(2,1)S(1)}, u32[]{:S(2)}, u32[]{:S(2)}) collective-permute-start(bf16[192,768]{1,0:T(8,128)(2,1)S(1)} %collective-permute-done.5.refs_0_), channel_id=1, source_target_pairs={{0,4},{4,0},{8,12},{12,8},{16,20},{20,16},{24,28},{28,24},{1,5},{5... | collective-permute-start | bytes 884744 | tf_op jit(solution)/shard_map/ppermute | solution.py:286
  64.6 15.1 %collective-permute-start.20 = (bf16[192,768]{1,0:T(8,128)(2,1)S(1)}, bf16[192,768]{1,0:T(8,128)(2,1)S(1)}, u32[]{:S(2)}, u32[]{:S(2)}) collective-permute-start(bf16[192,768]{1,0:T(8,128)(2,1)S(1)} %copy-done.6), channel_id=1, source_target_pairs={{0,16},{4,20},{8,24},{12,28},{16,0},{20,4},{24,8},{28,12},{1,17},{... | collective-permute-start | bytes 884744 | tf_op jit(solution)/shard_map/ppermute | solution.py:286
  64.7 11.6 %collective-permute-start.17 = (bf16[96,768]{1,0:T(8,128)(2,1)S(1)}, bf16[96,768]{1,0:T(8,128)(2,1)S(1)}, u32[]{:S(2)}, u32[]{:S(2)}) collective-permute-start(bf16[96,768]{1,0:T(8,128)(2,1)S(1)} %collective-permute-done.10.refs_1_), channel_id=1, source_target_pairs={{0,4},{4,0},{8,12},{12,8},{16,20},{20,16},{24,28},{28,24},{1,5},{5... | collective-permute-start | bytes 442376 | tf_op jit(solution)/shard_map/ppermute | solution.py:286
  65.6 14.1 %collective-permute-start.19 = (bf16[96,768]{1,0:T(8,128)(2,1)S(1)}, bf16[96,768]{1,0:T(8,128)(2,1)S(1)}, u32[]{:S(2)}, u32[]{:S(2)}) collective-permute-start(bf16[96,768]{1,0:T(8,128)(2,1)S(1)} %collective-permute-done.16.refs_4_), channel_id=1, source_target_pairs={{0,4},{4,0},{8,12},{12,8},{16,20},{20,16},{24,28},{28,24},{1,5},{5... | collective-permute-start | bytes 442376 | tf_op jit(solution)/shard_map/ppermute | solution.py:286
  79.7 15.5 %copy-start.1 = (bf16[192,1536]{1,0:T(8,128)(2,1)S(1)}, bf16[192,1536]{1,0:T(8,128)(2,1)}, u32[]{:S(2)}) copy-start(bf16[192,1536]{1,0:T(8,128)(2,1)} %whole.1) | copy-start | bytes 1769476
  79.8 8.9 %collective-permute-start.22 = (bf16[192,768]{1,0:T(8,128)(2,1)S(1)}, bf16[192,768]{1,0:T(8,128)(2,1)S(1)}, u32[]{:S(2)}, u32[]{:S(2)}) collective-permute-start(bf16[192,768]{1,0:T(8,128)(2,1)S(1)} %collective-permute-done.20.refs_7_), channel_id=1, source_target_pairs={{0,4},{4,0},{8,12},{12,8},{16,20},{20,16},{24,28},{28,24},{1,5},{5... | collective-permute-start | bytes 884744 | tf_op jit(solution)/shard_map/ppermute | solution.py:286
  81.3 1.4 %collective-permute-start.24 = (bf16[96,768]{1,0:T(8,128)(2,1)S(1)}, bf16[96,768]{1,0:T(8,128)(2,1)S(1)}, u32[]{:S(2)}, u32[]{:S(2)}) collective-permute-start(bf16[96,768]{1,0:T(8,128)(2,1)S(1)} %collective-permute-done.10.refs_1_), channel_id=1, source_target_pairs={{0,1},{1,0},{2,3},{3,2},{4,5},{5,4},{6,7},{7,6},{8,9},{9,8},{10,11... | collective-permute-start | bytes 442376 | tf_op jit(solution)/shard_map/ppermute | solution.py:286
  81.3 11.0 %collective-permute-start.23 = (bf16[192,768]{1,0:T(8,128)(2,1)S(1)}, bf16[192,768]{1,0:T(8,128)(2,1)S(1)}, u32[]{:S(2)}, u32[]{:S(2)}) collective-permute-start(bf16[192,768]{1,0:T(8,128)(2,1)S(1)} %collective-permute-done.5.refs_0_), channel_id=1, source_target_pairs={{0,1},{1,0},{2,3},{3,2},{4,5},{5,4},{6,7},{7,6},{8,9},{9,8},{10,11... | collective-permute-start | bytes 884744 | tf_op jit(solution)/shard_map/ppermute | solution.py:286
  81.8 11.1 %collective-permute-start.25 = (bf16[192,768]{1,0:T(8,128)(2,1)S(1)}, bf16[192,768]{1,0:T(8,128)(2,1)S(1)}, u32[]{:S(2)}, u32[]{:S(2)}) collective-permute-start(bf16[192,768]{1,0:T(8,128)(2,1)S(1)} %collective-permute-done.4.refs_2_), channel_id=1, source_target_pairs={{0,1},{1,0},{2,3},{3,2},{4,5},{5,4},{6,7},{7,6},{8,9},{9,8},{10,11... | collective-permute-start | bytes 884744 | tf_op jit(solution)/shard_map/ppermute | solution.py:286
  81.8 11.6 %collective-permute-start.32 = (bf16[512,384]{1,0:T(8,128)(2,1)S(1)}, bf16[512,384]{1,0:T(8,128)(2,1)S(1)}, u32[]{:S(2)}, u32[]{:S(2)}) collective-permute-start(bf16[512,384]{1,0:T(8,128)(2,1)S(1)} %expand_and_depthwise.6), channel_id=1, source_target_pairs={{0,1},{1,0},{2,3},{3,2},{4,5},{5,4},{6,7},{7,6},{8,9},{9,8},{10,11... | collective-permute-start | bytes 1179656 | tf_op jit(solution)/shard_map/ppermute | solution.py:286
  82.7 11.1 %collective-permute-start.33 = (bf16[512,384]{1,0:T(8,128)(2,1)S(1)}, bf16[512,384]{1,0:T(8,128)(2,1)S(1)}, u32[]{:S(2)}, u32[]{:S(2)}) collective-permute-start(bf16[512,384]{1,0:T(8,128)(2,1)S(1)} %expand_and_depthwise.5), channel_id=1, source_target_pairs={{0,3},{1,2},{2,1},{3,0},{4,7},{5,6},{6,5},{7,4},{8,11},{9,10},{10,... | collective-permute-start | bytes 1179656 | tf_op jit(solution)/shard_map/ppermute | solution.py:286
  88.7 4.2 %collective-permute-start.26 = (bf16[192,768]{1,0:T(8,128)(2,1)S(1)}, bf16[192,768]{1,0:T(8,128)(2,1)S(1)}, u32[]{:S(2)}, u32[]{:S(2)}) collective-permute-start(bf16[192,768]{1,0:T(8,128)(2,1)S(1)} %collective-permute-done.15.refs_3_), channel_id=1, source_target_pairs={{0,1},{1,0},{2,3},{3,2},{4,5},{5,4},{6,7},{7,6},{8,9},{9,8},{10,11... | collective-permute-start | bytes 884744 | tf_op jit(solution)/shard_map/ppermute | solution.py:286
  92.3 2.8 %collective-permute-start.30 = (bf16[192,768]{1,0:T(8,128)(2,1)S(1)}, bf16[192,768]{1,0:T(8,128)(2,1)S(1)}, u32[]{:S(2)}, u32[]{:S(2)}) collective-permute-start(bf16[192,768]{1,0:T(8,128)(2,1)S(1)} %collective-permute-done.20.refs_7_), channel_id=1, source_target_pairs={{0,1},{1,0},{2,3},{3,2},{4,5},{5,4},{6,7},{7,6},{8,9},{9,8},{10,11... | collective-permute-start | bytes 884744 | tf_op jit(solution)/shard_map/ppermute | solution.py:286
  92.8 2.3 %collective-permute-start.31 = (bf16[192,768]{1,0:T(8,128)(2,1)S(1)}, bf16[192,768]{1,0:T(8,128)(2,1)S(1)}, u32[]{:S(2)}, u32[]{:S(2)}) collective-permute-start(bf16[192,768]{1,0:T(8,128)(2,1)S(1)} %collective-permute-done.22.refs_8_), channel_id=1, source_target_pairs={{0,1},{1,0},{2,3},{3,2},{4,5},{5,4},{6,7},{7,6},{8,9},{9,8},{10,11... | collective-permute-start | bytes 884744 | tf_op jit(solution)/shard_map/ppermute | solution.py:286
  92.9 1.7 %collective-permute-start.27 = (bf16[96,768]{1,0:T(8,128)(2,1)S(1)}, bf16[96,768]{1,0:T(8,128)(2,1)S(1)}, u32[]{:S(2)}, u32[]{:S(2)}) collective-permute-start(bf16[96,768]{1,0:T(8,128)(2,1)S(1)} %collective-permute-done.16.refs_4_), channel_id=1, source_target_pairs={{0,1},{1,0},{2,3},{3,2},{4,5},{5,4},{6,7},{7,6},{8,9},{9,8},{10,11... | collective-permute-start | bytes 442376 | tf_op jit(solution)/shard_map/ppermute | solution.py:286
  93.4 1.5 %collective-permute-start.28 = (bf16[96,768]{1,0:T(8,128)(2,1)S(1)}, bf16[96,768]{1,0:T(8,128)(2,1)S(1)}, u32[]{:S(2)}, u32[]{:S(2)}) collective-permute-start(bf16[96,768]{1,0:T(8,128)(2,1)S(1)} %collective-permute-done.17.refs_5_), channel_id=1, source_target_pairs={{0,1},{1,0},{2,3},{3,2},{4,5},{5,4},{6,7},{7,6},{8,9},{9,8},{10,11... | collective-permute-start | bytes 442376 | tf_op jit(solution)/shard_map/ppermute | solution.py:286
  93.7 1.4 %collective-permute-start.29 = (bf16[96,768]{1,0:T(8,128)(2,1)S(1)}, bf16[96,768]{1,0:T(8,128)(2,1)S(1)}, u32[]{:S(2)}, u32[]{:S(2)}) collective-permute-start(bf16[96,768]{1,0:T(8,128)(2,1)S(1)} %collective-permute-done.19.refs_6_), channel_id=1, source_target_pairs={{0,1},{1,0},{2,3},{3,2},{4,5},{5,4},{6,7},{7,6},{8,9},{9,8},{10,11... | collective-permute-start | bytes 442376 | tf_op jit(solution)/shard_map/ppermute | solution.py:286

commit v3 on v2

--- a/solution.py
+++ b/solution.py
@@ -24,12 +24,10 @@
 
 GAIN, NBIAS, VBIAS, GBIAS, BSCALE, BSHIFT, PBIAS = range(7)
 EDGE = 16
-PIECES = (208, 416)
 FREE = pl.CostEstimate(flops=0, bytes_accessed=0, transcendentals=0)
 
 
-def cut_body(cuts, signal, expand, project, first, second, *refs):
-    pieces, sems = refs[:-1], refs[-1]
+def cut_body(expand, project, first, second, both, sems):
     seq = lax.axis_index("seq")
     share = first.shape[1] // 2
     half = second.shape[1]
@@ -41,37 +39,38 @@
 
     for side in range(2):
         at = pl.ds(pl.multiple_of(side * width + seq * share, LANES), share)
-        add(expand.at[:, at], first.at[:, side * share : (side + 1) * share])
-    add(project.at[:, pl.ds(pl.multiple_of((seq & 1) * half, LANES), half)], second)
-    for (start, stop), piece in zip(cuts, pieces):
-        add(signal.at[start:stop], piece)
+        for target in (first, both):
+            add(expand.at[:, at], target.at[:, side * share : (side + 1) * share])
+    at = pl.ds(pl.multiple_of((seq & 1) * half, LANES), half)
+    add(project.at[:, at], second)
+    add(project.at[:, at], both.at[:, 2 * share :])
     for copy in copies:
         copy.start()
     for copy in copies:
         copy.wait()
 
 
-def cut(cuts, signal, expand, project, parts):
+def cut(expand, project, parts):
     rows, width = project.shape
-    share = width // parts
-    shapes = [(rows, 2 * share), (rows, width // 2)] + [(b - a, width) for a, b in cuts]
+    shapes = [(rows, 2 * width // parts), (rows, width // 2)]
+    shapes.append((rows, shapes[0][1] + shapes[1][1]))
     return pl.pallas_call(
-        functools.partial(cut_body, cuts),
-        in_specs=[ANY] * 3,
+        cut_body,
+        in_specs=[ANY] * 2,
         out_specs=[VMEM] * len(shapes),
         out_shape=[jax.ShapeDtypeStruct(shape, expand.dtype) for shape in shapes],
-        scratch_shapes=[pltpu.SemaphoreType.DMA((len(cuts) + 3,))],
+        scratch_shapes=[pltpu.SemaphoreType.DMA((6,))],
         compiler_params=params(LARGE),
         cost_estimate=FREE,
-        name="cut",
-    )(signal, expand, project)
+        name="cut_weights",
+    )(expand, project)
 
 
 def norm_body(packed, *refs):
     pieces, out = refs[:-1], refs[-1]
     base = 0
     for piece in pieces:
-        tile = next(t for t in (128, 104, 96, 16) if piece.shape[0] % t == 0)
+        tile = next(t for t in (128, 64, 16) if piece.shape[0] % t == 0)
 
         def one(i, _, piece=piece, base=base, tile=tile):
             at = pl.multiple_of(i * tile, tile)
@@ -105,12 +104,14 @@
 def gather_body(places, *refs):
     pieces, out, sems = refs[: len(places)], refs[-2], refs[-1]
     dp = lax.axis_index("dp")
-    rows = pieces[0].shape[0]
+    rows, cols = pieces[0].shape[0], out.shape[1]
     copies = []
-    for piece, (bits, first) in zip(pieces, places):
-        at = pl.multiple_of((dp ^ bits) * rows + first, 16)
+    for i, (piece, (bits, first)) in enumerate(zip(pieces, places)):
+        at = i * rows if bits is None else pl.multiple_of((dp ^ bits) * rows, 16)
         copies.append(
-            pltpu.make_async_copy(piece, out.at[pl.ds(at, piece.shape[0])], sems.at[len(copies)])
+            pltpu.make_async_copy(
+                piece.at[:, first : first + cols], out.at[pl.ds(at, rows)], sems.at[i]
+            )
         )
     for copy in copies:
         copy.start()
@@ -119,12 +120,12 @@
 
 
 def gather(places, pieces):
-    rows = sum(piece.shape[0] for piece in pieces)
+    rows, cols = pieces[0].shape
     return pl.pallas_call(
         functools.partial(gather_body, places),
         in_specs=[ANY] * len(pieces),
         out_specs=VMEM,
-        out_shape=jax.ShapeDtypeStruct((rows, pieces[0].shape[1]), pieces[0].dtype),
+        out_shape=jax.ShapeDtypeStruct((rows * len(pieces), cols), pieces[0].dtype),
         scratch_shapes=[pltpu.SemaphoreType.DMA((len(pieces),))],
         compiler_params=params(),
         cost_estimate=FREE,
@@ -132,10 +133,12 @@
     )(*pieces)
 
 
-def conv_body(across_x, across_core, packed, kernel, weight, block, sibling, outer, out, frames, gated, taps):
+def conv_body(across_x, across_core, packed, kernel, weight, block, sibling, outer, *refs):
     seq = lax.axis_index("seq")
     chip, odd = (seq >> 1) ^ across_x, (seq & 1) ^ across_core
-    length, channels = out.shape
+    outs, (frames, gated, taps) = refs[:-3], refs[-3:]
+    part, channels = outs[0].shape
+    length = part * len(outs)
     count = kernel.shape[0]
     half = (count - 1) // 2
     lanes = [
@@ -178,7 +181,8 @@
                 first = start + EDGE - half + t
                 depth = depth + taps[b, t : t + 1, :] * gated[b, first : first + step, :]
             scaled = depth * scale + shift
-            out[start : start + step, b * LANES : (b + 1) * LANES] = (
+            at = start % part
+            outs[start // part][at : at + step, b * LANES : (b + 1) * LANES] = (
                 scaled * sigmoid(scaled)
             ).astype(jnp.bfloat16)
 
@@ -189,15 +193,15 @@
     depthwise(len(lanes) - 1)
 
 
-def conv(across_x, across_core, packed, kernel, weight, block, sibling, outer):
+def conv(across_x, across_core, parts, packed, kernel, weight, block, sibling, outer):
     length, width = block.shape
     channels = weight.shape[1] // 2
     extent = length + 2 * EDGE
     return pl.pallas_call(
         functools.partial(conv_body, across_x, across_core),
         in_specs=[VMEM] * 6,
-        out_specs=VMEM,
-        out_shape=jax.ShapeDtypeStruct((length, channels), jnp.bfloat16),
+        out_specs=[VMEM] * parts,
+        out_shape=[jax.ShapeDtypeStruct((length // parts, channels), jnp.bfloat16)] * parts,
         scratch_shapes=[
             pltpu.VMEM((extent, width), jnp.bfloat16),
             pltpu.VMEM((channels // LANES, extent, LANES), jnp.float32),
@@ -209,13 +213,13 @@
     )(packed, kernel, weight, block, sibling, outer)
 
 
-def project_body(places, packed, signal, whole, *refs):
-    count = 2 * len(places)
-    pieces, acts, out = refs[:count], refs[count : count + 4], refs[count + 4]
-    weight, left, frames, result, sems = refs[count + 5 :]
+def project_body(places, spots, packed, signal, whole, *refs):
+    count = 1 + max(which for side in places for which, _, _ in side)
+    pieces, acts, out = refs[:count], refs[count:-6], refs[-6]
+    weight, left, frames, result, sems = refs[-5:]
     seq, dp = lax.axis_index("seq"), lax.axis_index("dp")
     share = acts[0].shape[1]
-    rows, cols = whole.shape[0], pieces[0].shape[1]
+    rows, cols = whole.shape[0], weight.shape[2]
     length = out.shape[0]
     tile = 256
     copies = []
@@ -225,20 +229,20 @@
         copies[-1].start()
 
     ats = [pl.ds(pl.multiple_of(((seq & 1) ^ side) * cols, LANES), cols) for side in range(2)]
+    split = []
     for side in range(2):
-        sources = [(whole.at[:, ats[side]], 0, 0)]
-        sources += [
-            (piece, *place) for piece, place in zip(pieces[side * len(places) :], places)
-        ]
-        for source, bits, first in sources:
-            at = pl.ds(pl.multiple_of((dp ^ bits) * rows + first, 16), source.shape[0])
-            add(source, weight.at[side, at])
+        add(whole.at[:, ats[side]], weight.at[side, pl.ds(pl.multiple_of(dp * rows, 16), rows)])
+        for which, first, bits in places[side]:
+            add(
+                pieces[which].at[first : first + rows],
+                weight.at[side, pl.ds(pl.multiple_of((dp ^ bits) * rows, 16), rows)],
+            )
         if side == 0:
-            for k in range(4):
+            for act, (k, first) in zip(acts, spots):
                 at = pl.ds(pl.multiple_of((seq ^ k) * share, LANES), share)
-                add(acts[k], left.at[:, at])
+                add(act, left.at[first : first + act.shape[0], at])
             add(signal, frames)
-    split = len(places) + 6
+            split = len(copies)
     parts = []
     for side, ready in enumerate((copies[:split], copies[split:])):
         for copy in ready:
@@ -261,11 +265,11 @@
         part.wait()
 
 
-def project(packed, signal, whole, places, mine, other, acts):
+def project(packed, signal, whole, places, pieces, spots, acts):
     length, width = signal.shape
     return pl.pallas_call(
-        functools.partial(project_body, places),
-        in_specs=[VMEM] + [ANY] * (2 + 2 * len(places) + 4),
+        functools.partial(project_body, places, spots),
+        in_specs=[VMEM] + [ANY] * (2 + len(pieces) + len(acts)),
         out_specs=ANY,
         out_shape=jax.ShapeDtypeStruct((length, width), jnp.bfloat16),
         scratch_shapes=[
@@ -273,12 +277,12 @@
             pltpu.VMEM((length, width), jnp.bfloat16),
             pltpu.VMEM((length, width), jnp.bfloat16),
             pltpu.VMEM((2, length, width // 2), jnp.bfloat16),
-            pltpu.SemaphoreType.DMA((2 * len(places) + 7 + 2 * (length // 256),)),
+            pltpu.SemaphoreType.DMA((sum(map(len, places)) + 3 + len(acts) + 2 * (length // 256),)),
         ],
         compiler_params=params(),
         cost_estimate=FREE,
         name="project_and_residual",
-    )(packed, signal, whole, *mine, *other, *acts)
+    )(packed, signal, whole, *pieces, *acts)
 
 
 def across(array, axis, bits):
@@ -296,18 +300,13 @@
 ):
     width = signal.shape[2]
     own = signal[0]
-    length = own.shape[0]
-    marks = [0, PIECES[0], PIECES[1], length]
-    cuts = list(zip(marks[:-1], marks[1:]))
-    e_own, p_own, *pieces = cut(cuts, own, expand_weight, project_weight, 4)
-    fold = p_own.shape[0] // 2
-
-    facing = [across(pieces[0], "seq", 2)]
+    e_own, p_own, both = cut(expand_weight, project_weight, 4)
+    beside = across(own, "seq", 1)
+    facing = across(after(own, e_own), "seq", 2)
     e_far, e_near = across(e_own, "dp", 6), across(e_own, "dp", 2)
-    ey_own, py_own = across(e_own, "dp", 1), across(p_own, "dp", 1)
-    done = (facing[0], e_far, e_near, ey_own, py_own)
-
-    facing.append(across(after(pieces[1], *done), "seq", 2))
+    y_own = across(both, "dp", 1)
+    done = (e_far, e_near, y_own)
+
     e_middle = across(after(e_own, *done), "dp", 4)
     p_near = across(after(p_own, *done), "dp", 2)
     ey_near, ey_far = across(after(e_near, *done), "dp", 1), across(after(e_far, *done), "dp", 1)
@@ -319,51 +318,57 @@
         .astype(jnp.float32)
     )
     normed = norm(packed, own)
+    beside = norm(packed, beside)
     edges = jnp.concatenate([normed[:EDGE], normed[-EDGE:]], axis=0)
-    done = (facing[1], e_middle, p_near, ey_near, ey_far)
-
-    facing.append(across(after(pieces[2], *done), "seq", 2))
+    done = (facing, e_middle, p_near, ey_near, ey_far, beside, edges)
+
     ey_middle = across(after(e_middle, *done), "dp", 1)
-    p_far = [across(after(p_own[:fold], *done), "dp", 6)]
+    p_far = across(after(p_own, *done), "dp", 6)
     edges = across(after(edges, *done), "seq", 3)
-    beside = across(after(normed, *done), "seq", 1)
-    e_shards = [e_own, e_near, e_middle, e_far, ey_own, ey_near, ey_middle, ey_far]
-    done = (facing[2], ey_middle, p_far[0], edges, beside)
-
-    normed_facing = norm(packed, after(facing[0], *done), *facing[1:])
+    py_near = across(after(p_near, *done), "dp", 1)
+    normed_facing = norm(packed, after(facing, *done))
     diagonal = across(normed_facing, "seq", 1)
-    p_far.append(across(after(p_own[fold:], *done), "dp", 6))
-    py_near = across(after(p_near, *done), "dp", 1)
-    py_far = [across(p_far[0], "dp", 1)]
+    e_shards = [e_own, e_near, e_middle, e_far, y_own, ey_near, ey_middle, ey_far]
     weight = gather([(2 * (k % 4) + k // 4, 0) for k in range(8)], e_shards)
+    done = (ey_middle, edges, diagonal)
+
     run = functools.partial(conv, packed=packed, kernel=depth_kernel, weight=weight)
-    part_facing = run(1, 0, block=normed_facing, sibling=edges, outer=beside)
-    done = (part_facing, diagonal, p_far[1])
-
-    act_facing = across(part_facing, "seq", 2)
-    p_middle = across(after(p_own, *done), "dp", 4)
-    py_far.append(across(after(p_far[1], *done), "dp", 1))
-    part_diagonal = run(1, 1, block=after(diagonal, *done), sibling=normed_facing, outer=normed)
-    done = (part_diagonal, py_near, py_far[0])
-
+    part_facing = run(
+        1, 0, 2, block=after(normed_facing, *done), sibling=edges, outer=beside
+    )
+    act_facing = [across(part, "seq", 2) for part in part_facing]
+    p_middle = across(after(p_own, ey_middle, edges), "dp", 4)
+    py_far = across(after(p_far, part_facing[0]), "dp", 1)
+    done = (part_facing[0], p_far, py_near)
+
+    [part_diagonal] = run(
+        1, 1, 1, block=after(diagonal, *done), sibling=normed_facing, outer=normed
+    )
     act_diagonal = across(part_diagonal, "seq", 3)
-    swap = lambda array: across(after(array, *done), "seq", 1)
-    p_mine = [p_near, p_far[0], py_own, py_near]
-    p_other = [swap(piece) for piece in p_mine]
-    part_beside = run(0, 1, block=after(beside, *done), sibling=normed, outer=normed_facing)
-    done = (part_beside, p_middle, py_far[1], act_facing)
-
+    [part_beside] = run(
+        0, 1, 1, block=after(beside, part_diagonal), sibling=normed, outer=normed_facing
+    )
     act_beside = across(part_beside, "seq", 1)
-    py_middle = across(after(p_middle, *done), "dp", 1)
-    late = [p_far[1], py_far[0], py_far[1], p_middle]
-    p_mine += late
-    p_other += [swap(piece) for piece in late]
-    part_own = run(0, 0, block=after(normed, *done), sibling=beside, outer=diagonal)
-    p_mine.append(py_middle)
-    p_other.append(across(after(py_middle, part_own), "seq", 1))
-    places = [(2, 0), (6, 0), (1, 0), (3, 0), (6, fold), (7, 0), (7, fold), (4, 0), (5, 0)]
-    acts = [part_own, act_beside, act_facing, act_diagonal]
-    return project(packed, own, project_weight, places, p_mine, p_other, acts)[None]
+    [part_own] = run(
+        0, 0, 1, block=after(normed, part_beside, py_far, *act_facing), sibling=beside, outer=diagonal
+    )
+    py_middle = across(after(p_middle, part_own), "dp", 1)
+    columns = e_own.shape[1]
+    early = gather([(None, 0), (None, columns)], [after(p_near, ey_middle), y_own])
+    early_other = across(early, "seq", 1)
+    late = [py_near, p_far, py_far, p_middle, py_middle]
+    done = (part_own, act_diagonal, early_other)
+    swapped = [across(after(shard, *done), "seq", 1) for shard in late]
+    rows = e_own.shape[0]
+    places = [
+        [((1 + len(late)) * side, rows * k, bits) for k, bits in enumerate([2, 1])]
+        + [((1 + len(late)) * side + 1 + k, 0, bits) for k, bits in enumerate([3, 6, 7, 4, 5])]
+        for side in range(2)
+    ]
+    acts = [part_own, act_beside, act_diagonal, *act_facing]
+    tall = own.shape[0] // len(act_facing)
+    spots = [(0, 0), (1, 0), (3, 0)] + [(2, tall * k) for k in range(len(act_facing))]
+    return project(packed, own, project_weight, places, [early, *late, early_other, *swapped], spots, acts)[None]
 
 
 def extended(block, sides, width):

time: 102 us -> 93.6 us (0.918)
  waiting for transfers between devices: 41.3 us -> 36.2 us
  starting transfers between devices: 30.6 us -> 26.7 us
    ppermute x34 -> x27, waiting for transfers between devices: 41.3 us -> 36.2 us  [across(): return lax.ppermute(array, axis, [(i, i ^ bits) for i in range(count)])]
    pallas_call x2 -> x3, Pallas kernels: 2.76 us -> 6.68 us  [norm(): pl.pallas_call(norm_body, in_specs=[VMEM] * (1 + len(pieces)), out_specs=...]
    ppermute x34 -> x27, starting transfers between devices: 30.6 us -> 26.7 us  [across(): return lax.ppermute(array, axis, [(i, i ^ bits) for i in range(count)])]
    pallas_call x2, Pallas kernels: 9.79 us -> 7.51 us  [the longest x1 5.08 us: project(): pl.pallas_call(functools.partial(project_body, places, spots), in_specs=[...]
  transfers between devices with their start and end apart: 34 -> 27, of which waited for: 15 -> 9; matrix products, arithmetic and copies ran while one was open for 1% -> 1% of each run, Pallas kernels for 16% -> 22%
where the time goes in v3:
time: 93.6 us; the launch traced here: 93.4 us
  waiting for transfers between devices  36.2 us (39%)
  Pallas kernels  28.8 us (31%)
  starting transfers between devices  26.7 us (29%)
  local copies, waits for them, and re-layouts  1.23 us (1%)
    ppermute x27, waiting for transfers between devices, across(): return lax.ppermute(array, axis, [(i, i ^ bits) for i in range(count)])  36.2 us
    ppermute x27, starting transfers between devices, across(): return lax.ppermute(array, axis, [(i, i ^ bits) for i in range(count)])  26.7 us
    pallas_call x4, Pallas kernels, conv(): pl.pallas_call(functools.partial(conv_body, across_x, across_core), in_sp...  13.7 us
    pallas_call x3, Pallas kernels, norm(): pl.pallas_call(norm_body, in_specs=[VMEM] * (1 + len(pieces)), out_specs=...  6.68 us
    pallas_call x1, Pallas kernels, project(): pl.pallas_call(functools.partial(project_body, places, spots), in_specs=[...  5.08 us
    pallas_call x1, Pallas kernels, cut(): pl.pallas_call(cut_body, in_specs=[ANY] * 2, out_specs=[VMEM] * len(shape...  2.43 us
  transfers between devices with their start and end apart: 27, of which 9 were waited for; matrix products, arithmetic and copies ran while one was open for 1% of the time, Pallas kernels for 22%

profile of v3, /device:TPU:0, one launch (start us, length us, event | category | flops | bytes accessed | tf_op | source)
XLA Modules:
  0.0 93.4 jit_solution(1087301405200560127)
XLA Ops:
  0.0 0.5 collective-permute-start.8
  0.6 2.4 %cut_weights.1 = (bf16[192,768]{1,0:T(8,128)(2,1)}, bf16[192,768]{1,0:T(8,128)(2,1)}, bf16[192,1536]{1,0:T(8,128)(2,1)}) custom-call(bf16[192,3072]{1,0:T(8,128)(2,1)} %expand.1, bf16[192,1536]{1,0:T(8,128)(2,1)} %whole.1), custom_call_target="tpu_custom_call" | custom-call | tf_op jit(solution)/shard_map/cut_weights/pallas_call | solution.py:57
  3.0 2.6 %collective-permute-start.5 = (bf16[512,1536]{1,0:T(8,128)(2,1)S(1)}, bf16[512,1536]{1,0:T(8,128)(2,1)}, u32[]{:S(2)}, u32[]{:S(2)}) collective-permute-start(bf16[512,1536]{1,0:T(8,128)(2,1)S(1)} %bitcast.3), channel_id=1, source_target_pairs={{0,2},{1,3},{2,0},{3,1},{4,6},{5,7},{6,4},{7,5},{8,10},{9,11},{10,... | collective-permute-start | bytes 4718600 | tf_op jit(solution)/shard_map/ppermute | solution.py:290
  5.7 1.5 %collective-permute-start.2 = (bf16[192,1536]{1,0:T(8,128)(2,1)}, bf16[192,1536]{1,0:T(8,128)(2,1)S(1)}, u32[]{:S(2)}, u32[]{:S(2)}) collective-permute-start(bf16[192,1536]{1,0:T(8,128)(2,1)} %get-tuple-element.35), channel_id=1, source_target_pairs={{0,4},{4,0},{8,12},{12,8},{16,20},{20,16},{24,28},{28,24},{1,5},{5... | collective-permute-start | bytes 1769480 | tf_op jit(solution)/shard_map/ppermute | solution.py:290
  7.2 3.6 %collective-permute-start = (bf16[192,768]{1,0:T(8,128)(2,1)}, bf16[192,768]{1,0:T(8,128)(2,1)S(1)}, u32[]{:S(2)}, u32[]{:S(2)}) collective-permute-start(bf16[192,768]{1,0:T(8,128)(2,1)} %get-tuple-element.39.refs_0_), channel_id=1, source_target_pairs={{0,24},{4,28},{8,16},{12,20},{16,8},{20,12},{24,0},{28,4},{1,25},{... | collective-permute-start | bytes 884744 | tf_op jit(solution)/shard_map/ppermute | solution.py:290
  10.8 0.0 collective-permute-start.1
  10.8 8.3 %collective-permute-done.refs_3_ = bf16[192,768]{1,0:T(8,128)(2,1)S(1)} collective-permute-done((bf16[192,768]{1,0:T(8,128)(2,1)}, bf16[192,768]{1,0:T(8,128)(2,1)S(1)}, u32[]{:S(2)}, u32[]{:S(2)}) %collective-permute-start) | collective-permute-done | bytes 294944 | tf_op jit(solution)/shard_map/ppermute | solution.py:290
  19.1 5.3 %collective-permute-done.1.refs_1_ = bf16[192,768]{1,0:T(8,128)(2,1)S(1)} collective-permute-done((bf16[192,768]{1,0:T(8,128)(2,1)}, bf16[192,768]{1,0:T(8,128)(2,1)S(1)}, u32[]{:S(2)}, u32[]{:S(2)}) %collective-permute-start.1) | collective-permute-done | bytes 294944 | tf_op jit(solution)/shard_map/ppermute | solution.py:290
  24.4 0.0 collective-permute-done.2.refs_1_.refs_4_
  24.5 0.2 dynamic-update-slice
  24.7 0.3 dynamic-update-slice.1
  25.0 0.3 dynamic-update-slice.3
  25.3 0.3 dynamic-update-slice.4
  25.6 0.1 reshape.3.packed
  25.6 1.8 %collective-permute-start.3 = (bf16[192,768]{1,0:T(8,128)(2,1)}, bf16[192,768]{1,0:T(8,128)(2,1)S(1)}, u32[]{:S(2)}, u32[]{:S(2)}) collective-permute-start(bf16[192,768]{1,0:T(8,128)(2,1)} %get-tuple-element.52), channel_id=1, source_target_pairs={{0,8},{4,12},{8,0},{12,4},{16,24},{20,28},{24,16},{28,20},{1,9},{5... | collective-permute-start | bytes 884744 | tf_op jit(solution)/shard_map/ppermute | solution.py:290
  27.4 0.5 collective-permute-start.4
  27.9 0.5 collective-permute-start.6
  28.4 1.3 %layer_norm.4.outer.sibling.block = bf16[512,1536]{1,0:T(8,128)(2,1)S(1)} custom-call(f32[7,1536]{1,0:T(8,128)S(1)} %reshape.3.packed, bf16[512,1536]{1,0:T(8,128)(2,1)S(1)} %bitcast.4), custom_call_target="tpu_custom_call" | custom-call | tf_op jit(solution)/shard_map/layer_norm/pallas_call | solution.py:93
  29.7 0.0 collective-permute-done.8.refs_0_
  29.7 1.6 %collective-permute-start.7 = (bf16[192,768]{1,0:T(8,128)(2,1)S(1)}, bf16[192,768]{1,0:T(8,128)(2,1)S(1)}, u32[]{:S(2)}, u32[]{:S(2)}) collective-permute-start(bf16[192,768]{1,0:T(8,128)(2,1)S(1)} %collective-permute-done.refs_3_), channel_id=1, source_target_pairs={{0,4},{4,0},{8,12},{12,8},{16,20},{20,16},{24,28},{28,24},{1,5},{5... | collective-permute-start | bytes 884744 | tf_op jit(solution)/shard_map/ppermute | solution.py:290
  31.3 2.7 %layer_norm.3.outer.block.sibling = bf16[512,1536]{1,0:T(8,128)(2,1)S(1)} custom-call(f32[7,1536]{1,0:T(8,128)S(1)} %reshape.3.packed, bf16[512,1536]{1,0:T(8,128)(2,1)} %collective-permute-done.8.refs_0_), custom_call_target="tpu_custom_call" | custom-call | tf_op jit(solution)/shard_map/layer_norm/pallas_call | solution.py:93
  34.0 5.1 %collective-permute-done.3.refs_0_ = bf16[192,768]{1,0:T(8,128)(2,1)S(1)} collective-permute-done((bf16[192,768]{1,0:T(8,128)(2,1)}, bf16[192,768]{1,0:T(8,128)(2,1)S(1)}, u32[]{:S(2)}, u32[]{:S(2)}) %collective-permute-start.3) | collective-permute-done | bytes 294944 | tf_op jit(solution)/shard_map/ppermute | solution.py:290
  39.1 3.5 %collective-permute-done.4.refs_2_ = bf16[192,768]{1,0:T(8,128)(2,1)S(1)} collective-permute-done((bf16[192,768]{1,0:T(8,128)(2,1)}, bf16[192,768]{1,0:T(8,128)(2,1)S(1)}, u32[]{:S(2)}, u32[]{:S(2)}) %collective-permute-start.4) | collective-permute-done | bytes 294944 | tf_op jit(solution)/shard_map/ppermute | solution.py:290
  42.7 2.7 %layer_norm.5.block.sibling.outer = bf16[512,1536]{1,0:T(8,128)(2,1)S(1)} custom-call(f32[7,1536]{1,0:T(8,128)S(1)} %reshape.3.packed, bf16[512,1536]{1,0:T(8,128)(2,1)} %collective-permute-done.5.refs_0_), custom_call_target="tpu_custom_call" | custom-call | tf_op jit(solution)/shard_map/layer_norm/pallas_call | solution.py:93
  45.4 0.1 collective-permute-start.13
  45.4 0.6 collective-permute-start.9
  46.0 3.0 %collective-permute-start.11 = (bf16[192,768]{1,0:T(8,128)(2,1)S(1)}, bf16[192,768]{1,0:T(8,128)(2,1)S(1)}, u32[]{:S(2)}, u32[]{:S(2)}) collective-permute-start(bf16[192,768]{1,0:T(8,128)(2,1)S(1)} %copy-done.10), channel_id=1, source_target_pairs={{0,24},{4,28},{8,16},{12,20},{16,8},{20,12},{24,0},{28,4},{1,25},{... | collective-permute-start | bytes 884744 | tf_op jit(solution)/shard_map/ppermute | solution.py:290
  49.0 0.8 collective-permute-start.10
  49.8 0.4 collective-permute-start.12
  50.2 5.1 %collective-permute-done.9.refs_6_ = bf16[192,768]{1,0:T(8,128)(2,1)S(1)} collective-permute-done((bf16[192,768]{1,0:T(8,128)(2,1)S(1)}, bf16[192,768]{1,0:T(8,128)(2,1)S(1)}, u32[]{:S(2)}, u32[]{:S(2)}) %collective-permute-start.9) | collective-permute-done | bytes 294944 | tf_op jit(solution)/shard_map/ppermute | solution.py:290
  55.3 0.1 gather_shards.2.refs_0_
  55.4 0.0 copy-start.2
  55.4 0.1 collective-permute-start.19
  55.5 0.7 gather_shards.3.weight
  56.3 0.0 collective-permute-done.13.block.outer
  56.3 0.0 copy-done.2
  56.3 3.3 %expand_and_depthwise.4 = (bf16[256,384]{1,0:T(8,128)(2,1)S(1)}, bf16[256,384]{1,0:T(8,128)(2,1)S(1)}) custom-call(f32[7,1536]{1,0:T(8,128)S(1)} %reshape.3.packed, bf16[31,1536]{1,0:T(8,128)(2,1)S(1)} %copy-done.2, bf16[1536,768]{1,0:T(8,128)(2,1)S(1)} %gather_shards.3.weight, bf16[512,1536]{1,0:T(8,128)(2,1)S(1)} %layer_norm.5.block.sibling.outer, ...), custom_call_target="tpu_custom_call" | custom-call | tf_op jit(solution)/shard_map/expand_and_depthwise/pallas_call | solution.py:200
  59.7 0.6 collective-permute-start.16
  60.3 0.0 collective-permute-done.11.refs_2_
  60.3 0.8 collective-permute-start.14
  61.1 3.3 %collective-permute-start.15 = (bf16[192,768]{1,0:T(8,128)(2,1)S(1)}, bf16[192,768]{1,0:T(8,128)(2,1)S(1)}, u32[]{:S(2)}, u32[]{:S(2)}) collective-permute-start(bf16[192,768]{1,0:T(8,128)(2,1)S(1)} %copy-done.10), channel_id=1, source_target_pairs={{0,16},{4,20},{8,24},{12,28},{16,0},{20,4},{24,8},{28,12},{1,17},{... | collective-permute-start | bytes 884744 | tf_op jit(solution)/shard_map/ppermute | solution.py:290
  64.4 0.0 collective-permute-done.10.refs_1_
  64.4 0.9 %collective-permute-start.17 = (bf16[256,384]{1,0:T(8,128)(2,1)S(1)}, bf16[256,384]{1,0:T(8,128)(2,1)S(1)}, u32[]{:S(2)}, u32[]{:S(2)}) collective-permute-start(bf16[256,384]{1,0:T(8,128)(2,1)S(1)} %get-tuple-element.55), channel_id=1, source_target_pairs={{0,2},{1,3},{2,0},{3,1},{4,6},{5,7},{6,4},{7,5},{8,10},{9,11},{10,... | collective-permute-start | bytes 589832 | tf_op jit(solution)/shard_map/ppermute | solution.py:290
  65.4 3.4 %expand_and_depthwise.5 = bf16[512,384]{1,0:T(8,128)(2,1)S(1)} custom-call(f32[7,1536]{1,0:T(8,128)S(1)} %reshape.3.packed, bf16[31,1536]{1,0:T(8,128)(2,1)S(1)} %copy-done.2, bf16[1536,768]{1,0:T(8,128)(2,1)S(1)} %gather_shards.3.weight, bf16[512,1536]{1,0:T(8,128)(2,1)S(1)} %collective-permute-done.13.block.outer, ...), custom_call_target="tpu_custom_call" | custom-call | tf_op jit(solution)/shard_map/expand_and_depthwise/pallas_call | solution.py:200
  68.8 0.0 collective-permute-done.16.refs_15_
  68.8 0.1 collective-permute-start.20
  68.9 3.4 %expand_and_depthwise.6 = bf16[512,384]{1,0:T(8,128)(2,1)S(1)} custom-call(f32[7,1536]{1,0:T(8,128)S(1)} %reshape.3.packed, bf16[31,1536]{1,0:T(8,128)(2,1)S(1)} %copy-done.2, bf16[1536,768]{1,0:T(8,128)(2,1)S(1)} %gather_shards.3.weight, bf16[512,1536]{1,0:T(8,128)(2,1)S(1)} %layer_norm.3.outer.block.sibling, ...), custom_call_target="tpu_custom_call" | custom-call | tf_op jit(solution)/shard_map/expand_and_depthwise/pallas_call | solution.py:200
  72.3 0.0 copy-start.1
  72.3 0.0 collective-permute-done.17.refs_16_
  72.3 1.2 %collective-permute-start.26 = (bf16[512,384]{1,0:T(8,128)(2,1)S(1)}, bf16[512,384]{1,0:T(8,128)(2,1)S(1)}, u32[]{:S(2)}, u32[]{:S(2)}) collective-permute-start(bf16[512,384]{1,0:T(8,128)(2,1)S(1)} %expand_and_depthwise.6), channel_id=1, source_target_pairs={{0,1},{1,0},{2,3},{3,2},{4,5},{5,4},{6,7},{7,6},{8,9},{9,8},{10,11... | collective-permute-start | bytes 1179656 | tf_op jit(solution)/shard_map/ppermute | solution.py:290
  73.6 0.0 collective-permute-done.14.refs_3_
  73.6 3.6 %expand_and_depthwise.7.refs_12_ = bf16[512,384]{1,0:T(8,128)(2,1)S(1)} custom-call(f32[7,1536]{1,0:T(8,128)S(1)} %reshape.3.packed, bf16[31,1536]{1,0:T(8,128)(2,1)S(1)} %copy-done.2, bf16[1536,768]{1,0:T(8,128)(2,1)S(1)} %gather_shards.3.weight, bf16[512,1536]{1,0:T(8,128)(2,1)S(1)} %layer_norm.4.outer.sibling.block, ...), custom_call_target="tpu_custom_call" | custom-call | tf_op jit(solution)/shard_map/expand_and_depthwise/pallas_call | solution.py:200
  77.1 0.0 collective-permute-done.15.refs_4_
  77.2 1.2 %collective-permute-start.18 = (bf16[192,768]{1,0:T(8,128)(2,1)S(1)}, bf16[192,768]{1,0:T(8,128)(2,1)S(1)}, u32[]{:S(2)}, u32[]{:S(2)}) collective-permute-start(bf16[192,768]{1,0:T(8,128)(2,1)S(1)} %collective-permute-done.15.refs_4_), channel_id=1, source_target_pairs={{0,4},{4,0},{8,12},{12,8},{16,20},{20,16},{24,28},{28,24},{1,5},{5... | collective-permute-start | bytes 884744 | tf_op jit(solution)/shard_map/ppermute | solution.py:290
  78.3 1.6 %collective-permute-done.20.refs_14_ = bf16[512,384]{1,0:T(8,128)(2,1)S(1)} collective-permute-done((bf16[512,384]{1,0:T(8,128)(2,1)S(1)}, bf16[512,384]{1,0:T(8,128)(2,1)S(1)}, u32[]{:S(2)}, u32[]{:S(2)}) %collective-permute-start.20) | collective-permute-done | bytes 393248 | tf_op jit(solution)/shard_map/ppermute | solution.py:290
  79.9 0.0 collective-permute-start.21
  79.9 0.5 collective-permute-start.22
  80.4 0.0 collective-permute-start.23
  80.4 5.7 %collective-permute-done.18.refs_5_ = bf16[192,768]{1,0:T(8,128)(2,1)S(1)} collective-permute-done((bf16[192,768]{1,0:T(8,128)(2,1)S(1)}, bf16[192,768]{1,0:T(8,128)(2,1)S(1)}, u32[]{:S(2)}, u32[]{:S(2)}) %collective-permute-start.18) | collective-permute-done | bytes 294944 | tf_op jit(solution)/shard_map/ppermute | solution.py:290
  86.2 0.5 collective-permute-start.25
  86.7 0.0 collective-permute-done.23.refs_9_
  86.7 1.1 %collective-permute-done.24.refs_10_ = bf16[192,768]{1,0:T(8,128)(2,1)S(1)} collective-permute-done((bf16[192,768]{1,0:T(8,128)(2,1)S(1)}, bf16[192,768]{1,0:T(8,128)(2,1)S(1)}, u32[]{:S(2)}, u32[]{:S(2)}) %collective-permute-start.24) | collective-permute-done | bytes 294944 | tf_op jit(solution)/shard_map/ppermute | solution.py:290
  87.7 0.4 collective-permute-done.25.refs_11_
  88.2 5.1 %project_and_residual.1 = bf16[512,1536]{1,0:T(8,128)(2,1)} custom-call(f32[7,1536]{1,0:T(8,128)S(1)} %reshape.3.packed, bf16[512,1536]{1,0:T(8,128)(2,1)S(1)} %bitcast.5, bf16[192,1536]{1,0:T(8,128)(2,1)S(1)} %copy-done.1, bf16[384,768]{1,0:T(8,128)(2,1)S(1)} %gather_shards.2.refs_0_, bf16[192,768]{1,0:T(8,128)(2,1)S(1)} %collective-permute-done.10.refs_1_, ...), custom_call_target="tpu_custom_call" | custom-call | tf_op jit(solution)/shard_map/project_and_residual/pallas_call | solution.py:270
  (33 shorter events, 0.1 us)
Async XLA Ops:
  0.0 3.0 %copy-start = (bf16[1,512,1536]{2,1,0:T(8,128)(2,1)S(1)}, bf16[1,512,1536]{2,1,0:T(8,128)(2,1)}, u32[]{:S(2)}) copy-start(bf16[1,512,1536]{2,1,0:T(8,128)(2,1)} %param.10) | copy-start | bytes 4718596
  0.0 24.5 %copy-start.5 = (bf16[1536]{0:T(1024)(128)(2,1)S(1)}, bf16[1536]{0:T(1024)(128)(2,1)}, u32[]{:S(2)}) copy-start(bf16[1536]{0:T(1024)(128)(2,1)} %param.11) | copy-start | bytes 9220
  0.0 24.7 %copy-start.6 = (bf16[1536]{0:T(1024)(128)(2,1)S(1)}, bf16[1536]{0:T(1024)(128)(2,1)}, u32[]{:S(2)}) copy-start(bf16[1536]{0:T(1024)(128)(2,1)} %param.12) | copy-start | bytes 9220
  0.0 25.0 %copy-start.4 = (bf16[3072]{0:T(1024)(128)(2,1)S(1)}, bf16[3072]{0:T(1024)(128)(2,1)}, u32[]{:S(2)}) copy-start(bf16[3072]{0:T(1024)(128)(2,1)} %param.14) | copy-start | bytes 18436
  0.0 25.0 %copy-start.7 = (bf16[1536]{0:T(1024)(128)(2,1)S(1)}, bf16[1536]{0:T(1024)(128)(2,1)}, u32[]{:S(2)}) copy-start(bf16[1536]{0:T(1024)(128)(2,1)} %param.16) | copy-start | bytes 9220
  0.0 25.3 %copy-start.8 = (bf16[1536]{0:T(1024)(128)(2,1)S(1)}, bf16[1536]{0:T(1024)(128)(2,1)}, u32[]{:S(2)}) copy-start(bf16[1536]{0:T(1024)(128)(2,1)} %param.17) | copy-start | bytes 9220
  0.0 25.5 %copy-start.9 = (bf16[1536]{0:T(1024)(128)(2,1)S(1)}, bf16[1536]{0:T(1024)(128)(2,1)}, u32[]{:S(2)}) copy-start(bf16[1536]{0:T(1024)(128)(2,1)} %param.19) | copy-start | bytes 9220
  0.0 29.7 %collective-permute-start.8 = (bf16[512,1536]{1,0:T(8,128)(2,1)}, bf16[512,1536]{1,0:T(8,128)(2,1)}, u32[]{:S(2)}, u32[]{:S(2)}) collective-permute-start(bf16[512,1536]{1,0:T(8,128)(2,1)} %bitcast.2), channel_id=1, source_target_pairs={{0,1},{1,0},{2,3},{3,2},{4,5},{5,4},{6,7},{7,6},{8,9},{9,8},{10,11... | collective-permute-start | bytes 4718600 | tf_op jit(solution)/shard_map/ppermute | solution.py:290
  3.0 39.6 %collective-permute-start.5 = (bf16[512,1536]{1,0:T(8,128)(2,1)S(1)}, bf16[512,1536]{1,0:T(8,128)(2,1)}, u32[]{:S(2)}, u32[]{:S(2)}) collective-permute-start(bf16[512,1536]{1,0:T(8,128)(2,1)S(1)} %bitcast.3), channel_id=1, source_target_pairs={{0,2},{1,3},{2,0},{3,1},{4,6},{5,7},{6,4},{7,5},{8,10},{9,11},{10,... | collective-permute-start | bytes 4718600 | tf_op jit(solution)/shard_map/ppermute | solution.py:290
  5.7 18.8 %collective-permute-start.2 = (bf16[192,1536]{1,0:T(8,128)(2,1)}, bf16[192,1536]{1,0:T(8,128)(2,1)S(1)}, u32[]{:S(2)}, u32[]{:S(2)}) collective-permute-start(bf16[192,1536]{1,0:T(8,128)(2,1)} %get-tuple-element.35), channel_id=1, source_target_pairs={{0,4},{4,0},{8,12},{12,8},{16,20},{20,16},{24,28},{28,24},{1,5},{5... | collective-permute-start | bytes 1769480 | tf_op jit(solution)/shard_map/ppermute | solution.py:290
  7.2 11.9 %collective-permute-start = (bf16[192,768]{1,0:T(8,128)(2,1)}, bf16[192,768]{1,0:T(8,128)(2,1)S(1)}, u32[]{:S(2)}, u32[]{:S(2)}) collective-permute-start(bf16[192,768]{1,0:T(8,128)(2,1)} %get-tuple-element.39.refs_0_), channel_id=1, source_target_pairs={{0,24},{4,28},{8,16},{12,20},{16,8},{20,12},{24,0},{28,4},{1,25},{... | collective-permute-start | bytes 884744 | tf_op jit(solution)/shard_map/ppermute | solution.py:290
  10.8 13.7 %collective-permute-start.1 = (bf16[192,768]{1,0:T(8,128)(2,1)}, bf16[192,768]{1,0:T(8,128)(2,1)S(1)}, u32[]{:S(2)}, u32[]{:S(2)}) collective-permute-start(bf16[192,768]{1,0:T(8,128)(2,1)} %get-tuple-element.39.refs_0_), channel_id=1, source_target_pairs={{0,8},{4,12},{8,0},{12,4},{16,24},{20,28},{24,16},{28,20},{1,9},{5... | collective-permute-start | bytes 884744 | tf_op jit(solution)/shard_map/ppermute | solution.py:290
  25.6 13.5 %collective-permute-start.3 = (bf16[192,768]{1,0:T(8,128)(2,1)}, bf16[192,768]{1,0:T(8,128)(2,1)S(1)}, u32[]{:S(2)}, u32[]{:S(2)}) collective-permute-start(bf16[192,768]{1,0:T(8,128)(2,1)} %get-tuple-element.52), channel_id=1, source_target_pairs={{0,8},{4,12},{8,0},{12,4},{16,24},{20,28},{24,16},{28,20},{1,9},{5... | collective-permute-start | bytes 884744 | tf_op jit(solution)/shard_map/ppermute | solution.py:290
  27.4 15.3 %collective-permute-start.4 = (bf16[192,768]{1,0:T(8,128)(2,1)}, bf16[192,768]{1,0:T(8,128)(2,1)S(1)}, u32[]{:S(2)}, u32[]{:S(2)}) collective-permute-start(bf16[192,768]{1,0:T(8,128)(2,1)} %get-tuple-element.39.refs_0_), channel_id=1, source_target_pairs={{0,16},{4,20},{8,24},{12,28},{16,0},{20,4},{24,8},{28,12},{1,17},{... | collective-permute-start | bytes 884744 | tf_op jit(solution)/shard_map/ppermute | solution.py:290
  27.9 14.7 %collective-permute-start.6 = (bf16[192,768]{1,0:T(8,128)(2,1)S(1)}, bf16[192,768]{1,0:T(8,128)(2,1)S(1)}, u32[]{:S(2)}, u32[]{:S(2)}) collective-permute-start(bf16[192,768]{1,0:T(8,128)(2,1)S(1)} %collective-permute-done.1.refs_1_), channel_id=1, source_target_pairs={{0,4},{4,0},{8,12},{12,8},{16,20},{20,16},{24,28},{28,24},{1,5},{5... | collective-permute-start | bytes 884744 | tf_op jit(solution)/shard_map/ppermute | solution.py:290
  29.7 12.9 %collective-permute-start.7 = (bf16[192,768]{1,0:T(8,128)(2,1)S(1)}, bf16[192,768]{1,0:T(8,128)(2,1)S(1)}, u32[]{:S(2)}, u32[]{:S(2)}) collective-permute-start(bf16[192,768]{1,0:T(8,128)(2,1)S(1)} %collective-permute-done.refs_3_), channel_id=1, source_target_pairs={{0,4},{4,0},{8,12},{12,8},{16,20},{20,16},{24,28},{28,24},{1,5},{5... | collective-permute-start | bytes 884744 | tf_op jit(solution)/shard_map/ppermute | solution.py:290
  34.0 12.0 %copy-start.10 = (bf16[192,768]{1,0:T(8,128)(2,1)S(1)}, bf16[192,768]{1,0:T(8,128)(2,1)}, u32[]{:S(2)}) copy-start(bf16[192,768]{1,0:T(8,128)(2,1)} %get-tuple-element.52) | copy-start | bytes 884740
  34.0 21.5 %copy-start.3 = (bf16[192,768]{1,0:T(8,128)(2,1)S(1)}, bf16[192,768]{1,0:T(8,128)(2,1)}, u32[]{:S(2)}) copy-start(bf16[192,768]{1,0:T(8,128)(2,1)} %get-tuple-element.39.refs_0_) | copy-start | bytes 884740
  45.4 10.9 %collective-permute-start.13 = (bf16[512,1536]{1,0:T(8,128)(2,1)S(1)}, bf16[512,1536]{1,0:T(8,128)(2,1)S(1)}, u32[]{:S(2)}, u32[]{:S(2)}) collective-permute-start(bf16[512,1536]{1,0:T(8,128)(2,1)S(1)} %layer_norm.5.block.sibling.outer), channel_id=1, source_target_pairs={{0,1},{1,0},{2,3},{3,2},{4,5},{5,4},{6,7},{7,6},{8,9},{9,8},{10,11... | collective-permute-start | bytes 4718600 | tf_op jit(solution)/shard_map/ppermute | solution.py:290
  45.4 9.9 %collective-permute-start.9 = (bf16[192,768]{1,0:T(8,128)(2,1)S(1)}, bf16[192,768]{1,0:T(8,128)(2,1)S(1)}, u32[]{:S(2)}, u32[]{:S(2)}) collective-permute-start(bf16[192,768]{1,0:T(8,128)(2,1)S(1)} %collective-permute-done.4.refs_2_), channel_id=1, source_target_pairs={{0,4},{4,0},{8,12},{12,8},{16,20},{20,16},{24,28},{28,24},{1,5},{5... | collective-permute-start | bytes 884744 | tf_op jit(solution)/shard_map/ppermute | solution.py:290
  46.0 14.2 %collective-permute-start.11 = (bf16[192,768]{1,0:T(8,128)(2,1)S(1)}, bf16[192,768]{1,0:T(8,128)(2,1)S(1)}, u32[]{:S(2)}, u32[]{:S(2)}) collective-permute-start(bf16[192,768]{1,0:T(8,128)(2,1)S(1)} %copy-done.10), channel_id=1, source_target_pairs={{0,24},{4,28},{8,16},{12,20},{16,8},{20,12},{24,0},{28,4},{1,25},{... | collective-permute-start | bytes 884744 | tf_op jit(solution)/shard_map/ppermute | solution.py:290
  49.0 15.4 %collective-permute-start.10 = (bf16[192,768]{1,0:T(8,128)(2,1)S(1)}, bf16[192,768]{1,0:T(8,128)(2,1)S(1)}, u32[]{:S(2)}, u32[]{:S(2)}) collective-permute-start(bf16[192,768]{1,0:T(8,128)(2,1)S(1)} %collective-permute-done.3.refs_0_), channel_id=1, source_target_pairs={{0,4},{4,0},{8,12},{12,8},{16,20},{20,16},{24,28},{28,24},{1,5},{5... | collective-permute-start | bytes 884744 | tf_op jit(solution)/shard_map/ppermute | solution.py:290
  49.8 6.5 %collective-permute-start.12 = (bf16[32,1536]{1,0:T(8,128)(2,1)S(1)}, bf16[32,1536]{1,0:T(8,128)(2,1)S(1)}, u32[]{:S(2)}, u32[]{:S(2)}) collective-permute-start(bf16[32,1536]{1,0:T(8,128)(2,1)S(1)} %pad_maximum_fusion), channel_id=1, source_target_pairs={{0,3},{1,2},{2,1},{3,0},{4,7},{5,6},{6,5},{7,4},{8,11},{9,10},{10,... | collective-permute-start | bytes 294920 | tf_op jit(solution)/shard_map/ppermute | solution.py:290
  55.4 0.9 copy-start.2
  55.4 22.9 %collective-permute-start.19 = (bf16[384,768]{1,0:T(8,128)(2,1)S(1)}, bf16[384,768]{1,0:T(8,128)(2,1)S(1)}, u32[]{:S(2)}, u32[]{:S(2)}) collective-permute-start(bf16[384,768]{1,0:T(8,128)(2,1)S(1)} %gather_shards.2.refs_0_), channel_id=1, source_target_pairs={{0,1},{1,0},{2,3},{3,2},{4,5},{5,4},{6,7},{7,6},{8,9},{9,8},{10,11... | collective-permute-start | bytes 1769480 | tf_op jit(solution)/shard_map/ppermute | solution.py:290
  59.7 9.1 %collective-permute-start.16 = (bf16[256,384]{1,0:T(8,128)(2,1)S(1)}, bf16[256,384]{1,0:T(8,128)(2,1)S(1)}, u32[]{:S(2)}, u32[]{:S(2)}) collective-permute-start(bf16[256,384]{1,0:T(8,128)(2,1)S(1)} %get-tuple-element.50), channel_id=1, source_target_pairs={{0,2},{1,3},{2,0},{3,1},{4,6},{5,7},{6,4},{7,5},{8,10},{9,11},{10,... | collective-permute-start | bytes 589832 | tf_op jit(solution)/shard_map/ppermute | solution.py:290
  60.3 13.3 %collective-permute-start.14 = (bf16[192,768]{1,0:T(8,128)(2,1)S(1)}, bf16[192,768]{1,0:T(8,128)(2,1)S(1)}, u32[]{:S(2)}, u32[]{:S(2)}) collective-permute-start(bf16[192,768]{1,0:T(8,128)(2,1)S(1)} %collective-permute-done.11.refs_2_), channel_id=1, source_target_pairs={{0,4},{4,0},{8,12},{12,8},{16,20},{20,16},{24,28},{28,24},{1,5},{5... | collective-permute-start | bytes 884744 | tf_op jit(solution)/shard_map/ppermute | solution.py:290
  61.1 16.1 %collective-permute-start.15 = (bf16[192,768]{1,0:T(8,128)(2,1)S(1)}, bf16[192,768]{1,0:T(8,128)(2,1)S(1)}, u32[]{:S(2)}, u32[]{:S(2)}) collective-permute-start(bf16[192,768]{1,0:T(8,128)(2,1)S(1)} %copy-done.10), channel_id=1, source_target_pairs={{0,16},{4,20},{8,24},{12,28},{16,0},{20,4},{24,8},{28,12},{1,17},{... | collective-permute-start | bytes 884744 | tf_op jit(solution)/shard_map/ppermute | solution.py:290
  64.4 7.9 %collective-permute-start.17 = (bf16[256,384]{1,0:T(8,128)(2,1)S(1)}, bf16[256,384]{1,0:T(8,128)(2,1)S(1)}, u32[]{:S(2)}, u32[]{:S(2)}) collective-permute-start(bf16[256,384]{1,0:T(8,128)(2,1)S(1)} %get-tuple-element.55), channel_id=1, source_target_pairs={{0,2},{1,3},{2,0},{3,1},{4,6},{5,7},{6,4},{7,5},{8,10},{9,11},{10,... | collective-permute-start | bytes 589832 | tf_op jit(solution)/shard_map/ppermute | solution.py:290
  68.8 11.1 %collective-permute-start.20 = (bf16[512,384]{1,0:T(8,128)(2,1)S(1)}, bf16[512,384]{1,0:T(8,128)(2,1)S(1)}, u32[]{:S(2)}, u32[]{:S(2)}) collective-permute-start(bf16[512,384]{1,0:T(8,128)(2,1)S(1)} %expand_and_depthwise.5), channel_id=1, source_target_pairs={{0,3},{1,2},{2,1},{3,0},{4,7},{5,6},{6,5},{7,4},{8,11},{9,10},{10,... | collective-permute-start | bytes 1179656 | tf_op jit(solution)/shard_map/ppermute | solution.py:290
  72.3 15.8 %copy-start.1 = (bf16[192,1536]{1,0:T(8,128)(2,1)S(1)}, bf16[192,1536]{1,0:T(8,128)(2,1)}, u32[]{:S(2)}) copy-start(bf16[192,1536]{1,0:T(8,128)(2,1)} %whole.1) | copy-start | bytes 1769476
  72.3 13.8 %collective-permute-start.26 = (bf16[512,384]{1,0:T(8,128)(2,1)S(1)}, bf16[512,384]{1,0:T(8,128)(2,1)S(1)}, u32[]{:S(2)}, u32[]{:S(2)}) collective-permute-start(bf16[512,384]{1,0:T(8,128)(2,1)S(1)} %expand_and_depthwise.6), channel_id=1, source_target_pairs={{0,1},{1,0},{2,3},{3,2},{4,5},{5,4},{6,7},{7,6},{8,9},{9,8},{10,11... | collective-permute-start | bytes 1179656 | tf_op jit(solution)/shard_map/ppermute | solution.py:290
  77.2 9.0 %collective-permute-start.18 = (bf16[192,768]{1,0:T(8,128)(2,1)S(1)}, bf16[192,768]{1,0:T(8,128)(2,1)S(1)}, u32[]{:S(2)}, u32[]{:S(2)}) collective-permute-start(bf16[192,768]{1,0:T(8,128)(2,1)S(1)} %collective-permute-done.15.refs_4_), channel_id=1, source_target_pairs={{0,4},{4,0},{8,12},{12,8},{16,20},{20,16},{24,28},{28,24},{1,5},{5... | collective-permute-start | bytes 884744 | tf_op jit(solution)/shard_map/ppermute | solution.py:290
  79.9 6.7 %collective-permute-start.21 = (bf16[192,768]{1,0:T(8,128)(2,1)S(1)}, bf16[192,768]{1,0:T(8,128)(2,1)S(1)}, u32[]{:S(2)}, u32[]{:S(2)}) collective-permute-start(bf16[192,768]{1,0:T(8,128)(2,1)S(1)} %collective-permute-done.10.refs_1_), channel_id=1, source_target_pairs={{0,1},{1,0},{2,3},{3,2},{4,5},{5,4},{6,7},{7,6},{8,9},{9,8},{10,11... | collective-permute-start | bytes 884744 | tf_op jit(solution)/shard_map/ppermute | solution.py:290
  79.9 6.7 %collective-permute-start.22 = (bf16[192,768]{1,0:T(8,128)(2,1)S(1)}, bf16[192,768]{1,0:T(8,128)(2,1)S(1)}, u32[]{:S(2)}, u32[]{:S(2)}) collective-permute-start(bf16[192,768]{1,0:T(8,128)(2,1)S(1)} %collective-permute-done.11.refs_2_), channel_id=1, source_target_pairs={{0,1},{1,0},{2,3},{3,2},{4,5},{5,4},{6,7},{7,6},{8,9},{9,8},{10,11... | collective-permute-start | bytes 884744 | tf_op jit(solution)/shard_map/ppermute | solution.py:290
  80.4 6.2 %collective-permute-start.23 = (bf16[192,768]{1,0:T(8,128)(2,1)S(1)}, bf16[192,768]{1,0:T(8,128)(2,1)S(1)}, u32[]{:S(2)}, u32[]{:S(2)}) collective-permute-start(bf16[192,768]{1,0:T(8,128)(2,1)S(1)} %collective-permute-done.14.refs_3_), channel_id=1, source_target_pairs={{0,1},{1,0},{2,3},{3,2},{4,5},{5,4},{6,7},{7,6},{8,9},{9,8},{10,11... | collective-permute-start | bytes 884744 | tf_op jit(solution)/shard_map/ppermute | solution.py:290
  86.1 1.6 %collective-permute-start.24 = (bf16[192,768]{1,0:T(8,128)(2,1)S(1)}, bf16[192,768]{1,0:T(8,128)(2,1)S(1)}, u32[]{:S(2)}, u32[]{:S(2)}) collective-permute-start(bf16[192,768]{1,0:T(8,128)(2,1)S(1)} %collective-permute-done.15.refs_4_), channel_id=1, source_target_pairs={{0,1},{1,0},{2,3},{3,2},{4,5},{5,4},{6,7},{7,6},{8,9},{9,8},{10,11... | collective-permute-start | bytes 884744 | tf_op jit(solution)/shard_map/ppermute | solution.py:290
  86.2 2.0 %collective-permute-start.25 = (bf16[192,768]{1,0:T(8,128)(2,1)S(1)}, bf16[192,768]{1,0:T(8,128)(2,1)S(1)}, u32[]{:S(2)}, u32[]{:S(2)}) collective-permute-start(bf16[192,768]{1,0:T(8,128)(2,1)S(1)} %collective-permute-done.18.refs_5_), channel_id=1, source_target_pairs={{0,1},{1,0},{2,3},{3,2},{4,5},{5,4},{6,7},{7,6},{8,9},{9,8},{10,11... | collective-permute-start | bytes 884744 | tf_op jit(solution)/shard_map/ppermute | solution.py:290

commit v4 on v3

--- a/solution.py
+++ b/solution.py
@@ -305,7 +305,7 @@
     facing = across(after(own, e_own), "seq", 2)
     e_far, e_near = across(e_own, "dp", 6), across(e_own, "dp", 2)
     y_own = across(both, "dp", 1)
-    done = (e_far, e_near, y_own)
+    done = (e_far,  y_own)
 
     e_middle = across(after(e_own, *done), "dp", 4)
     p_near = across(after(p_own, *done), "dp", 2)

time: 93.6 us -> 93.1 us (level)
  waiting for transfers between devices: 36.2 us -> 30.7 us
  starting transfers between devices: 26.7 us -> 31.8 us
    ppermute x27, waiting for transfers between devices: 36.2 us -> 30.7 us  [across(): return lax.ppermute(array, axis, [(i, i ^ bits) for i in range(count)])]
    ppermute x27, starting transfers between devices: 26.7 us -> 31.8 us  [across(): return lax.ppermute(array, axis, [(i, i ^ bits) for i in range(count)])]
  transfers between devices with their start and end apart: 27 -> 27, of which waited for: 9 -> 11; matrix products, arithmetic and copies ran while one was open for 1% -> 1% of each run, Pallas kernels for 22% -> 23%
where the time goes in v4:
time: 93.1 us; the launch traced here: 92.9 us
  starting transfers between devices  31.8 us (34%)
  waiting for transfers between devices  30.7 us (33%)
  Pallas kernels  28.8 us (31%)
  local copies, waits for them, and re-layouts  1.15 us (1%)
    ppermute x27, starting transfers between devices, across(): return lax.ppermute(array, axis, [(i, i ^ bits) for i in range(count)])  31.8 us
    ppermute x27, waiting for transfers between devices, across(): return lax.ppermute(array, axis, [(i, i ^ bits) for i in range(count)])  30.7 us
    pallas_call x4, Pallas kernels, conv(): pl.pallas_call(functools.partial(conv_body, across_x, across_core), in_sp...  13.7 us
    pallas_call x3, Pallas kernels, norm(): pl.pallas_call(norm_body, in_specs=[VMEM] * (1 + len(pieces)), out_specs=...  6.68 us
    pallas_call x1, Pallas kernels, project(): pl.pallas_call(functools.partial(project_body, places, spots), in_specs=[...  5.08 us
    pallas_call x1, Pallas kernels, cut(): pl.pallas_call(cut_body, in_specs=[ANY] * 2, out_specs=[VMEM] * len(shape...  2.43 us
  transfers between devices with their start and end apart: 27, of which 11 were waited for; matrix products, arithmetic and copies ran while one was open for 1% of the time, Pallas kernels for 23%

profile of v4, /device:TPU:0, one launch (start us, length us, event | category | flops | bytes accessed | tf_op | source)
XLA Modules:
  0.0 92.9 jit_solution(7228505015428522897)
XLA Ops:
  0.0 0.5 collective-permute-start.8
  0.6 2.4 %cut_weights.1 = (bf16[192,768]{1,0:T(8,128)(2,1)}, bf16[192,768]{1,0:T(8,128)(2,1)}, bf16[192,1536]{1,0:T(8,128)(2,1)}) custom-call(bf16[192,3072]{1,0:T(8,128)(2,1)} %expand.1, bf16[192,1536]{1,0:T(8,128)(2,1)} %whole.1), custom_call_target="tpu_custom_call" | custom-call | tf_op jit(solution)/shard_map/cut_weights/pallas_call | solution.py:57
  3.0 2.6 %collective-permute-start.4 = (bf16[512,1536]{1,0:T(8,128)(2,1)S(1)}, bf16[512,1536]{1,0:T(8,128)(2,1)}, u32[]{:S(2)}, u32[]{:S(2)}) collective-permute-start(bf16[512,1536]{1,0:T(8,128)(2,1)S(1)} %bitcast.3), channel_id=1, source_target_pairs={{0,2},{1,3},{2,0},{3,1},{4,6},{5,7},{6,4},{7,5},{8,10},{9,11},{10,... | collective-permute-start | bytes 4718600 | tf_op jit(solution)/shard_map/ppermute | solution.py:290
  5.7 1.5 %collective-permute-start.1 = (bf16[192,1536]{1,0:T(8,128)(2,1)}, bf16[192,1536]{1,0:T(8,128)(2,1)S(1)}, u32[]{:S(2)}, u32[]{:S(2)}) collective-permute-start(bf16[192,1536]{1,0:T(8,128)(2,1)} %get-tuple-element.35), channel_id=1, source_target_pairs={{0,4},{4,0},{8,12},{12,8},{16,20},{20,16},{24,28},{28,24},{1,5},{5... | collective-permute-start | bytes 1769480 | tf_op jit(solution)/shard_map/ppermute | solution.py:290
  7.2 3.6 %collective-permute-start = (bf16[192,768]{1,0:T(8,128)(2,1)}, bf16[192,768]{1,0:T(8,128)(2,1)S(1)}, u32[]{:S(2)}, u32[]{:S(2)}) collective-permute-start(bf16[192,768]{1,0:T(8,128)(2,1)} %get-tuple-element.39.refs_0_), channel_id=1, source_target_pairs={{0,24},{4,28},{8,16},{12,20},{16,8},{20,12},{24,0},{28,4},{1,25},{... | collective-permute-start | bytes 884744 | tf_op jit(solution)/shard_map/ppermute | solution.py:290
  10.8 8.3 %collective-permute-done.refs_3_ = bf16[192,768]{1,0:T(8,128)(2,1)S(1)} collective-permute-done((bf16[192,768]{1,0:T(8,128)(2,1)}, bf16[192,768]{1,0:T(8,128)(2,1)S(1)}, u32[]{:S(2)}, u32[]{:S(2)}) %collective-permute-start) | collective-permute-done | bytes 294944 | tf_op jit(solution)/shard_map/ppermute | solution.py:290
  19.1 2.1 %collective-permute-done.1.refs_1_.refs_4_ = bf16[192,1536]{1,0:T(8,128)(2,1)S(1)} collective-permute-done((bf16[192,1536]{1,0:T(8,128)(2,1)}, bf16[192,1536]{1,0:T(8,128)(2,1)S(1)}, u32[]{:S(2)}, u32[]{:S(2)}) %collective-permute-start.1) | collective-permute-done | bytes 589856 | tf_op jit(solution)/shard_map/ppermute | solution.py:290
  21.2 0.2 dynamic-update-slice
  21.4 0.3 dynamic-update-slice.1
  21.7 0.3 dynamic-update-slice.3
  22.0 0.3 dynamic-update-slice.4
  22.3 0.1 reshape.3.packed
  22.4 2.9 %collective-permute-start.2 = (bf16[192,768]{1,0:T(8,128)(2,1)}, bf16[192,768]{1,0:T(8,128)(2,1)S(1)}, u32[]{:S(2)}, u32[]{:S(2)}) collective-permute-start(bf16[192,768]{1,0:T(8,128)(2,1)} %get-tuple-element.52), channel_id=1, source_target_pairs={{0,8},{4,12},{8,0},{12,4},{16,24},{20,28},{24,16},{28,20},{1,9},{5... | collective-permute-start | bytes 884744 | tf_op jit(solution)/shard_map/ppermute | solution.py:290
  25.3 1.3 %collective-permute-start.3 = (bf16[192,768]{1,0:T(8,128)(2,1)}, bf16[192,768]{1,0:T(8,128)(2,1)S(1)}, u32[]{:S(2)}, u32[]{:S(2)}) collective-permute-start(bf16[192,768]{1,0:T(8,128)(2,1)} %get-tuple-element.39.refs_0_), channel_id=1, source_target_pairs={{0,16},{4,20},{8,24},{12,28},{16,0},{20,4},{24,8},{28,12},{1,17},{... | collective-permute-start | bytes 884744 | tf_op jit(solution)/shard_map/ppermute | solution.py:290
  26.6 0.0 collective-permute-done.5.refs_1_
  26.6 1.5 %collective-permute-start.6 = (bf16[192,768]{1,0:T(8,128)(2,1)S(1)}, bf16[192,768]{1,0:T(8,128)(2,1)S(1)}, u32[]{:S(2)}, u32[]{:S(2)}) collective-permute-start(bf16[192,768]{1,0:T(8,128)(2,1)S(1)} %collective-permute-done.5.refs_1_), channel_id=1, source_target_pairs={{0,4},{4,0},{8,12},{12,8},{16,20},{20,16},{24,28},{28,24},{1,5},{5... | collective-permute-start | bytes 884744 | tf_op jit(solution)/shard_map/ppermute | solution.py:290
  28.1 1.3 %layer_norm.4.outer.sibling.block = bf16[512,1536]{1,0:T(8,128)(2,1)S(1)} custom-call(f32[7,1536]{1,0:T(8,128)S(1)} %reshape.3.packed, bf16[512,1536]{1,0:T(8,128)(2,1)S(1)} %bitcast.4), custom_call_target="tpu_custom_call" | custom-call | tf_op jit(solution)/shard_map/layer_norm/pallas_call | solution.py:93
  29.4 0.6 collective-permute-start.7
  30.0 2.7 %layer_norm.3.outer.block.sibling = bf16[512,1536]{1,0:T(8,128)(2,1)S(1)} custom-call(f32[7,1536]{1,0:T(8,128)S(1)} %reshape.3.packed, bf16[512,1536]{1,0:T(8,128)(2,1)} %collective-permute-done.8.refs_0_), custom_call_target="tpu_custom_call" | custom-call | tf_op jit(solution)/shard_map/layer_norm/pallas_call | solution.py:93
  32.7 5.3 %collective-permute-done.2.refs_0_ = bf16[192,768]{1,0:T(8,128)(2,1)S(1)} collective-permute-done((bf16[192,768]{1,0:T(8,128)(2,1)}, bf16[192,768]{1,0:T(8,128)(2,1)S(1)}, u32[]{:S(2)}, u32[]{:S(2)}) %collective-permute-start.2) | collective-permute-done | bytes 294944 | tf_op jit(solution)/shard_map/ppermute | solution.py:290
  38.0 2.7 %collective-permute-done.3.refs_2_ = bf16[192,768]{1,0:T(8,128)(2,1)S(1)} collective-permute-done((bf16[192,768]{1,0:T(8,128)(2,1)}, bf16[192,768]{1,0:T(8,128)(2,1)S(1)}, u32[]{:S(2)}, u32[]{:S(2)}) %collective-permute-start.3) | collective-permute-done | bytes 294944 | tf_op jit(solution)/shard_map/ppermute | solution.py:290
  40.7 0.0 collective-permute-done.7.refs_7_
  40.7 0.0 collective-permute-done.4.refs_0_
  40.7 2.7 %layer_norm.5.block.sibling.outer = bf16[512,1536]{1,0:T(8,128)(2,1)S(1)} custom-call(f32[7,1536]{1,0:T(8,128)S(1)} %reshape.3.packed, bf16[512,1536]{1,0:T(8,128)(2,1)} %collective-permute-done.4.refs_0_), custom_call_target="tpu_custom_call" | custom-call | tf_op jit(solution)/shard_map/layer_norm/pallas_call | solution.py:93
  43.4 0.1 collective-permute-start.13
  43.5 1.9 %collective-permute-start.9 = (bf16[192,768]{1,0:T(8,128)(2,1)S(1)}, bf16[192,768]{1,0:T(8,128)(2,1)S(1)}, u32[]{:S(2)}, u32[]{:S(2)}) collective-permute-start(bf16[192,768]{1,0:T(8,128)(2,1)S(1)} %collective-permute-done.3.refs_2_), channel_id=1, source_target_pairs={{0,4},{4,0},{8,12},{12,8},{16,20},{20,16},{24,28},{28,24},{1,5},{5... | collective-permute-start | bytes 884744 | tf_op jit(solution)/shard_map/ppermute | solution.py:290
  45.4 3.6 %collective-permute-start.11 = (bf16[192,768]{1,0:T(8,128)(2,1)S(1)}, bf16[192,768]{1,0:T(8,128)(2,1)S(1)}, u32[]{:S(2)}, u32[]{:S(2)}) collective-permute-start(bf16[192,768]{1,0:T(8,128)(2,1)S(1)} %copy-done.10), channel_id=1, source_target_pairs={{0,24},{4,28},{8,16},{12,20},{16,8},{20,12},{24,0},{28,4},{1,25},{... | collective-permute-start | bytes 884744 | tf_op jit(solution)/shard_map/ppermute | solution.py:290
  49.0 0.5 collective-permute-start.10
  49.5 0.7 collective-permute-start.12
  50.2 3.2 %collective-permute-done.9.refs_6_ = bf16[192,768]{1,0:T(8,128)(2,1)S(1)} collective-permute-done((bf16[192,768]{1,0:T(8,128)(2,1)S(1)}, bf16[192,768]{1,0:T(8,128)(2,1)S(1)}, u32[]{:S(2)}, u32[]{:S(2)}) %collective-permute-start.9) | collective-permute-done | bytes 294944 | tf_op jit(solution)/shard_map/ppermute | solution.py:290
  53.4 0.1 gather_shards.2.refs_0_
  53.5 0.0 copy-start.2
  53.5 0.1 collective-permute-start.19
  53.6 0.7 gather_shards.3.weight
  54.3 0.2 collective-permute-done.12.sibling
  54.5 0.0 collective-permute-done.13.block.outer
  54.5 3.3 %expand_and_depthwise.4 = (bf16[256,384]{1,0:T(8,128)(2,1)S(1)}, bf16[256,384]{1,0:T(8,128)(2,1)S(1)}) custom-call(f32[7,1536]{1,0:T(8,128)S(1)} %reshape.3.packed, bf16[31,1536]{1,0:T(8,128)(2,1)S(1)} %copy-done.2, bf16[1536,768]{1,0:T(8,128)(2,1)S(1)} %gather_shards.3.weight, bf16[512,1536]{1,0:T(8,128)(2,1)S(1)} %layer_norm.5.block.sibling.outer, ...), custom_call_target="tpu_custom_call" | custom-call | tf_op jit(solution)/shard_map/expand_and_depthwise/pallas_call | solution.py:200
  57.9 1.7 %collective-permute-start.16 = (bf16[256,384]{1,0:T(8,128)(2,1)S(1)}, bf16[256,384]{1,0:T(8,128)(2,1)S(1)}, u32[]{:S(2)}, u32[]{:S(2)}) collective-permute-start(bf16[256,384]{1,0:T(8,128)(2,1)S(1)} %get-tuple-element.50), channel_id=1, source_target_pairs={{0,2},{1,3},{2,0},{3,1},{4,6},{5,7},{6,4},{7,5},{8,10},{9,11},{10,... | collective-permute-start | bytes 589832 | tf_op jit(solution)/shard_map/ppermute | solution.py:290
  59.6 0.0 collective-permute-done.11.refs_2_
  59.6 1.5 %collective-permute-start.14 = (bf16[192,768]{1,0:T(8,128)(2,1)S(1)}, bf16[192,768]{1,0:T(8,128)(2,1)S(1)}, u32[]{:S(2)}, u32[]{:S(2)}) collective-permute-start(bf16[192,768]{1,0:T(8,128)(2,1)S(1)} %collective-permute-done.11.refs_2_), channel_id=1, source_target_pairs={{0,4},{4,0},{8,12},{12,8},{16,20},{20,16},{24,28},{28,24},{1,5},{5... | collective-permute-start | bytes 884744 | tf_op jit(solution)/shard_map/ppermute | solution.py:290
  61.1 2.8 %collective-permute-start.15 = (bf16[192,768]{1,0:T(8,128)(2,1)S(1)}, bf16[192,768]{1,0:T(8,128)(2,1)S(1)}, u32[]{:S(2)}, u32[]{:S(2)}) collective-permute-start(bf16[192,768]{1,0:T(8,128)(2,1)S(1)} %copy-done.10), channel_id=1, source_target_pairs={{0,16},{4,20},{8,24},{12,28},{16,0},{20,4},{24,8},{28,12},{1,17},{... | collective-permute-start | bytes 884744 | tf_op jit(solution)/shard_map/ppermute | solution.py:290
  63.9 0.0 collective-permute-done.10.refs_1_
  63.9 1.5 %collective-permute-start.17 = (bf16[256,384]{1,0:T(8,128)(2,1)S(1)}, bf16[256,384]{1,0:T(8,128)(2,1)S(1)}, u32[]{:S(2)}, u32[]{:S(2)}) collective-permute-start(bf16[256,384]{1,0:T(8,128)(2,1)S(1)} %get-tuple-element.55), channel_id=1, source_target_pairs={{0,2},{1,3},{2,0},{3,1},{4,6},{5,7},{6,4},{7,5},{8,10},{9,11},{10,... | collective-permute-start | bytes 589832 | tf_op jit(solution)/shard_map/ppermute | solution.py:290
  65.4 3.4 %expand_and_depthwise.5 = bf16[512,384]{1,0:T(8,128)(2,1)S(1)} custom-call(f32[7,1536]{1,0:T(8,128)S(1)} %reshape.3.packed, bf16[31,1536]{1,0:T(8,128)(2,1)S(1)} %copy-done.2, bf16[1536,768]{1,0:T(8,128)(2,1)S(1)} %gather_shards.3.weight, bf16[512,1536]{1,0:T(8,128)(2,1)S(1)} %collective-permute-done.13.block.outer, ...), custom_call_target="tpu_custom_call" | custom-call | tf_op jit(solution)/shard_map/expand_and_depthwise/pallas_call | solution.py:200
  68.8 0.0 collective-permute-done.16.refs_15_
  68.8 0.1 collective-permute-start.20
  68.9 3.4 %expand_and_depthwise.6 = bf16[512,384]{1,0:T(8,128)(2,1)S(1)} custom-call(f32[7,1536]{1,0:T(8,128)S(1)} %reshape.3.packed, bf16[31,1536]{1,0:T(8,128)(2,1)S(1)} %copy-done.2, bf16[1536,768]{1,0:T(8,128)(2,1)S(1)} %gather_shards.3.weight, bf16[512,1536]{1,0:T(8,128)(2,1)S(1)} %layer_norm.3.outer.block.sibling, ...), custom_call_target="tpu_custom_call" | custom-call | tf_op jit(solution)/shard_map/expand_and_depthwise/pallas_call | solution.py:200
  72.3 0.0 copy-start.1
  72.3 0.7 collective-permute-start.26
  73.0 0.0 collective-permute-done.14.refs_3_
  73.0 3.6 %expand_and_depthwise.7.refs_12_ = bf16[512,384]{1,0:T(8,128)(2,1)S(1)} custom-call(f32[7,1536]{1,0:T(8,128)S(1)} %reshape.3.packed, bf16[31,1536]{1,0:T(8,128)(2,1)S(1)} %copy-done.2, bf16[1536,768]{1,0:T(8,128)(2,1)S(1)} %gather_shards.3.weight, bf16[512,1536]{1,0:T(8,128)(2,1)S(1)} %layer_norm.4.outer.sibling.block, ...), custom_call_target="tpu_custom_call" | custom-call | tf_op jit(solution)/shard_map/expand_and_depthwise/pallas_call | solution.py:200
  76.6 0.5 collective-permute-done.15.refs_4_
  77.1 1.1 %collective-permute-start.18 = (bf16[192,768]{1,0:T(8,128)(2,1)S(1)}, bf16[192,768]{1,0:T(8,128)(2,1)S(1)}, u32[]{:S(2)}, u32[]{:S(2)}) collective-permute-start(bf16[192,768]{1,0:T(8,128)(2,1)S(1)} %collective-permute-done.15.refs_4_), channel_id=1, source_target_pairs={{0,4},{4,0},{8,12},{12,8},{16,20},{20,16},{24,28},{28,24},{1,5},{5... | collective-permute-start | bytes 884744 | tf_op jit(solution)/shard_map/ppermute | solution.py:290
  78.2 0.0 collective-permute-done.19.refs_6_
  78.2 1.2 %collective-permute-done.20.refs_14_ = bf16[512,384]{1,0:T(8,128)(2,1)S(1)} collective-permute-done((bf16[512,384]{1,0:T(8,128)(2,1)S(1)}, bf16[512,384]{1,0:T(8,128)(2,1)S(1)}, u32[]{:S(2)}, u32[]{:S(2)}) %collective-permute-start.20) | collective-permute-done | bytes 393248 | tf_op jit(solution)/shard_map/ppermute | solution.py:290
  79.4 0.5 collective-permute-start.22
  79.9 0.0 collective-permute-start.23
  79.9 5.7 %collective-permute-done.18.refs_5_ = bf16[192,768]{1,0:T(8,128)(2,1)S(1)} collective-permute-done((bf16[192,768]{1,0:T(8,128)(2,1)S(1)}, bf16[192,768]{1,0:T(8,128)(2,1)S(1)}, u32[]{:S(2)}, u32[]{:S(2)}) %collective-permute-start.18) | collective-permute-done | bytes 294944 | tf_op jit(solution)/shard_map/ppermute | solution.py:290
  85.6 0.5 collective-permute-start.25
  86.1 0.0 collective-permute-done.22.refs_8_
  86.1 0.0 collective-permute-done.23.refs_9_
  86.1 1.1 %collective-permute-done.24.refs_10_ = bf16[192,768]{1,0:T(8,128)(2,1)S(1)} collective-permute-done((bf16[192,768]{1,0:T(8,128)(2,1)S(1)}, bf16[192,768]{1,0:T(8,128)(2,1)S(1)}, u32[]{:S(2)}, u32[]{:S(2)}) %collective-permute-start.24) | collective-permute-done | bytes 294944 | tf_op jit(solution)/shard_map/ppermute | solution.py:290
  87.2 0.4 collective-permute-done.25.refs_11_
  87.6 5.1 %project_and_residual.1 = bf16[512,1536]{1,0:T(8,128)(2,1)} custom-call(f32[7,1536]{1,0:T(8,128)S(1)} %reshape.3.packed, bf16[512,1536]{1,0:T(8,128)(2,1)S(1)} %bitcast.5, bf16[192,1536]{1,0:T(8,128)(2,1)S(1)} %copy-done.1, bf16[384,768]{1,0:T(8,128)(2,1)S(1)} %gather_shards.2.refs_0_, bf16[192,768]{1,0:T(8,128)(2,1)S(1)} %collective-permute-done.10.refs_1_, ...), custom_call_target="tpu_custom_call" | custom-call | tf_op jit(solution)/shard_map/project_and_residual/pallas_call | solution.py:270
  (33 shorter events, 0.1 us)
Async XLA Ops:
  0.0 3.0 %copy-start = (bf16[1,512,1536]{2,1,0:T(8,128)(2,1)S(1)}, bf16[1,512,1536]{2,1,0:T(8,128)(2,1)}, u32[]{:S(2)}) copy-start(bf16[1,512,1536]{2,1,0:T(8,128)(2,1)} %param.10) | copy-start | bytes 4718596
  0.0 21.2 %copy-start.5 = (bf16[1536]{0:T(1024)(128)(2,1)S(1)}, bf16[1536]{0:T(1024)(128)(2,1)}, u32[]{:S(2)}) copy-start(bf16[1536]{0:T(1024)(128)(2,1)} %param.11) | copy-start | bytes 9220
  0.0 21.4 %copy-start.6 = (bf16[1536]{0:T(1024)(128)(2,1)S(1)}, bf16[1536]{0:T(1024)(128)(2,1)}, u32[]{:S(2)}) copy-start(bf16[1536]{0:T(1024)(128)(2,1)} %param.12) | copy-start | bytes 9220
  0.0 21.7 %copy-start.4 = (bf16[3072]{0:T(1024)(128)(2,1)S(1)}, bf16[3072]{0:T(1024)(128)(2,1)}, u32[]{:S(2)}) copy-start(bf16[3072]{0:T(1024)(128)(2,1)} %param.14) | copy-start | bytes 18436
  0.0 21.7 %copy-start.7 = (bf16[1536]{0:T(1024)(128)(2,1)S(1)}, bf16[1536]{0:T(1024)(128)(2,1)}, u32[]{:S(2)}) copy-start(bf16[1536]{0:T(1024)(128)(2,1)} %param.16) | copy-start | bytes 9220
  0.0 22.0 %copy-start.8 = (bf16[1536]{0:T(1024)(128)(2,1)S(1)}, bf16[1536]{0:T(1024)(128)(2,1)}, u32[]{:S(2)}) copy-start(bf16[1536]{0:T(1024)(128)(2,1)} %param.17) | copy-start | bytes 9220
  0.0 22.3 %copy-start.9 = (bf16[1536]{0:T(1024)(128)(2,1)S(1)}, bf16[1536]{0:T(1024)(128)(2,1)}, u32[]{:S(2)}) copy-start(bf16[1536]{0:T(1024)(128)(2,1)} %param.19) | copy-start | bytes 9220
  0.0 29.4 %collective-permute-start.8 = (bf16[512,1536]{1,0:T(8,128)(2,1)}, bf16[512,1536]{1,0:T(8,128)(2,1)}, u32[]{:S(2)}, u32[]{:S(2)}) collective-permute-start(bf16[512,1536]{1,0:T(8,128)(2,1)} %bitcast.2), channel_id=1, source_target_pairs={{0,1},{1,0},{2,3},{3,2},{4,5},{5,4},{6,7},{7,6},{8,9},{9,8},{10,11... | collective-permute-start | bytes 4718600 | tf_op jit(solution)/shard_map/ppermute | solution.py:290
  3.0 37.7 %collective-permute-start.4 = (bf16[512,1536]{1,0:T(8,128)(2,1)S(1)}, bf16[512,1536]{1,0:T(8,128)(2,1)}, u32[]{:S(2)}, u32[]{:S(2)}) collective-permute-start(bf16[512,1536]{1,0:T(8,128)(2,1)S(1)} %bitcast.3), channel_id=1, source_target_pairs={{0,2},{1,3},{2,0},{3,1},{4,6},{5,7},{6,4},{7,5},{8,10},{9,11},{10,... | collective-permute-start | bytes 4718600 | tf_op jit(solution)/shard_map/ppermute | solution.py:290
  5.7 15.6 %collective-permute-start.1 = (bf16[192,1536]{1,0:T(8,128)(2,1)}, bf16[192,1536]{1,0:T(8,128)(2,1)S(1)}, u32[]{:S(2)}, u32[]{:S(2)}) collective-permute-start(bf16[192,1536]{1,0:T(8,128)(2,1)} %get-tuple-element.35), channel_id=1, source_target_pairs={{0,4},{4,0},{8,12},{12,8},{16,20},{20,16},{24,28},{28,24},{1,5},{5... | collective-permute-start | bytes 1769480 | tf_op jit(solution)/shard_map/ppermute | solution.py:290
  7.2 11.9 %collective-permute-start = (bf16[192,768]{1,0:T(8,128)(2,1)}, bf16[192,768]{1,0:T(8,128)(2,1)S(1)}, u32[]{:S(2)}, u32[]{:S(2)}) collective-permute-start(bf16[192,768]{1,0:T(8,128)(2,1)} %get-tuple-element.39.refs_0_), channel_id=1, source_target_pairs={{0,24},{4,28},{8,16},{12,20},{16,8},{20,12},{24,0},{28,4},{1,25},{... | collective-permute-start | bytes 884744 | tf_op jit(solution)/shard_map/ppermute | solution.py:290
  10.8 15.8 %collective-permute-start.5 = (bf16[192,768]{1,0:T(8,128)(2,1)}, bf16[192,768]{1,0:T(8,128)(2,1)S(1)}, u32[]{:S(2)}, u32[]{:S(2)}) collective-permute-start(bf16[192,768]{1,0:T(8,128)(2,1)} %get-tuple-element.39.refs_0_), channel_id=1, source_target_pairs={{0,8},{4,12},{8,0},{12,4},{16,24},{20,28},{24,16},{28,20},{1,9},{5... | collective-permute-start | bytes 884744 | tf_op jit(solution)/shard_map/ppermute | solution.py:290
  22.4 15.6 %collective-permute-start.2 = (bf16[192,768]{1,0:T(8,128)(2,1)}, bf16[192,768]{1,0:T(8,128)(2,1)S(1)}, u32[]{:S(2)}, u32[]{:S(2)}) collective-permute-start(bf16[192,768]{1,0:T(8,128)(2,1)} %get-tuple-element.52), channel_id=1, source_target_pairs={{0,8},{4,12},{8,0},{12,4},{16,24},{20,28},{24,16},{28,20},{1,9},{5... | collective-permute-start | bytes 884744 | tf_op jit(solution)/shard_map/ppermute | solution.py:290
  25.3 15.4 %collective-permute-start.3 = (bf16[192,768]{1,0:T(8,128)(2,1)}, bf16[192,768]{1,0:T(8,128)(2,1)S(1)}, u32[]{:S(2)}, u32[]{:S(2)}) collective-permute-start(bf16[192,768]{1,0:T(8,128)(2,1)} %get-tuple-element.39.refs_0_), channel_id=1, source_target_pairs={{0,16},{4,20},{8,24},{12,28},{16,0},{20,4},{24,8},{28,12},{1,17},{... | collective-permute-start | bytes 884744 | tf_op jit(solution)/shard_map/ppermute | solution.py:290
  26.6 14.1 %collective-permute-start.6 = (bf16[192,768]{1,0:T(8,128)(2,1)S(1)}, bf16[192,768]{1,0:T(8,128)(2,1)S(1)}, u32[]{:S(2)}, u32[]{:S(2)}) collective-permute-start(bf16[192,768]{1,0:T(8,128)(2,1)S(1)} %collective-permute-done.5.refs_1_), channel_id=1, source_target_pairs={{0,4},{4,0},{8,12},{12,8},{16,20},{20,16},{24,28},{28,24},{1,5},{5... | collective-permute-start | bytes 884744 | tf_op jit(solution)/shard_map/ppermute | solution.py:290
  29.4 11.3 %collective-permute-start.7 = (bf16[192,768]{1,0:T(8,128)(2,1)S(1)}, bf16[192,768]{1,0:T(8,128)(2,1)S(1)}, u32[]{:S(2)}, u32[]{:S(2)}) collective-permute-start(bf16[192,768]{1,0:T(8,128)(2,1)S(1)} %collective-permute-done.refs_3_), channel_id=1, source_target_pairs={{0,4},{4,0},{8,12},{12,8},{16,20},{20,16},{24,28},{28,24},{1,5},{5... | collective-permute-start | bytes 884744 | tf_op jit(solution)/shard_map/ppermute | solution.py:290
  32.7 12.6 %copy-start.10 = (bf16[192,768]{1,0:T(8,128)(2,1)S(1)}, bf16[192,768]{1,0:T(8,128)(2,1)}, u32[]{:S(2)}) copy-start(bf16[192,768]{1,0:T(8,128)(2,1)} %get-tuple-element.52) | copy-start | bytes 884740
  32.7 20.8 %copy-start.3 = (bf16[192,768]{1,0:T(8,128)(2,1)S(1)}, bf16[192,768]{1,0:T(8,128)(2,1)}, u32[]{:S(2)}) copy-start(bf16[192,768]{1,0:T(8,128)(2,1)} %get-tuple-element.39.refs_0_) | copy-start | bytes 884740
  43.4 11.1 %collective-permute-start.13 = (bf16[512,1536]{1,0:T(8,128)(2,1)S(1)}, bf16[512,1536]{1,0:T(8,128)(2,1)S(1)}, u32[]{:S(2)}, u32[]{:S(2)}) collective-permute-start(bf16[512,1536]{1,0:T(8,128)(2,1)S(1)} %layer_norm.5.block.sibling.outer), channel_id=1, source_target_pairs={{0,1},{1,0},{2,3},{3,2},{4,5},{5,4},{6,7},{7,6},{8,9},{9,8},{10,11... | collective-permute-start | bytes 4718600 | tf_op jit(solution)/shard_map/ppermute | solution.py:290
  43.5 9.9 %collective-permute-start.9 = (bf16[192,768]{1,0:T(8,128)(2,1)S(1)}, bf16[192,768]{1,0:T(8,128)(2,1)S(1)}, u32[]{:S(2)}, u32[]{:S(2)}) collective-permute-start(bf16[192,768]{1,0:T(8,128)(2,1)S(1)} %collective-permute-done.3.refs_2_), channel_id=1, source_target_pairs={{0,4},{4,0},{8,12},{12,8},{16,20},{20,16},{24,28},{28,24},{1,5},{5... | collective-permute-start | bytes 884744 | tf_op jit(solution)/shard_map/ppermute | solution.py:290
  45.4 14.2 %collective-permute-start.11 = (bf16[192,768]{1,0:T(8,128)(2,1)S(1)}, bf16[192,768]{1,0:T(8,128)(2,1)S(1)}, u32[]{:S(2)}, u32[]{:S(2)}) collective-permute-start(bf16[192,768]{1,0:T(8,128)(2,1)S(1)} %copy-done.10), channel_id=1, source_target_pairs={{0,24},{4,28},{8,16},{12,20},{16,8},{20,12},{24,0},{28,4},{1,25},{... | collective-permute-start | bytes 884744 | tf_op jit(solution)/shard_map/ppermute | solution.py:290
  49.0 14.9 %collective-permute-start.10 = (bf16[192,768]{1,0:T(8,128)(2,1)S(1)}, bf16[192,768]{1,0:T(8,128)(2,1)S(1)}, u32[]{:S(2)}, u32[]{:S(2)}) collective-permute-start(bf16[192,768]{1,0:T(8,128)(2,1)S(1)} %collective-permute-done.2.refs_0_), channel_id=1, source_target_pairs={{0,4},{4,0},{8,12},{12,8},{16,20},{20,16},{24,28},{28,24},{1,5},{5... | collective-permute-start | bytes 884744 | tf_op jit(solution)/shard_map/ppermute | solution.py:290
  49.5 5.1 %collective-permute-start.12 = (bf16[32,1536]{1,0:T(8,128)(2,1)S(1)}, bf16[32,1536]{1,0:T(8,128)(2,1)S(1)}, u32[]{:S(2)}, u32[]{:S(2)}) collective-permute-start(bf16[32,1536]{1,0:T(8,128)(2,1)S(1)} %pad_maximum_fusion), channel_id=1, source_target_pairs={{0,3},{1,2},{2,1},{3,0},{4,7},{5,6},{6,5},{7,4},{8,11},{9,10},{10,... | collective-permute-start | bytes 294920 | tf_op jit(solution)/shard_map/ppermute | solution.py:290
  53.5 1.1 %copy-start.2 = (bf16[31,1536]{1,0:T(8,128)(2,1)S(1)}, bf16[31,1536]{1,0:T(8,128)(2,1)}, u32[]{:S(2)}) copy-start(bf16[31,1536]{1,0:T(8,128)(2,1)} %kernel.7) | copy-start | bytes 285700
  53.5 24.7 %collective-permute-start.19 = (bf16[384,768]{1,0:T(8,128)(2,1)S(1)}, bf16[384,768]{1,0:T(8,128)(2,1)S(1)}, u32[]{:S(2)}, u32[]{:S(2)}) collective-permute-start(bf16[384,768]{1,0:T(8,128)(2,1)S(1)} %gather_shards.2.refs_0_), channel_id=1, source_target_pairs={{0,1},{1,0},{2,3},{3,2},{4,5},{5,4},{6,7},{7,6},{8,9},{9,8},{10,11... | collective-permute-start | bytes 1769480 | tf_op jit(solution)/shard_map/ppermute | solution.py:290
  57.9 10.9 %collective-permute-start.16 = (bf16[256,384]{1,0:T(8,128)(2,1)S(1)}, bf16[256,384]{1,0:T(8,128)(2,1)S(1)}, u32[]{:S(2)}, u32[]{:S(2)}) collective-permute-start(bf16[256,384]{1,0:T(8,128)(2,1)S(1)} %get-tuple-element.50), channel_id=1, source_target_pairs={{0,2},{1,3},{2,0},{3,1},{4,6},{5,7},{6,4},{7,5},{8,10},{9,11},{10,... | collective-permute-start | bytes 589832 | tf_op jit(solution)/shard_map/ppermute | solution.py:290
  59.6 13.5 %collective-permute-start.14 = (bf16[192,768]{1,0:T(8,128)(2,1)S(1)}, bf16[192,768]{1,0:T(8,128)(2,1)S(1)}, u32[]{:S(2)}, u32[]{:S(2)}) collective-permute-start(bf16[192,768]{1,0:T(8,128)(2,1)S(1)} %collective-permute-done.11.refs_2_), channel_id=1, source_target_pairs={{0,4},{4,0},{8,12},{12,8},{16,20},{20,16},{24,28},{28,24},{1,5},{5... | collective-permute-start | bytes 884744 | tf_op jit(solution)/shard_map/ppermute | solution.py:290
  61.1 16.0 %collective-permute-start.15 = (bf16[192,768]{1,0:T(8,128)(2,1)S(1)}, bf16[192,768]{1,0:T(8,128)(2,1)S(1)}, u32[]{:S(2)}, u32[]{:S(2)}) collective-permute-start(bf16[192,768]{1,0:T(8,128)(2,1)S(1)} %copy-done.10), channel_id=1, source_target_pairs={{0,16},{4,20},{8,24},{12,28},{16,0},{20,4},{24,8},{28,12},{1,17},{... | collective-permute-start | bytes 884744 | tf_op jit(solution)/shard_map/ppermute | solution.py:290
  63.9 8.5 %collective-permute-start.17 = (bf16[256,384]{1,0:T(8,128)(2,1)S(1)}, bf16[256,384]{1,0:T(8,128)(2,1)S(1)}, u32[]{:S(2)}, u32[]{:S(2)}) collective-permute-start(bf16[256,384]{1,0:T(8,128)(2,1)S(1)} %get-tuple-element.55), channel_id=1, source_target_pairs={{0,2},{1,3},{2,0},{3,1},{4,6},{5,7},{6,4},{7,5},{8,10},{9,11},{10,... | collective-permute-start | bytes 589832 | tf_op jit(solution)/shard_map/ppermute | solution.py:290
  68.8 10.6 %collective-permute-start.20 = (bf16[512,384]{1,0:T(8,128)(2,1)S(1)}, bf16[512,384]{1,0:T(8,128)(2,1)S(1)}, u32[]{:S(2)}, u32[]{:S(2)}) collective-permute-start(bf16[512,384]{1,0:T(8,128)(2,1)S(1)} %expand_and_depthwise.5), channel_id=1, source_target_pairs={{0,3},{1,2},{2,1},{3,0},{4,7},{5,6},{6,5},{7,4},{8,11},{9,10},{10,... | collective-permute-start | bytes 1179656 | tf_op jit(solution)/shard_map/ppermute | solution.py:290
  72.3 15.3 %copy-start.1 = (bf16[192,1536]{1,0:T(8,128)(2,1)S(1)}, bf16[192,1536]{1,0:T(8,128)(2,1)}, u32[]{:S(2)}) copy-start(bf16[192,1536]{1,0:T(8,128)(2,1)} %whole.1) | copy-start | bytes 1769476
  72.3 13.3 %collective-permute-start.26 = (bf16[512,384]{1,0:T(8,128)(2,1)S(1)}, bf16[512,384]{1,0:T(8,128)(2,1)S(1)}, u32[]{:S(2)}, u32[]{:S(2)}) collective-permute-start(bf16[512,384]{1,0:T(8,128)(2,1)S(1)} %expand_and_depthwise.6), channel_id=1, source_target_pairs={{0,1},{1,0},{2,3},{3,2},{4,5},{5,4},{6,7},{7,6},{8,9},{9,8},{10,11... | collective-permute-start | bytes 1179656 | tf_op jit(solution)/shard_map/ppermute | solution.py:290
  77.1 8.5 %collective-permute-start.18 = (bf16[192,768]{1,0:T(8,128)(2,1)S(1)}, bf16[192,768]{1,0:T(8,128)(2,1)S(1)}, u32[]{:S(2)}, u32[]{:S(2)}) collective-permute-start(bf16[192,768]{1,0:T(8,128)(2,1)S(1)} %collective-permute-done.15.refs_4_), channel_id=1, source_target_pairs={{0,4},{4,0},{8,12},{12,8},{16,20},{20,16},{24,28},{28,24},{1,5},{5... | collective-permute-start | bytes 884744 | tf_op jit(solution)/shard_map/ppermute | solution.py:290
  79.4 6.7 %collective-permute-start.21 = (bf16[192,768]{1,0:T(8,128)(2,1)S(1)}, bf16[192,768]{1,0:T(8,128)(2,1)S(1)}, u32[]{:S(2)}, u32[]{:S(2)}) collective-permute-start(bf16[192,768]{1,0:T(8,128)(2,1)S(1)} %collective-permute-done.10.refs_1_), channel_id=1, source_target_pairs={{0,1},{1,0},{2,3},{3,2},{4,5},{5,4},{6,7},{7,6},{8,9},{9,8},{10,11... | collective-permute-start | bytes 884744 | tf_op jit(solution)/shard_map/ppermute | solution.py:290
  79.4 6.7 %collective-permute-start.22 = (bf16[192,768]{1,0:T(8,128)(2,1)S(1)}, bf16[192,768]{1,0:T(8,128)(2,1)S(1)}, u32[]{:S(2)}, u32[]{:S(2)}) collective-permute-start(bf16[192,768]{1,0:T(8,128)(2,1)S(1)} %collective-permute-done.11.refs_2_), channel_id=1, source_target_pairs={{0,1},{1,0},{2,3},{3,2},{4,5},{5,4},{6,7},{7,6},{8,9},{9,8},{10,11... | collective-permute-start | bytes 884744 | tf_op jit(solution)/shard_map/ppermute | solution.py:290
  79.9 6.2 %collective-permute-start.23 = (bf16[192,768]{1,0:T(8,128)(2,1)S(1)}, bf16[192,768]{1,0:T(8,128)(2,1)S(1)}, u32[]{:S(2)}, u32[]{:S(2)}) collective-permute-start(bf16[192,768]{1,0:T(8,128)(2,1)S(1)} %collective-permute-done.14.refs_3_), channel_id=1, source_target_pairs={{0,1},{1,0},{2,3},{3,2},{4,5},{5,4},{6,7},{7,6},{8,9},{9,8},{10,11... | collective-permute-start | bytes 884744 | tf_op jit(solution)/shard_map/ppermute | solution.py:290
  85.6 1.6 %collective-permute-start.24 = (bf16[192,768]{1,0:T(8,128)(2,1)S(1)}, bf16[192,768]{1,0:T(8,128)(2,1)S(1)}, u32[]{:S(2)}, u32[]{:S(2)}) collective-permute-start(bf16[192,768]{1,0:T(8,128)(2,1)S(1)} %collective-permute-done.15.refs_4_), channel_id=1, source_target_pairs={{0,1},{1,0},{2,3},{3,2},{4,5},{5,4},{6,7},{7,6},{8,9},{9,8},{10,11... | collective-permute-start | bytes 884744 | tf_op jit(solution)/shard_map/ppermute | solution.py:290
  85.6 2.0 %collective-permute-start.25 = (bf16[192,768]{1,0:T(8,128)(2,1)S(1)}, bf16[192,768]{1,0:T(8,128)(2,1)S(1)}, u32[]{:S(2)}, u32[]{:S(2)}) collective-permute-start(bf16[192,768]{1,0:T(8,128)(2,1)S(1)} %collective-permute-done.18.refs_5_), channel_id=1, source_target_pairs={{0,1},{1,0},{2,3},{3,2},{4,5},{5,4},{6,7},{7,6},{8,9},{9,8},{10,11... | collective-permute-start | bytes 884744 | tf_op jit(solution)/shard_map/ppermute | solution.py:290
